TPU v7x, 32 devices: a whole 2x2x4 slice. The times are simulated.
32 devices in a mesh: grp: 2 (over x), smp: 16 (over z, y, core).
Axes of the slice: x: 2, y: 2, z: 4, core: 2. Of those that a mesh axis runs over, the one named last changes fastest.
Arguments:
- activations: bfloat16 [64, 384, 768], P(('grp', 'smp')), parts along dimension 0, may hold values from -24 to 24
- cotangent: bfloat16 [64, 384, 768], P(('grp', 'smp')), parts along dimension 0, may hold values from -6 to 6
- pair_rep: bfloat16 [768, 384, 128], P(('grp', 'smp')), parts along dimension 0, may hold values from -6 to 6
- pair_gain: float32 [128], replicated, may hold values from 0.5 to 1.5
- w_pair: bfloat16 [128, 16], replicated, may hold values from -0.5 to 0.5
- w_query: bfloat16 [768, 768], replicated, may hold values from -0.21875 to 0.21875
- w_key: bfloat16 [768, 768], replicated, may hold values from -0.21875 to 0.21875
- w_value: bfloat16 [768, 768], replicated, may hold values from -0.21875 to 0.21875
- w_out: bfloat16 [768, 768], replicated, may hold values from -0.21875 to 0.21875
- token_mask: int32 [768], P('grp'), parts along dimension 0, may hold values from 0 to 1, as said below
Outputs:
- attended: bfloat16 [64, 384, 768], P(('grp', 'smp')), parts along dimension 0
- grad_pair: bfloat16 [768, 384, 128], P(('grp', 'smp')), parts along dimension 0
- grad_projection: float32 [256, 16], P('grp'), parts along dimension 0
There are 2 independent parts, one for each index of `grp`. A program takes and returns all parts, laid end to end along the dimension named above; an argument that names none is the same for every part. Nothing has to cross between parts.
Inputs may be any that keep to these rules, and one draw needn't show every extreme that they name: `token_mask`: position 0 is always 1.
All inputs are finite; a program needn't handle non-finite values.
Results may differ from a plain program's by a relative error of at most 0.0045.
The roundings to bfloat16 on the way count: a program that leaves them out, or rounds other values in their place, can miss the bound.
Values may be sent and summed in bfloat16 or wider, within the bound.
No kernel may reach another device: no remote copies, remote signals or barrier semaphores. Data moves between devices by JAX's collectives and lax.ppermute only.
A program may use at most 192 MiB of HBM per device.

v0:
```python
import functools
import math

import jax
import jax.numpy as jnp
from jax import lax
from jax.experimental import pallas as pl
from jax.experimental.pallas import tpu as pltpu
from jax.sharding import PartitionSpec as P

F32 = jnp.float32
BF16 = jnp.bfloat16
LOG2E = math.log2(math.e)
NT = (((1,), (1,)), ((), ()))
TN = (((0,), (0,)), ((), ()))
VMEM_LIMIT = 48 * 1024 * 1024
HEAD_CHUNKS = 2
ROW_STEP = 128


def normalize(pair_rep, pair_gain):
    values_f = pair_rep.astype(F32)
    centre = jnp.mean(values_f, axis=-1, keepdims=True)
    spread = jnp.mean((values_f - centre) ** 2, axis=-1, keepdims=True)
    rstd = lax.rsqrt(spread + 1e-05)
    centred = (values_f - centre) * rstd
    return (centred * pair_gain, centred, rstd)


def per_device_plain(
    activations, cotangent, pair_rep, pair_gain, w_pair, w_query, w_key, w_value, w_out, token_mask
):
    head_count = w_pair.shape[1]
    model_width = w_query.shape[0]
    head_width = model_width // head_count
    tok_count = token_mask.shape[0]
    normed, centred, rstd = normalize(pair_rep, pair_gain)
    bias_rows = jnp.einsum(
        "rjc,ch->rhj", normed, w_pair.astype(F32), precision=lax.Precision.HIGHEST
    ).astype(BF16)
    bias_full = lax.all_gather(bias_rows, "smp", axis=0, tiled=True).astype(F32)
    live_keys = token_mask > 0
    outputs = []
    grad_total = None
    for sample_index in range(activations.shape[0]):
        sample_act = activations[sample_index]

        def project(weight):
            return (
                jnp.dot(sample_act, weight, preferred_element_type=F32)
                .astype(BF16)
                .reshape(tok_count, head_count, head_width)
            )

        queries, keys_proj, values_proj = project(w_query), project(w_key), project(w_value)
        scores = (
            jnp.einsum("ihd,jhd->ihj", queries, keys_proj, preferred_element_type=F32)
            * head_width ** (-0.5)
            + bias_full
        )
        scores = jnp.where(live_keys[None, None, :], scores, -1e30)
        exps = jnp.exp(scores - jnp.max(scores, axis=-1, keepdims=True))
        probs = exps / jnp.sum(exps, axis=-1, keepdims=True)
        mixed = (
            jnp.einsum("ihj,jhd->ihd", probs.astype(BF16), values_proj, preferred_element_type=F32)
            .astype(BF16)
            .reshape(tok_count, model_width)
        )
        output = jnp.dot(mixed, w_out, preferred_element_type=F32)
        outputs.append(jnp.where(live_keys[:, None], output, 0.0).astype(BF16))
        sample_cot = cotangent[sample_index]
        masked_cot = jnp.where(live_keys[:, None], sample_cot, jnp.zeros_like(sample_cot))
        d_mixed = (
            jnp.dot(masked_cot, w_out.T, preferred_element_type=F32)
            .astype(BF16)
            .reshape(tok_count, head_count, head_width)
        )
        d_probs = jnp.einsum("ihd,jhd->ihj", d_mixed, values_proj, preferred_element_type=F32)
        d_scores = probs * (d_probs - jnp.sum(probs * d_probs, axis=-1, keepdims=True))
        grad_total = d_scores if grad_total is None else grad_total + d_scores
    bias_grad = lax.psum_scatter(grad_total, "smp", scatter_dimension=0, tiled=True)
    proj_local = jnp.einsum("rjc,rhj->ch", normed, bias_grad, precision=lax.Precision.HIGHEST)
    grad_projection = lax.psum(proj_local, "smp")
    d_normed = (
        jnp.einsum("rhj,ch->rjc", bias_grad, w_pair.astype(F32), precision=lax.Precision.HIGHEST)
        * pair_gain
    )
    first_mean = jnp.mean(d_normed, axis=-1, keepdims=True)
    second_mean = jnp.mean(d_normed * centred, axis=-1, keepdims=True)
    grad_pair = (rstd * (d_normed - first_mean - centred * second_mean)).astype(BF16)
    return (jnp.stack(outputs), grad_pair, grad_projection)


def dot(left, right, dims=None):
    if dims is None:
        return jnp.dot(left, right, preferred_element_type=F32)
    return lax.dot_general(left, right, dims, preferred_element_type=F32)


def pieces3(value):
    high = value.astype(BF16)
    rest = value - high.astype(F32)
    mid = rest.astype(BF16)
    low = (rest - mid.astype(F32)).astype(BF16)
    return high, mid, low


def bias_kernel(core_ref, pair_ref, gain_ref, wt_ref, mask_ref, own_ref, other_ref, mean_ref, rstd_ref, held):
    rows, tok, chan = pair_ref.shape
    heads = wt_ref.shape[0]
    half = heads // 2
    scaled = wt_ref[...].astype(F32) * gain_ref[...]
    total = jnp.sum(scaled, axis=1, keepdims=True)
    left = jnp.concatenate([*pieces3(scaled), jnp.ones((16, chan), BF16)], axis=0)
    ones_c = jnp.ones((chan, chan), BF16)
    ones_r = jnp.ones((8, 3 * chan), BF16)
    live = mask_ref[...] > 0
    for i in range(rows):
        values = pair_ref[i]
        sums = dot(left, values, NT)
        mean_row = sums[3 * heads : 3 * heads + 1] * (1.0 / chan)
        diff = values.astype(F32) - dot(values, ones_c) * (1.0 / chan)
        squares = jnp.concatenate(pieces3(diff * diff), axis=1)
        spread = dot(ones_r, squares, NT)[0:1] * (1.0 / chan)
        rstd_row = lax.rsqrt(spread + 1e-05)
        raw = sums[0:heads] + (sums[heads : 2 * heads] + sums[2 * heads : 3 * heads])
        bias = (raw - total * mean_row) * rstd_row
        bias = jnp.where(live, bias, -1e30)
        held[:, i, :] = bias
        mean_ref[i : i + 1, :] = mean_row
        rstd_ref[i : i + 1, :] = rstd_row
    core = core_ref[0]
    own_ref[...] = held[pl.ds(core * half, half)].astype(BF16)
    other_ref[...] = held[pl.ds((1 - core) * half, half)].astype(BF16)


def bias_call(core, pair_rep, gain, w_t, mask_row):
    rows, tok, chan = pair_rep.shape
    heads = w_t.shape[0]
    half = heads // 2
    vm = pl.BlockSpec(memory_space=pltpu.VMEM)
    return pl.pallas_call(
        bias_kernel,
        out_shape=[
            jax.ShapeDtypeStruct((half, rows, tok), BF16),
            jax.ShapeDtypeStruct((half, rows, tok), BF16),
            jax.ShapeDtypeStruct((rows, tok), F32),
            jax.ShapeDtypeStruct((rows, tok), F32),
        ],
        in_specs=[pl.BlockSpec(memory_space=pltpu.SMEM)] + [vm] * 4,
        out_specs=[vm] * 4,
        scratch_shapes=[pltpu.VMEM((heads, rows, tok), F32)],
        compiler_params=pltpu.CompilerParams(vmem_limit_bytes=VMEM_LIMIT),
        cost_estimate=pl.CostEstimate(flops=int(6e9), bytes_accessed=int(4e6), transcendentals=0),
        name="pair_bias",
    )(core, pair_rep, gain, w_t, mask_row)


def project_kernel(core_ref, act_ref, cot_ref, wq_ref, wk_ref, wv_ref, wo_ref, mask_ref, q_ref, k_ref, v_ref, d_ref):
    act = act_ref[0]
    for weight, out in ((wq_ref, q_ref), (wk_ref, k_ref), (wv_ref, v_ref)):
        out[0] = dot(act, weight[...]).T.astype(BF16)
    live = mask_ref[...] > 0
    d_ref[0] = jnp.where(live, dot(wo_ref[...], cot_ref[0], NT), 0.0).astype(BF16)


def project_call(core, act, cot, w_query, w_key, w_value, w_out, mask_row):
    samples, tok, width = act.shape
    half = width // 2
    columns = pl.BlockSpec((width, half), lambda s, c: (0, c[0]))
    per_sample = pl.BlockSpec((1, tok, width), lambda s, c: (s, 0, 0))
    out = pl.BlockSpec((1, half, tok), lambda s, c: (s, 0, 0))
    return pl.pallas_call(
        project_kernel,
        grid_spec=pltpu.PrefetchScalarGridSpec(
            num_scalar_prefetch=1,
            grid=(samples,),
            in_specs=[per_sample, per_sample, columns, columns, columns,
                      pl.BlockSpec((half, width), lambda s, c: (c[0], 0)),
                      pl.BlockSpec((1, tok), lambda s, c: (0, 0))],
            out_specs=[out] * 4,
        ),
        out_shape=[jax.ShapeDtypeStruct((samples, half, tok), BF16)] * 4,
        compiler_params=pltpu.CompilerParams(vmem_limit_bytes=VMEM_LIMIT),
        cost_estimate=pl.CostEstimate(
            flops=8 * samples * tok * width * half, bytes_accessed=int(6e6), transcendentals=0
        ),
        name="projections",
    )(core, act, cot, w_query, w_key, w_value, w_out, mask_row)


def code16(block):
    top = jnp.max(jnp.abs(block), axis=0, keepdims=True)
    inverse = jnp.where(top > 0, 32766.0 / jnp.where(top > 0, top, 1.0), 0.0)
    codes = jnp.round(block * inverse).astype(jnp.int32).astype(jnp.int16)
    return codes, top * (1.0 / 32766.0)


def decode16(codes, scale):
    return codes.astype(jnp.int32).astype(F32) * scale


def attention_kernel(za, yb, head_width, offs_ref, *refs):
    slots = za * yb
    bias_refs = refs[:slots]
    q0, k0, v0, d0, q1, k1, v1, d1 = refs[slots : slots + 8]
    mixed0, mixed1, own_ref, code_ref, scale_ref, bias_f, grad = refs[slots + 8 :]
    tok = bias_f.shape[0]
    part = bias_refs[0].shape[1] // 2
    for slot in range(slots):
        block = bias_refs[slot][0].astype(F32) * LOG2E
        for side in range(2):
            start = pl.multiple_of(offs_ref[slot * 2 + side], 8)
            bias_f[pl.ds(start, part), :] = block[side * part : (side + 1) * part]
    factor = head_width ** (-0.5) * LOG2E
    count = q0.shape[0]
    for s in range(2 * count):
        qr, kr, vr, dr, mr = (q0, k0, v0, d0, mixed0) if s < count else (q1, k1, v1, d1, mixed1)
        at = s % count
        query, key_t, value_t, dmix = qr[at].T, kr[at], vr[at], dr[at].T
        value = value_t.T
        for r in range(0, tok, ROW_STEP):
            rows = slice(r, r + ROW_STEP)
            scores = dot(query[rows], key_t) * factor + bias_f[rows, :]
            top = jnp.max(scores, axis=1, keepdims=True)
            exps = jnp.exp2(scores - top)
            probs = exps * (1.0 / jnp.sum(exps, axis=1, keepdims=True))
            mixed = dot(probs.astype(BF16), value)
            mr[at, :, rows] = mixed.T.astype(BF16)
            d_probs = dot(dmix[rows], value_t)
            delta = jnp.sum(probs * d_probs, axis=1, keepdims=True)
            d_scores = probs * (d_probs - delta)
            if s == 0:
                grad[rows, :] = d_scores
            else:
                grad[rows, :] += d_scores
    for ky in range(yb):
        for kz in range(za):
            at = 2 * slots + (ky * za + kz) * 2
            block = jnp.concatenate(
                [grad[pl.ds(pl.multiple_of(offs_ref[at + side], 8), part), :] for side in range(2)], axis=0
            )
            if ky == 0:
                own_ref[kz, 0] = block
            else:
                codes, scale = code16(block)
                code_ref[ky - 1, kz, 0] = codes
                scale_ref[ky - 1, kz, 0] = scale


def attention_call(za, yb, head_width, offsets, bias_slots, first, own_proj, sib_proj):
    chunk, rows, tok = bias_slots[0].shape
    count = own_proj[0].shape[0]
    slots = za * yb
    head = pl.BlockSpec((count, head_width, tok), lambda h, o: (0, first + h, 0))
    mixed = pl.BlockSpec((count, head_width, tok), lambda h, o: (0, h, 0))
    away = max(yb - 1, 1)
    tiles = 2 * count * chunk
    return pl.pallas_call(
        functools.partial(attention_kernel, za, yb, head_width),
        grid_spec=pltpu.PrefetchScalarGridSpec(
            num_scalar_prefetch=1,
            grid=(chunk,),
            in_specs=[pl.BlockSpec((1, rows, tok), lambda h, o: (h, 0, 0))] * slots + [head] * 8,
            out_specs=[
                mixed,
                mixed,
                pl.BlockSpec((za, 1, rows, tok), lambda h, o: (0, h, 0, 0)),
                pl.BlockSpec((away, za, 1, rows, tok), lambda h, o: (0, 0, h, 0, 0)),
                pl.BlockSpec((away, za, 1, 1, tok), lambda h, o: (0, 0, h, 0, 0)),
            ],
            scratch_shapes=[pltpu.VMEM((tok, tok), F32), pltpu.VMEM((tok, tok), F32)],
        ),
        out_shape=[
            jax.ShapeDtypeStruct((count, chunk * head_width, tok), BF16),
            jax.ShapeDtypeStruct((count, chunk * head_width, tok), BF16),
            jax.ShapeDtypeStruct((za, chunk, rows, tok), F32),
            jax.ShapeDtypeStruct((away, za, chunk, rows, tok), jnp.int16),
            jax.ShapeDtypeStruct((away, za, chunk, 1, tok), F32),
        ],
        compiler_params=pltpu.CompilerParams(vmem_limit_bytes=VMEM_LIMIT),
        cost_estimate=pl.CostEstimate(
            flops=tiles * 6 * tok * tok * 256, bytes_accessed=int(8e6), transcendentals=tiles * tok * tok
        ),
        name="attention",
    )(offsets, *bias_slots, *own_proj, *sib_proj)


def join_kernel(za, yb, own_ref, code_ref, scale_ref, stay_ref, next_code_ref, next_scale_ref):
    for kz in range(za):
        block = own_ref[kz, 0]
        for ky in range(yb - 1):
            block = block + decode16(code_ref[ky, kz, 0], scale_ref[ky, kz, 0])
        if kz == 0:
            stay_ref[0] = block
        else:
            codes, scale = code16(block)
            next_code_ref[kz - 1, 0] = codes
            next_scale_ref[kz - 1, 0] = scale


def join_call(own, codes, scales):
    za, chunk, rows, tok = own.shape
    away = codes.shape[0]
    return pl.pallas_call(
        functools.partial(join_kernel, za, away + 1),
        grid=(chunk,),
        in_specs=[
            pl.BlockSpec((za, 1, rows, tok), lambda h: (0, h, 0, 0)),
            pl.BlockSpec((away, za, 1, rows, tok), lambda h: (0, 0, h, 0, 0)),
            pl.BlockSpec((away, za, 1, 1, tok), lambda h: (0, 0, h, 0, 0)),
        ],
        out_specs=[
            pl.BlockSpec((1, rows, tok), lambda h: (h, 0, 0)),
            pl.BlockSpec((za - 1, 1, rows, tok), lambda h: (0, h, 0, 0)),
            pl.BlockSpec((za - 1, 1, 1, tok), lambda h: (0, h, 0, 0)),
        ],
        out_shape=[
            jax.ShapeDtypeStruct((chunk, rows, tok), F32),
            jax.ShapeDtypeStruct((za - 1, chunk, rows, tok), jnp.int16),
            jax.ShapeDtypeStruct((za - 1, chunk, 1, tok), F32),
        ],
        compiler_params=pltpu.CompilerParams(vmem_limit_bytes=VMEM_LIMIT),
        cost_estimate=pl.CostEstimate(flops=int(4e6), bytes_accessed=int(6e6), transcendentals=0),
        name="join_y",
    )(own, codes, scales)


def total_kernel(count, *refs):
    stay_ref = refs[0]
    code_refs, scale_refs = refs[1 : 1 + count], refs[1 + count : 1 + 2 * count]
    own_ref, sib_ref = refs[1 + 2 * count :]
    part = own_ref.shape[1]
    block = stay_ref[0]
    for codes, scale in zip(code_refs, scale_refs):
        block = block + decode16(codes[0], scale[0])
    own_ref[0] = block[:part]
    sib_ref[0] = block[part:]


def total_call(stay, codes, scales):
    chunk, rows, tok = stay.shape
    block = pl.BlockSpec((1, rows, tok), lambda h: (h, 0, 0))
    row = pl.BlockSpec((1, 1, tok), lambda h: (h, 0, 0))
    out = pl.BlockSpec((1, rows // 2, tok), lambda h: (h, 0, 0))
    return pl.pallas_call(
        functools.partial(total_kernel, len(codes)),
        grid=(chunk,),
        in_specs=[block] * (1 + len(codes)) + [row] * len(scales),
        out_specs=[out, out],
        out_shape=[jax.ShapeDtypeStruct((chunk, rows // 2, tok), F32)] * 2,
        compiler_params=pltpu.CompilerParams(vmem_limit_bytes=VMEM_LIMIT),
        cost_estimate=pl.CostEstimate(flops=int(2e6), bytes_accessed=int(3e6), transcendentals=0),
        name="join_z",
    )(stay, *codes, *scales)


def output_kernel(parts, core_ref, *refs):
    own_refs, other_refs = refs[:parts], refs[parts : 2 * parts]
    w_own, w_other, mask_ref, out_ref = refs[2 * parts :]
    live = mask_ref[...] > 0
    total = None
    for group, weight in ((own_refs, w_own), (other_refs, w_other)):
        start = 0
        for ref in group:
            size = ref.shape[1]
            mixed = ref[0]
            mixed = jnp.where(live, mixed.astype(F32), 0.0).T.astype(BF16)
            term = dot(mixed, weight[start : start + size, :])
            total = term if total is None else total + term
            start += size
    out_ref[0] = total.astype(BF16)


def output_call(core, own, other, w_out, mask_row):
    samples, size, tok = own[0].shape
    parts = len(own)
    width = w_out.shape[0]
    half = width // 2
    block = pl.BlockSpec((1, size, tok), lambda s, c: (s, 0, 0))
    return pl.pallas_call(
        functools.partial(output_kernel, parts),
        grid_spec=pltpu.PrefetchScalarGridSpec(
            num_scalar_prefetch=1,
            grid=(samples,),
            in_specs=[block] * (2 * parts)
            + [
                pl.BlockSpec((half, width), lambda s, c: (c[0], 0)),
                pl.BlockSpec((half, width), lambda s, c: (1 - c[0], 0)),
                pl.BlockSpec((1, tok), lambda s, c: (0, 0)),
            ],
            out_specs=pl.BlockSpec((1, tok, width), lambda s, c: (s, 0, 0)),
        ),
        out_shape=jax.ShapeDtypeStruct((samples, tok, width), BF16),
        compiler_params=pltpu.CompilerParams(vmem_limit_bytes=VMEM_LIMIT),
        cost_estimate=pl.CostEstimate(
            flops=2 * samples * tok * width * width, bytes_accessed=int(4e6), transcendentals=0
        ),
        name="output",
    )(core, *own, *other, w_out, w_out, mask_row)


def load_rows(refs, i):
    return jnp.concatenate([ref[:, i, :] for ref in refs], axis=0)


def projection_kernel(parts, core_ref, *refs):
    own_refs, other_refs = refs[:parts], refs[parts : 2 * parts]
    pair_ref, gain_ref, mean_ref, rstd_ref, out_ref = refs[2 * parts :]
    rows, tok, chan = pair_ref.shape
    heads = out_ref.shape[0]
    half = heads // 2
    total = jnp.zeros((3 * heads, chan), F32)
    means = jnp.zeros((heads, tok), F32)
    for i in range(rows):
        grads = load_rows([*own_refs, *other_refs], i) * rstd_ref[i : i + 1, :]
        means = means + grads * mean_ref[i : i + 1, :]
        total = total + dot(jnp.concatenate(pieces3(grads), axis=0), pair_ref[i])
    raw = total[:heads] + (total[heads : 2 * heads] + total[2 * heads :])
    result = (raw - jnp.sum(means, axis=1, keepdims=True)) * gain_ref[...]
    core = core_ref[0]
    out_ref[pl.ds(pl.multiple_of(core * half, half), half), :] = result[:half]
    out_ref[pl.ds(pl.multiple_of((1 - core) * half, half), half), :] = result[half:]


def pair_grad_kernel(parts, core_ref, *refs):
    own_refs, other_refs = refs[:parts], refs[parts : 2 * parts]
    pair_ref, gain_ref, wt_ref, rstd_ref, out_ref = refs[2 * parts :]
    rows, tok, chan = pair_ref.shape
    half = wt_ref.shape[0] // 2
    core = core_ref[0]
    weights = jnp.concatenate(
        [
            wt_ref[pl.ds(pl.multiple_of(core * half, half), half), :],
            wt_ref[pl.ds(pl.multiple_of((1 - core) * half, half), half), :],
        ],
        axis=0,
    )
    scaled = weights * gain_ref[...]
    scaled = scaled - jnp.mean(scaled, axis=1, keepdims=True)
    wh, wm, wl = pieces3(scaled)
    right = jnp.concatenate([wh, wm, wh, wl, wm, wh], axis=0)
    for i in range(rows):
        grads = load_rows([*own_refs, *other_refs], i) * rstd_ref[i : i + 1, :]
        gh, gm, gl = pieces3(grads)
        left = jnp.concatenate([gh, gh, gm, gh, gm, gl], axis=0)
        slope = dot(left, right, TN)
        values = pair_ref[i].astype(F32)
        diff = values - jnp.sum(values, axis=1, keepdims=True) * (1.0 / chan)
        spread = jnp.sum(diff * diff, axis=1, keepdims=True) * (1.0 / chan)
        along = jnp.sum(slope * diff, axis=1, keepdims=True) * (1.0 / chan)
        out_ref[i] = (slope - diff * (along / (spread + 1e-05))).astype(BF16)


def final_call(kernel, name, core, own, other, operands, out_shape):
    vm = pl.BlockSpec(memory_space=pltpu.VMEM)
    parts = len(own)
    return pl.pallas_call(
        functools.partial(kernel, parts),
        in_specs=[pl.BlockSpec(memory_space=pltpu.SMEM)] + [vm] * (2 * parts + len(operands)),
        out_specs=vm,
        out_shape=out_shape,
        compiler_params=pltpu.CompilerParams(vmem_limit_bytes=VMEM_LIMIT),
        cost_estimate=pl.CostEstimate(flops=int(4e9), bytes_accessed=int(8e6), transcendentals=0),
        name=name,
    )(core, *own, *other, *operands)


def grid_of(devices):
    chips = devices // 2
    yb = 1 << ((chips.bit_length() - 1) // 2)
    return chips // yb, yb


def per_device_tiled(
    devices, activations, cotangent, pair_rep, pair_gain, w_pair, w_query, w_key, w_value, w_out, token_mask
):
    za, yb = grid_of(devices)
    rows, tok, chan = pair_rep.shape
    heads = w_pair.shape[1]
    half = heads // 2
    head_width = w_query.shape[0] // heads
    me = lax.axis_index("smp")
    core = lax.rem(me, 2)
    chip = me // 2
    my_z, my_y = chip // yb, lax.rem(chip, yb)

    def swap_core(x):
        return lax.ppermute(x, "smp", [(d, d ^ 1) for d in range(devices)])

    def shift(x, kz, ky):
        perm = []
        for d in range(devices):
            z, y, c = d // 2 // yb, d // 2 % yb, d % 2
            perm.append((d, (((z + kz) % za) * yb + (y + ky) % yb) * 2 + c))
        return lax.ppermute(x, "smp", perm)

    offsets = []
    for sign in (-1, 1):
        for ky in range(yb):
            for kz in range(za):
                there = lax.rem(my_z + sign * kz + za, za) * yb + lax.rem(my_y + sign * ky + yb, yb)
                offsets += [there * 2 * rows + core * rows, there * 2 * rows + (1 - core) * rows]
    offsets = jnp.stack(offsets).astype(jnp.int32)
    core_1 = core.reshape(1).astype(jnp.int32)
    gain = pair_gain.reshape(1, chan)
    w_t = w_pair.T.astype(F32)
    mask_row = token_mask.reshape(1, tok)

    sib_act, sib_cot = swap_core(activations), swap_core(cotangent)
    bias_own, bias_other, mean_rows, rstd_rows = bias_call(core_1, pair_rep, gain, w_t, mask_row)
    bias_chip = jnp.concatenate([bias_own, swap_core(bias_other)], axis=1)

    chunk = half // HEAD_CHUNKS
    slots = []
    for n in range(HEAD_CHUNKS):
        mine = bias_chip[n * chunk : (n + 1) * chunk]
        column = [mine] + [shift(mine, kz, 0) for kz in range(1, za)]
        slots.append([shift(block, 0, ky) if ky else block for ky in range(yb) for block in column])
    weights = (w_query, w_key, w_value, w_out)
    own_proj = project_call(core_1, activations, cotangent, *weights, mask_row)
    sib_proj = project_call(core_1, sib_act, sib_cot, *weights, mask_row)

    mixed_own, mixed_other, grads_own, grads_other = [], [], [], []
    for n in range(HEAD_CHUNKS):
        mixed0, mixed1, own, codes, scales = attention_call(
            za, yb, head_width, offsets, slots[n], n * chunk, own_proj, sib_proj
        )
        mixed_own.append(mixed0)
        mixed_other.append(swap_core(mixed1))
        far_codes = jnp.stack([shift(codes[ky - 1], 0, ky) for ky in range(1, yb)]) if yb > 2 else shift(codes, 0, 1)
        far_scales = jnp.stack([shift(scales[ky - 1], 0, ky) for ky in range(1, yb)]) if yb > 2 else shift(scales, 0, 1)
        stay, codes, scales = join_call(own, far_codes, far_scales)
        codes = [shift(codes[kz - 1], kz, 0) for kz in range(1, za)]
        scales = [shift(scales[kz - 1], kz, 0) for kz in range(1, za)]
        here, there = total_call(stay, codes, scales)
        grads_own.append(here)
        grads_other.append(swap_core(there))

    attended = output_call(core_1, mixed_own, mixed_other, w_out, mask_row)
    projection = final_call(
        projection_kernel, "pair_projection", core_1, grads_own, grads_other,
        (pair_rep, gain, mean_rows, rstd_rows), jax.ShapeDtypeStruct((heads, chan), F32),
    )
    step = 1
    while step < devices:
        projection = projection + lax.ppermute(projection, "smp", [(d, d ^ step) for d in range(devices)])
        step *= 2
    grad_pair = final_call(
        pair_grad_kernel, "pair_gradient", core_1, grads_own, grads_other,
        (pair_rep, gain, w_t, rstd_rows), jax.ShapeDtypeStruct(pair_rep.shape, BF16),
    )
    return (attended, grad_pair, projection.T)


def per_device(devices, activations, *rest):
    pair_rep, w_pair = rest[1], rest[3]
    rows, heads = pair_rep.shape[0], w_pair.shape[1]
    power = devices >= 8 and devices & (devices - 1) == 0
    if power and rows % 8 == 0 and heads % (2 * HEAD_CHUNKS) == 0 and pair_rep.shape[1] % ROW_STEP == 0:
        return per_device_tiled(devices, activations, *rest)
    return per_device_plain(activations, *rest)


def solution(mesh):
    split = P(("grp", "smp"), None, None)
    return jax.shard_map(
        functools.partial(per_device, mesh.shape["smp"]),
        mesh=mesh,
        in_specs=(split, split, split, P(), P(), P(), P(), P(), P(), P("grp")),
        out_specs=(split, split, P("grp", None)),
        check_vma=False,
    )
```

profile of v0, /device:TPU:0, one launch (start us, length us, event | category | flops | bytes accessed | tf_op | source)
XLA Modules:
  0.0 162.4 jit_solution(5804898823029743534)
XLA Ops:
  1.2 0.7 reshape.17.mask_ref.refs_6_
  1.9 0.7 convert_bitcast_fusion.wt_ref.refs_6_
  2.6 1.7 %copy-done.7 = bf16[24,384,128]{2,1,0:T(8,128)(2,1)S(1)} copy-done((bf16[24,384,128]{2,1,0:T(8,128)(2,1)S(1)}, bf16[24,384,128]{2,1,0:T(8,128)(2,1)}, u32[]{:S(2)}) %copy-start.7) | copy-done | bytes 2359320
  4.9 7.1 %pair_bias.1 = (bf16[8,24,384]{2,1,0:T(8,128)(2,1)S(1)}, bf16[8,24,384]{2,1,0:T(8,128)(2,1)S(1)}, f32[24,384]{1,0:T(8,128)S(1)}, f32[24,384]{1,0:T(8,128)S(1)}) custom-call(s32[1]{0:T(128)} %bitcast.core_ref, bf16[24,384,128]{2,1,0:T(8,128)(2,1)S(1)} %copy-done.7, f32[1,128]{1,0:T(1,128)S(1)} %bitcast.60, f32[16,128]{1,0:T(8,128)S(1)} %convert_bitcast_fusion.wt_ref.refs_6_, ...), custom_call_target="tpu_custom_call" | custom-call | flops 6000000000 | bytes 4000000 | tf_op jit(solution)/shard_map/pair_bias/pallas_call | solution.py:142
  13.7 1.0 collective-permute-done
  14.7 0.7 fusion
  15.5 2.9 %collective-permute-start.10 = (bf16[4,48,384]{2,1,0:T(8,128)(2,1)}, bf16[4,48,384]{2,1,0:T(8,128)(2,1)}, u32[]{:S(2)}, u32[]{:S(2)}) collective-permute-start(bf16[4,48,384]{2,1,0:T(8,128)(2,1)} %get-tuple-element.73.refs_0_), channel_id=1, source_target_pairs={{0,4},{1,5},{2,6},{3,7},{4,8},{5,9},{6,10},{7,11},{8,12},{9,13},{1... | collective-permute-start | bytes 442376 | tf_op jit(solution)/shard_map/ppermute | solution.py:496
  18.4 2.6 %collective-permute-start.11 = (bf16[4,48,384]{2,1,0:T(8,128)(2,1)}, bf16[4,48,384]{2,1,0:T(8,128)(2,1)}, u32[]{:S(2)}, u32[]{:S(2)}) collective-permute-start(bf16[4,48,384]{2,1,0:T(8,128)(2,1)} %get-tuple-element.73.refs_0_), channel_id=1, source_target_pairs={{0,8},{1,9},{2,10},{3,11},{4,12},{5,13},{6,14},{7,15},{8,0},{9,1},... | collective-permute-start | bytes 442376 | tf_op jit(solution)/shard_map/ppermute | solution.py:496
  21.1 1.4 collective-permute-start.12
  22.5 3.0 %collective-permute-done.10.refs_1_ = bf16[4,48,384]{2,1,0:T(8,128)(2,1)} collective-permute-done((bf16[4,48,384]{2,1,0:T(8,128)(2,1)}, bf16[4,48,384]{2,1,0:T(8,128)(2,1)}, u32[]{:S(2)}, u32[]{:S(2)}) %collective-permute-start.10) | collective-permute-done | bytes 147488 | tf_op jit(solution)/shard_map/ppermute | solution.py:496
  25.5 1.8 %collective-permute-start.13 = (bf16[4,48,384]{2,1,0:T(8,128)(2,1)}, bf16[4,48,384]{2,1,0:T(8,128)(2,1)S(1)}, u32[]{:S(2)}, u32[]{:S(2)}) collective-permute-start(bf16[4,48,384]{2,1,0:T(8,128)(2,1)} %get-tuple-element.73.refs_0_), channel_id=1, source_target_pairs={{0,2},{1,3},{2,0},{3,1},{4,6},{5,7},{6,4},{7,5},{8,10},{9,11},{10,... | collective-permute-start | bytes 442376 | tf_op jit(solution)/shard_map/ppermute | solution.py:496
  27.3 4.1 %collective-permute-done.11.refs_2_ = bf16[4,48,384]{2,1,0:T(8,128)(2,1)} collective-permute-done((bf16[4,48,384]{2,1,0:T(8,128)(2,1)}, bf16[4,48,384]{2,1,0:T(8,128)(2,1)}, u32[]{:S(2)}, u32[]{:S(2)}) %collective-permute-start.11) | collective-permute-done | bytes 147488 | tf_op jit(solution)/shard_map/ppermute | solution.py:496
  31.3 1.9 %collective-permute-start.1 = (bf16[4,48,384]{2,1,0:T(8,128)(2,1)}, bf16[4,48,384]{2,1,0:T(8,128)(2,1)S(1)}, u32[]{:S(2)}, u32[]{:S(2)}) collective-permute-start(bf16[4,48,384]{2,1,0:T(8,128)(2,1)} %get-tuple-element.74.refs_0_), channel_id=1, source_target_pairs={{0,4},{1,5},{2,6},{3,7},{4,8},{5,9},{6,10},{7,11},{8,12},{9,13},{1... | collective-permute-start | bytes 442376 | tf_op jit(solution)/shard_map/ppermute | solution.py:496
  33.2 4.3 %projections.2 = (bf16[2,384,384]{2,1,0:T(8,128)(2,1)S(1)}, bf16[2,384,384]{2,1,0:T(8,128)(2,1)S(1)}, bf16[2,384,384]{2,1,0:T(8,128)(2,1)S(1)}, bf16[2,384,384]{2,1,0:T(8,128)(2,1)S(1)}) custom-call(s32[1]{0:T(128)} %bitcast.core_ref, bf16[2,384,768]{2,1,0:T(8,128)(2,1)S(1)} %copy-done.4, bf16[2,384,768]{2,1,0:T(8,128)(2,1)S(1)} %copy-done.5, ...), custom_call_target="tpu_custom_call" | custom-call | flops 1811939328 | bytes 6000000 | tf_op jit(solution)/shard_map/projections/pallas_call | solution.py:173
  37.6 3.4 %collective-permute-start.2 = (bf16[4,48,384]{2,1,0:T(8,128)(2,1)S(1)}, bf16[4,48,384]{2,1,0:T(8,128)(2,1)S(1)}, u32[]{:S(2)}, u32[]{:S(2)}) collective-permute-start(bf16[4,48,384]{2,1,0:T(8,128)(2,1)S(1)} %copy-done.6), channel_id=1, source_target_pairs={{0,8},{1,9},{2,10},{3,11},{4,12},{5,13},{6,14},{7,15},{8,0},{9,1},... | collective-permute-start | bytes 442376 | tf_op jit(solution)/shard_map/ppermute | solution.py:496
  41.7 1.0 collective-permute-start.14
  42.6 1.1 collective-permute-start.15
  43.7 1.0 collective-permute-start.16
  44.7 4.6 %projections.3 = (bf16[2,384,384]{2,1,0:T(8,128)(2,1)S(1)}, bf16[2,384,384]{2,1,0:T(8,128)(2,1)S(1)}, bf16[2,384,384]{2,1,0:T(8,128)(2,1)S(1)}, bf16[2,384,384]{2,1,0:T(8,128)(2,1)S(1)}) custom-call(s32[1]{0:T(128)} %bitcast.core_ref, bf16[2,384,768]{2,1,0:T(8,128)(2,1)} %collective-permute-done.8.act_ref, ...), custom_call_target="tpu_custom_call" | custom-call | flops 1811939328 | bytes 6000000 | tf_op jit(solution)/shard_map/projections/pallas_call | solution.py:173
  49.3 0.8 copy-done.9
  50.1 0.8 copy-done.10
  51.0 1.1 collective-permute-start.4
  52.0 1.0 collective-permute-start.5
  53.0 1.1 collective-permute-start.6
  54.1 1.0 collective-permute-start.7
  55.0 21.7 %attention.3 = (bf16[2,192,384]{2,1,0:T(8,128)(2,1)S(1)}, bf16[2,192,384]{2,1,0:T(8,128)(2,1)S(1)}, f32[4,4,48,384]{3,2,1,0:T(8,128)}, s16[1,4,4,48,384]{4,3,2,1,0:T(8,128)(2,1)S(1)}, f32[1,4,4,1,384]{4,3,2,1,0:T(1,128)S(1)}) custom-call(s32[32]{0:T(128)S(1)} %stack.125.offs_ref, bf16[4,48,384]{2,1,0:T(8,128)(2,1)} %get-tuple-element.73.refs_0_, ...), custom_call_target="tpu_custom_call" | custom-call | flops 3623878656 | bytes 8000000 | tf_op jit(solution)/shard_map/attention/pallas_call | solution.py:259
  76.8 1.1 collective-permute-start.27
  77.9 21.7 %attention.2 = (bf16[2,192,384]{2,1,0:T(8,128)(2,1)S(1)}, bf16[2,192,384]{2,1,0:T(8,128)(2,1)S(1)}, f32[4,4,48,384]{3,2,1,0:T(8,128)}, s16[1,4,4,48,384]{4,3,2,1,0:T(8,128)(2,1)S(1)}, f32[1,4,4,1,384]{4,3,2,1,0:T(1,128)S(1)}) custom-call(s32[32]{0:T(128)S(1)} %stack.125.offs_ref, bf16[4,48,384]{2,1,0:T(8,128)(2,1)S(1)} %copy-done.6, ...), custom_call_target="tpu_custom_call" | custom-call | flops 3623878656 | bytes 8000000 | tf_op jit(solution)/shard_map/attention/pallas_call | solution.py:259
  99.6 1.0 collective-permute-start.19
  100.5 1.1 collective-permute-start.28
  101.6 1.0 collective-permute-start.20
  102.6 9.0 %collective-permute-done.28.scale_ref = f32[1,4,4,1,384]{4,3,2,1,0:T(1,128)S(1)} collective-permute-done((f32[1,4,4,1,384]{4,3,2,1,0:T(1,128)S(1)}, f32[1,4,4,1,384]{4,3,2,1,0:T(1,128)S(1)}, u32[]{:S(2)}, u32[]{:S(2)}) %collective-permute-start.28) | collective-permute-done | bytes 24608 | tf_op jit(solution)/shard_map/ppermute | solution.py:496
  112.3 1.7 %collective-permute-start.29 = (s16[4,48,384]{2,1,0:T(8,128)(2,1)S(1)}, s16[4,48,384]{2,1,0:T(8,128)(2,1)S(1)}, u32[]{:S(2)}, u32[]{:S(2)}) collective-permute-start(s16[4,48,384]{2,1,0:T(8,128)(2,1)S(1)} %get-tuple-element.69), channel_id=1, source_target_pairs={{0,4},{1,5},{2,6},{3,7},{4,8},{5,9},{6,10},{7,11},{8,12},{9,13},{1... | collective-permute-start | bytes 442376 | tf_op jit(solution)/shard_map/ppermute | solution.py:496
  114.0 2.6 %collective-permute-start.30 = (s16[4,48,384]{2,1,0:T(8,128)(2,1)S(1)}, s16[4,48,384]{2,1,0:T(8,128)(2,1)S(1)}, u32[]{:S(2)}, u32[]{:S(2)}) collective-permute-start(s16[4,48,384]{2,1,0:T(8,128)(2,1)S(1)} %get-tuple-element.68), channel_id=1, source_target_pairs={{0,8},{1,9},{2,10},{3,11},{4,12},{5,13},{6,14},{7,15},{8,0},{9,1},... | collective-permute-start | bytes 442376 | tf_op jit(solution)/shard_map/ppermute | solution.py:496
  116.7 2.0 %collective-permute-start.32 = (f32[4,1,384]{2,1,0:T(1,128)S(1)}, f32[4,1,384]{2,1,0:T(1,128)S(1)}, u32[]{:S(2)}, u32[]{:S(2)}) collective-permute-start(f32[4,1,384]{2,1,0:T(1,128)S(1)} %get-tuple-element.77), channel_id=1, source_target_pairs={{0,4},{1,5},{2,6},{3,7},{4,8},{5,9},{6,10},{7,11},{8,12},{9,13},{1... | collective-permute-start | bytes 18440 | tf_op jit(solution)/shard_map/ppermute | solution.py:496
  119.7 3.3 %collective-permute-done.32.refs_4_ = f32[4,1,384]{2,1,0:T(1,128)S(1)} collective-permute-done((f32[4,1,384]{2,1,0:T(1,128)S(1)}, f32[4,1,384]{2,1,0:T(1,128)S(1)}, u32[]{:S(2)}, u32[]{:S(2)}) %collective-permute-start.32) | collective-permute-done | bytes 6176 | tf_op jit(solution)/shard_map/ppermute | solution.py:496
  123.0 3.2 %collective-permute-done.33.refs_5_ = f32[4,1,384]{2,1,0:T(1,128)S(1)} collective-permute-done((f32[4,1,384]{2,1,0:T(1,128)S(1)}, f32[4,1,384]{2,1,0:T(1,128)S(1)}, u32[]{:S(2)}, u32[]{:S(2)}) %collective-permute-start.33) | collective-permute-done | bytes 6176 | tf_op jit(solution)/shard_map/ppermute | solution.py:496
  126.6 1.9 %collective-permute-start.21 = (s16[4,48,384]{2,1,0:T(8,128)(2,1)S(1)}, s16[4,48,384]{2,1,0:T(8,128)(2,1)S(1)}, u32[]{:S(2)}, u32[]{:S(2)}) collective-permute-start(s16[4,48,384]{2,1,0:T(8,128)(2,1)S(1)} %get-tuple-element.72), channel_id=1, source_target_pairs={{0,4},{1,5},{2,6},{3,7},{4,8},{5,9},{6,10},{7,11},{8,12},{9,13},{1... | collective-permute-start | bytes 442376 | tf_op jit(solution)/shard_map/ppermute | solution.py:496
  128.6 3.2 %collective-permute-done.24.refs_4_ = f32[4,1,384]{2,1,0:T(1,128)S(1)} collective-permute-done((f32[4,1,384]{2,1,0:T(1,128)S(1)}, f32[4,1,384]{2,1,0:T(1,128)S(1)}, u32[]{:S(2)}, u32[]{:S(2)}) %collective-permute-start.24) | collective-permute-done | bytes 6176 | tf_op jit(solution)/shard_map/ppermute | solution.py:496
  131.8 1.2 collective-permute-start.23
  133.0 1.8 %collective-permute-start.25 = (f32[4,1,384]{2,1,0:T(1,128)S(1)}, f32[4,1,384]{2,1,0:T(1,128)S(1)}, u32[]{:S(2)}, u32[]{:S(2)}) collective-permute-start(f32[4,1,384]{2,1,0:T(1,128)S(1)} %get-tuple-element.79), channel_id=1, source_target_pairs={{0,8},{1,9},{2,10},{3,11},{4,12},{5,13},{6,14},{7,15},{8,0},{9,1},... | collective-permute-start | bytes 18440 | tf_op jit(solution)/shard_map/ppermute | solution.py:496
  134.8 1.7 %collective-permute-start.26 = (f32[4,1,384]{2,1,0:T(1,128)S(1)}, f32[4,1,384]{2,1,0:T(1,128)S(1)}, u32[]{:S(2)}, u32[]{:S(2)}) collective-permute-start(f32[4,1,384]{2,1,0:T(1,128)S(1)} %get-tuple-element.78), channel_id=1, source_target_pairs={{0,12},{1,13},{2,14},{3,15},{4,0},{5,1},{6,2},{7,3},{8,4},{9,5},{1... | collective-permute-start | bytes 18440 | tf_op jit(solution)/shard_map/ppermute | solution.py:496
  136.6 5.5 %collective-permute-done.25.refs_5_ = f32[4,1,384]{2,1,0:T(1,128)S(1)} collective-permute-done((f32[4,1,384]{2,1,0:T(1,128)S(1)}, f32[4,1,384]{2,1,0:T(1,128)S(1)}, u32[]{:S(2)}, u32[]{:S(2)}) %collective-permute-start.25) | collective-permute-done | bytes 6176 | tf_op jit(solution)/shard_map/ppermute | solution.py:496
  145.0 0.8 collective-permute-done.37
  145.8 3.6 %collective-permute-done.38 = f32[16,128]{1,0:T(8,128)S(1)} collective-permute-done((f32[16,128]{1,0:T(8,128)S(1)}, f32[16,128]{1,0:T(8,128)S(1)}, u32[]{:S(2)}, u32[]{:S(2)}) %collective-permute-start.38) | collective-permute-done | bytes 8224 | tf_op jit(solution)/shard_map/ppermute | solution.py:547
  150.0 2.5 %output.1 = bf16[2,384,768]{2,1,0:T(8,128)(2,1)} custom-call(s32[1]{0:T(128)} %bitcast.core_ref, bf16[2,192,384]{2,1,0:T(8,128)(2,1)S(1)} %get-tuple-element.45.refs_0_, bf16[2,192,384]{2,1,0:T(8,128)(2,1)S(1)} %get-tuple-element.46.refs_1_, bf16[2,192,384]{2,1,0:T(8,128)(2,1)S(1)} %collective-permute-done.17.refs_2_, ...), custom_call_target="tpu_custom_call" | custom-call | flops 905969664 | bytes 4000000 | tf_op jit(solution)/shard_map/output/pallas_call | solution.py:381
  153.2 1.2 collective-permute-start.40
  154.3 7.5 %pair_gradient.1 = bf16[24,384,128]{2,1,0:T(8,128)(2,1)} custom-call(s32[1]{0:T(128)} %bitcast.core_ref, f32[4,24,384]{2,1,0:T(8,128)S(1)} %get-tuple-element.55.refs_0_, f32[4,24,384]{2,1,0:T(8,128)S(1)} %get-tuple-element.62.refs_1_, f32[4,24,384]{2,1,0:T(8,128)S(1)} %collective-permute-done.35.refs_2_, f32[4,24,384]{2,1,0:T(8,128)S(1)} %collective-permute-done.36.refs_3_, ...), custom_call_target="tpu_custom_call" | custom-call | flops 4000000000 | bytes 8000000 | tf_op jit(solution)/shard_map/pair_gradient/pallas_call | solution.py:458
  (94 shorter events, 10.8 us)
Async XLA Ops:
  0.6 42.0 %collective-permute-start.8 = (bf16[2,384,768]{2,1,0:T(8,128)(2,1)}, bf16[2,384,768]{2,1,0:T(8,128)(2,1)}, u32[]{:S(2)}, u32[]{:S(2)}) collective-permute-start(bf16[2,384,768]{2,1,0:T(8,128)(2,1)} %act_ref.1), channel_id=1, source_target_pairs={{0,1},{1,0},{2,3},{3,2},{4,5},{5,4},{6,7},{7,6},{8,9},{9,8},{10,11... | collective-permute-start | bytes 3538952 | tf_op jit(solution)/shard_map/ppermute | solution.py:489
  1.1 42.5 %collective-permute-start.9 = (bf16[2,384,768]{2,1,0:T(8,128)(2,1)}, bf16[2,384,768]{2,1,0:T(8,128)(2,1)}, u32[]{:S(2)}, u32[]{:S(2)}) collective-permute-start(bf16[2,384,768]{2,1,0:T(8,128)(2,1)} %cot_ref.1), channel_id=1, source_target_pairs={{0,1},{1,0},{2,3},{3,2},{4,5},{5,4},{6,7},{7,6},{8,9},{9,8},{10,11... | collective-permute-start | bytes 3538952 | tf_op jit(solution)/shard_map/ppermute | solution.py:489
  4.9 28.3 %copy-start.4 = (bf16[2,384,768]{2,1,0:T(8,128)(2,1)S(1)}, bf16[2,384,768]{2,1,0:T(8,128)(2,1)}, u32[]{:S(2)}) copy-start(bf16[2,384,768]{2,1,0:T(8,128)(2,1)} %act_ref.1) | copy-start | bytes 3538948
  4.9 28.3 %copy-start.5 = (bf16[2,384,768]{2,1,0:T(8,128)(2,1)S(1)}, bf16[2,384,768]{2,1,0:T(8,128)(2,1)}, u32[]{:S(2)}) copy-start(bf16[2,384,768]{2,1,0:T(8,128)(2,1)} %cot_ref.1) | copy-start | bytes 3538948
  13.3 19.9 %copy-start.1 = (bf16[768,768]{1,0:T(8,128)(2,1)S(1)}, bf16[768,768]{1,0:T(8,128)(2,1)}, u32[]{:S(2)}) copy-start(bf16[768,768]{1,0:T(8,128)(2,1)} %wq_ref.3) | copy-start | bytes 3538948
  13.3 1.4 collective-permute-start
  15.5 10.0 %collective-permute-start.10 = (bf16[4,48,384]{2,1,0:T(8,128)(2,1)}, bf16[4,48,384]{2,1,0:T(8,128)(2,1)}, u32[]{:S(2)}, u32[]{:S(2)}) collective-permute-start(bf16[4,48,384]{2,1,0:T(8,128)(2,1)} %get-tuple-element.73.refs_0_), channel_id=1, source_target_pairs={{0,4},{1,5},{2,6},{3,7},{4,8},{5,9},{6,10},{7,11},{8,12},{9,13},{1... | collective-permute-start | bytes 442376 | tf_op jit(solution)/shard_map/ppermute | solution.py:496
  18.4 12.9 %collective-permute-start.11 = (bf16[4,48,384]{2,1,0:T(8,128)(2,1)}, bf16[4,48,384]{2,1,0:T(8,128)(2,1)}, u32[]{:S(2)}, u32[]{:S(2)}) collective-permute-start(bf16[4,48,384]{2,1,0:T(8,128)(2,1)} %get-tuple-element.73.refs_0_), channel_id=1, source_target_pairs={{0,8},{1,9},{2,10},{3,11},{4,12},{5,13},{6,14},{7,15},{8,0},{9,1},... | collective-permute-start | bytes 442376 | tf_op jit(solution)/shard_map/ppermute | solution.py:496
  21.1 16.5 %collective-permute-start.12 = (bf16[4,48,384]{2,1,0:T(8,128)(2,1)}, bf16[4,48,384]{2,1,0:T(8,128)(2,1)S(1)}, u32[]{:S(2)}, u32[]{:S(2)}) collective-permute-start(bf16[4,48,384]{2,1,0:T(8,128)(2,1)} %get-tuple-element.73.refs_0_), channel_id=1, source_target_pairs={{0,12},{1,13},{2,14},{3,15},{4,0},{5,1},{6,2},{7,3},{8,4},{9,5},{1... | collective-permute-start | bytes 442376 | tf_op jit(solution)/shard_map/ppermute | solution.py:496
  25.5 15.5 %collective-permute-start.13 = (bf16[4,48,384]{2,1,0:T(8,128)(2,1)}, bf16[4,48,384]{2,1,0:T(8,128)(2,1)S(1)}, u32[]{:S(2)}, u32[]{:S(2)}) collective-permute-start(bf16[4,48,384]{2,1,0:T(8,128)(2,1)} %get-tuple-element.73.refs_0_), channel_id=1, source_target_pairs={{0,2},{1,3},{2,0},{3,1},{4,6},{5,7},{6,4},{7,5},{8,10},{9,11},{10,... | collective-permute-start | bytes 442376 | tf_op jit(solution)/shard_map/ppermute | solution.py:496
  31.3 10.3 %collective-permute-start.1 = (bf16[4,48,384]{2,1,0:T(8,128)(2,1)}, bf16[4,48,384]{2,1,0:T(8,128)(2,1)S(1)}, u32[]{:S(2)}, u32[]{:S(2)}) collective-permute-start(bf16[4,48,384]{2,1,0:T(8,128)(2,1)} %get-tuple-element.74.refs_0_), channel_id=1, source_target_pairs={{0,4},{1,5},{2,6},{3,7},{4,8},{5,9},{6,10},{7,11},{8,12},{9,13},{1... | collective-permute-start | bytes 442376 | tf_op jit(solution)/shard_map/ppermute | solution.py:496
  37.6 13.4 %collective-permute-start.2 = (bf16[4,48,384]{2,1,0:T(8,128)(2,1)S(1)}, bf16[4,48,384]{2,1,0:T(8,128)(2,1)S(1)}, u32[]{:S(2)}, u32[]{:S(2)}) collective-permute-start(bf16[4,48,384]{2,1,0:T(8,128)(2,1)S(1)} %copy-done.6), channel_id=1, source_target_pairs={{0,8},{1,9},{2,10},{3,11},{4,12},{5,13},{6,14},{7,15},{8,0},{9,1},... | collective-permute-start | bytes 442376 | tf_op jit(solution)/shard_map/ppermute | solution.py:496
  41.0 11.0 %collective-permute-start.3 = (bf16[4,48,384]{2,1,0:T(8,128)(2,1)S(1)}, bf16[4,48,384]{2,1,0:T(8,128)(2,1)S(1)}, u32[]{:S(2)}, u32[]{:S(2)}) collective-permute-start(bf16[4,48,384]{2,1,0:T(8,128)(2,1)S(1)} %copy-done.6), channel_id=1, source_target_pairs={{0,12},{1,13},{2,14},{3,15},{4,0},{5,1},{6,2},{7,3},{8,4},{9,5},{1... | collective-permute-start | bytes 442376 | tf_op jit(solution)/shard_map/ppermute | solution.py:496
  41.7 11.4 %collective-permute-start.14 = (bf16[4,48,384]{2,1,0:T(8,128)(2,1)}, bf16[4,48,384]{2,1,0:T(8,128)(2,1)S(1)}, u32[]{:S(2)}, u32[]{:S(2)}) collective-permute-start(bf16[4,48,384]{2,1,0:T(8,128)(2,1)} %collective-permute-done.10.refs_1_), channel_id=1, source_target_pairs={{0,2},{1,3},{2,0},{3,1},{4,6},{5,7},{6,4},{7,5},{8,10},{9,11},{10,... | collective-permute-start | bytes 442376 | tf_op jit(solution)/shard_map/ppermute | solution.py:496
  42.6 11.4 %collective-permute-start.15 = (bf16[4,48,384]{2,1,0:T(8,128)(2,1)}, bf16[4,48,384]{2,1,0:T(8,128)(2,1)S(1)}, u32[]{:S(2)}, u32[]{:S(2)}) collective-permute-start(bf16[4,48,384]{2,1,0:T(8,128)(2,1)} %collective-permute-done.11.refs_2_), channel_id=1, source_target_pairs={{0,2},{1,3},{2,0},{3,1},{4,6},{5,7},{6,4},{7,5},{8,10},{9,11},{10,... | collective-permute-start | bytes 442376 | tf_op jit(solution)/shard_map/ppermute | solution.py:496
  43.7 11.4 %collective-permute-start.16 = (bf16[4,48,384]{2,1,0:T(8,128)(2,1)S(1)}, bf16[4,48,384]{2,1,0:T(8,128)(2,1)S(1)}, u32[]{:S(2)}, u32[]{:S(2)}) collective-permute-start(bf16[4,48,384]{2,1,0:T(8,128)(2,1)S(1)} %collective-permute-done.12.refs_3_), channel_id=1, source_target_pairs={{0,2},{1,3},{2,0},{3,1},{4,6},{5,7},{6,4},{7,5},{8,10},{9,11},{10,... | collective-permute-start | bytes 442376 | tf_op jit(solution)/shard_map/ppermute | solution.py:496
  51.0 26.9 %collective-permute-start.4 = (bf16[4,48,384]{2,1,0:T(8,128)(2,1)S(1)}, bf16[4,48,384]{2,1,0:T(8,128)(2,1)S(1)}, u32[]{:S(2)}, u32[]{:S(2)}) collective-permute-start(bf16[4,48,384]{2,1,0:T(8,128)(2,1)S(1)} %copy-done.6), channel_id=1, source_target_pairs={{0,2},{1,3},{2,0},{3,1},{4,6},{5,7},{6,4},{7,5},{8,10},{9,11},{10,... | collective-permute-start | bytes 442376 | tf_op jit(solution)/shard_map/ppermute | solution.py:496
  52.0 25.8 %collective-permute-start.5 = (bf16[4,48,384]{2,1,0:T(8,128)(2,1)S(1)}, bf16[4,48,384]{2,1,0:T(8,128)(2,1)S(1)}, u32[]{:S(2)}, u32[]{:S(2)}) collective-permute-start(bf16[4,48,384]{2,1,0:T(8,128)(2,1)S(1)} %collective-permute-done.1.refs_1_), channel_id=1, source_target_pairs={{0,2},{1,3},{2,0},{3,1},{4,6},{5,7},{6,4},{7,5},{8,10},{9,11},{10,... | collective-permute-start | bytes 442376 | tf_op jit(solution)/shard_map/ppermute | solution.py:496
  53.0 24.8 %collective-permute-start.6 = (bf16[4,48,384]{2,1,0:T(8,128)(2,1)S(1)}, bf16[4,48,384]{2,1,0:T(8,128)(2,1)S(1)}, u32[]{:S(2)}, u32[]{:S(2)}) collective-permute-start(bf16[4,48,384]{2,1,0:T(8,128)(2,1)S(1)} %collective-permute-done.2.refs_2_), channel_id=1, source_target_pairs={{0,2},{1,3},{2,0},{3,1},{4,6},{5,7},{6,4},{7,5},{8,10},{9,11},{10,... | collective-permute-start | bytes 442376 | tf_op jit(solution)/shard_map/ppermute | solution.py:496
  54.1 23.8 %collective-permute-start.7 = (bf16[4,48,384]{2,1,0:T(8,128)(2,1)S(1)}, bf16[4,48,384]{2,1,0:T(8,128)(2,1)S(1)}, u32[]{:S(2)}, u32[]{:S(2)}) collective-permute-start(bf16[4,48,384]{2,1,0:T(8,128)(2,1)S(1)} %collective-permute-done.3.refs_3_), channel_id=1, source_target_pairs={{0,2},{1,3},{2,0},{3,1},{4,6},{5,7},{6,4},{7,5},{8,10},{9,11},{10,... | collective-permute-start | bytes 442376 | tf_op jit(solution)/shard_map/ppermute | solution.py:496
  76.8 34.7 %copy-start.3 = (f32[4,4,48,384]{3,2,1,0:T(8,128)S(1)}, f32[4,4,48,384]{3,2,1,0:T(8,128)}, u32[]{:S(2)}) copy-start(f32[4,4,48,384]{3,2,1,0:T(8,128)} %get-tuple-element.56.own_ref) | copy-start | bytes 3538948
  76.8 34.7 %collective-permute-start.27 = (s16[1,4,4,48,384]{4,3,2,1,0:T(8,128)(2,1)S(1)}, s16[1,4,4,48,384]{4,3,2,1,0:T(8,128)(2,1)S(1)}, u32[]{:S(2)}, u32[]{:S(2)}) collective-permute-start(s16[1,4,4,48,384]{4,3,2,1,0:T(8,128)(2,1)S(1)} %get-tuple-element.57), channel_id=1, source_target_pairs={{0,2},{1,3},{2,0},{3,1},{4,6},{5,7},{6,4},{7,5},{8,10},{9,11},{10,... | collective-permute-start | bytes 1769480 | tf_op jit(solution)/shard_map/ppermute | solution.py:496
  99.6 19.1 %collective-permute-start.19 = (s16[1,4,4,48,384]{4,3,2,1,0:T(8,128)(2,1)S(1)}, s16[1,4,4,48,384]{4,3,2,1,0:T(8,128)(2,1)S(1)}, u32[]{:S(2)}, u32[]{:S(2)}) collective-permute-start(s16[1,4,4,48,384]{4,3,2,1,0:T(8,128)(2,1)S(1)} %get-tuple-element.50), channel_id=1, source_target_pairs={{0,2},{1,3},{2,0},{3,1},{4,6},{5,7},{6,4},{7,5},{8,10},{9,11},{10,... | collective-permute-start | bytes 1769480 | tf_op jit(solution)/shard_map/ppermute | solution.py:496
  100.5 11.0 %collective-permute-start.28 = (f32[1,4,4,1,384]{4,3,2,1,0:T(1,128)S(1)}, f32[1,4,4,1,384]{4,3,2,1,0:T(1,128)S(1)}, u32[]{:S(2)}, u32[]{:S(2)}) collective-permute-start(f32[1,4,4,1,384]{4,3,2,1,0:T(1,128)S(1)} %get-tuple-element.58), channel_id=1, source_target_pairs={{0,2},{1,3},{2,0},{3,1},{4,6},{5,7},{6,4},{7,5},{8,10},{9,11},{10,... | collective-permute-start | bytes 73736 | tf_op jit(solution)/shard_map/ppermute | solution.py:496
  101.6 15.1 %collective-permute-start.20 = (f32[1,4,4,1,384]{4,3,2,1,0:T(1,128)S(1)}, f32[1,4,4,1,384]{4,3,2,1,0:T(1,128)S(1)}, u32[]{:S(2)}, u32[]{:S(2)}) collective-permute-start(f32[1,4,4,1,384]{4,3,2,1,0:T(1,128)S(1)} %get-tuple-element.51), channel_id=1, source_target_pairs={{0,2},{1,3},{2,0},{3,1},{4,6},{5,7},{6,4},{7,5},{8,10},{9,11},{10,... | collective-permute-start | bytes 73736 | tf_op jit(solution)/shard_map/ppermute | solution.py:496
  112.3 19.5 %collective-permute-start.29 = (s16[4,48,384]{2,1,0:T(8,128)(2,1)S(1)}, s16[4,48,384]{2,1,0:T(8,128)(2,1)S(1)}, u32[]{:S(2)}, u32[]{:S(2)}) collective-permute-start(s16[4,48,384]{2,1,0:T(8,128)(2,1)S(1)} %get-tuple-element.69), channel_id=1, source_target_pairs={{0,4},{1,5},{2,6},{3,7},{4,8},{5,9},{6,10},{7,11},{8,12},{9,13},{1... | collective-permute-start | bytes 442376 | tf_op jit(solution)/shard_map/ppermute | solution.py:496
  114.0 19.0 %collective-permute-start.30 = (s16[4,48,384]{2,1,0:T(8,128)(2,1)S(1)}, s16[4,48,384]{2,1,0:T(8,128)(2,1)S(1)}, u32[]{:S(2)}, u32[]{:S(2)}) collective-permute-start(s16[4,48,384]{2,1,0:T(8,128)(2,1)S(1)} %get-tuple-element.68), channel_id=1, source_target_pairs={{0,8},{1,9},{2,10},{3,11},{4,12},{5,13},{6,14},{7,15},{8,0},{9,1},... | collective-permute-start | bytes 442376 | tf_op jit(solution)/shard_map/ppermute | solution.py:496
  116.6 18.2 %collective-permute-start.31 = (s16[4,48,384]{2,1,0:T(8,128)(2,1)S(1)}, s16[4,48,384]{2,1,0:T(8,128)(2,1)S(1)}, u32[]{:S(2)}, u32[]{:S(2)}) collective-permute-start(s16[4,48,384]{2,1,0:T(8,128)(2,1)S(1)} %get-tuple-element.67), channel_id=1, source_target_pairs={{0,12},{1,13},{2,14},{3,15},{4,0},{5,1},{6,2},{7,3},{8,4},{9,5},{1... | collective-permute-start | bytes 442376 | tf_op jit(solution)/shard_map/ppermute | solution.py:496
  116.7 6.3 %collective-permute-start.32 = (f32[4,1,384]{2,1,0:T(1,128)S(1)}, f32[4,1,384]{2,1,0:T(1,128)S(1)}, u32[]{:S(2)}, u32[]{:S(2)}) collective-permute-start(f32[4,1,384]{2,1,0:T(1,128)S(1)} %get-tuple-element.77), channel_id=1, source_target_pairs={{0,4},{1,5},{2,6},{3,7},{4,8},{5,9},{6,10},{7,11},{8,12},{9,13},{1... | collective-permute-start | bytes 18440 | tf_op jit(solution)/shard_map/ppermute | solution.py:496
  118.7 7.5 %collective-permute-start.33 = (f32[4,1,384]{2,1,0:T(1,128)S(1)}, f32[4,1,384]{2,1,0:T(1,128)S(1)}, u32[]{:S(2)}, u32[]{:S(2)}) collective-permute-start(f32[4,1,384]{2,1,0:T(1,128)S(1)} %get-tuple-element.76), channel_id=1, source_target_pairs={{0,8},{1,9},{2,10},{3,11},{4,12},{5,13},{6,14},{7,15},{8,0},{9,1},... | collective-permute-start | bytes 18440 | tf_op jit(solution)/shard_map/ppermute | solution.py:496
  119.7 24.2 %copy-start.16 = (f32[24,384]{1,0:T(8,128)S(1)}, f32[24,384]{1,0:T(8,128)}, u32[]{:S(2)}) copy-start(f32[24,384]{1,0:T(8,128)} %copy-done.15) | copy-start | bytes 110596
  123.0 3.6 %collective-permute-start.34 = (f32[4,1,384]{2,1,0:T(1,128)S(1)}, f32[4,1,384]{2,1,0:T(1,128)S(1)}, u32[]{:S(2)}, u32[]{:S(2)}) collective-permute-start(f32[4,1,384]{2,1,0:T(1,128)S(1)} %get-tuple-element.75), channel_id=1, source_target_pairs={{0,12},{1,13},{2,14},{3,15},{4,0},{5,1},{6,2},{7,3},{8,4},{9,5},{1... | collective-permute-start | bytes 18440 | tf_op jit(solution)/shard_map/ppermute | solution.py:496
  126.2 5.6 %collective-permute-start.24 = (f32[4,1,384]{2,1,0:T(1,128)S(1)}, f32[4,1,384]{2,1,0:T(1,128)S(1)}, u32[]{:S(2)}, u32[]{:S(2)}) collective-permute-start(f32[4,1,384]{2,1,0:T(1,128)S(1)} %get-tuple-element.80), channel_id=1, source_target_pairs={{0,4},{1,5},{2,6},{3,7},{4,8},{5,9},{6,10},{7,11},{8,12},{9,13},{1... | collective-permute-start | bytes 18440 | tf_op jit(solution)/shard_map/ppermute | solution.py:496
  126.2 17.7 %copy-start.12 = (f32[128]{0:T(128)S(1)}, f32[128]{0:T(128)}, u32[]{:S(2)}) copy-start(f32[128]{0:T(128)} %param.13) | copy-start | bytes 1540
  126.2 17.7 %copy-start.14 = (f32[24,384]{1,0:T(8,128)S(1)}, f32[24,384]{1,0:T(8,128)}, u32[]{:S(2)}) copy-start(f32[24,384]{1,0:T(8,128)} %copy-done.13) | copy-start | bytes 110596
  126.6 15.5 %collective-permute-start.21 = (s16[4,48,384]{2,1,0:T(8,128)(2,1)S(1)}, s16[4,48,384]{2,1,0:T(8,128)(2,1)S(1)}, u32[]{:S(2)}, u32[]{:S(2)}) collective-permute-start(s16[4,48,384]{2,1,0:T(8,128)(2,1)S(1)} %get-tuple-element.72), channel_id=1, source_target_pairs={{0,4},{1,5},{2,6},{3,7},{4,8},{5,9},{6,10},{7,11},{8,12},{9,13},{1... | collective-permute-start | bytes 442376 | tf_op jit(solution)/shard_map/ppermute | solution.py:496
  131.7 10.4 %collective-permute-start.22 = (s16[4,48,384]{2,1,0:T(8,128)(2,1)S(1)}, s16[4,48,384]{2,1,0:T(8,128)(2,1)S(1)}, u32[]{:S(2)}, u32[]{:S(2)}) collective-permute-start(s16[4,48,384]{2,1,0:T(8,128)(2,1)S(1)} %get-tuple-element.71), channel_id=1, source_target_pairs={{0,8},{1,9},{2,10},{3,11},{4,12},{5,13},{6,14},{7,15},{8,0},{9,1},... | collective-permute-start | bytes 442376 | tf_op jit(solution)/shard_map/ppermute | solution.py:496
  131.8 10.4 %collective-permute-start.23 = (s16[4,48,384]{2,1,0:T(8,128)(2,1)S(1)}, s16[4,48,384]{2,1,0:T(8,128)(2,1)S(1)}, u32[]{:S(2)}, u32[]{:S(2)}) collective-permute-start(s16[4,48,384]{2,1,0:T(8,128)(2,1)S(1)} %get-tuple-element.70), channel_id=1, source_target_pairs={{0,12},{1,13},{2,14},{3,15},{4,0},{5,1},{6,2},{7,3},{8,4},{9,5},{1... | collective-permute-start | bytes 442376 | tf_op jit(solution)/shard_map/ppermute | solution.py:496
  133.0 9.1 %collective-permute-start.25 = (f32[4,1,384]{2,1,0:T(1,128)S(1)}, f32[4,1,384]{2,1,0:T(1,128)S(1)}, u32[]{:S(2)}, u32[]{:S(2)}) collective-permute-start(f32[4,1,384]{2,1,0:T(1,128)S(1)} %get-tuple-element.79), channel_id=1, source_target_pairs={{0,8},{1,9},{2,10},{3,11},{4,12},{5,13},{6,14},{7,15},{8,0},{9,1},... | collective-permute-start | bytes 18440 | tf_op jit(solution)/shard_map/ppermute | solution.py:496
  134.8 7.3 %collective-permute-start.26 = (f32[4,1,384]{2,1,0:T(1,128)S(1)}, f32[4,1,384]{2,1,0:T(1,128)S(1)}, u32[]{:S(2)}, u32[]{:S(2)}) collective-permute-start(f32[4,1,384]{2,1,0:T(1,128)S(1)} %get-tuple-element.78), channel_id=1, source_target_pairs={{0,12},{1,13},{2,14},{3,15},{4,0},{5,1},{6,2},{7,3},{8,4},{9,5},{1... | collective-permute-start | bytes 18440 | tf_op jit(solution)/shard_map/ppermute | solution.py:496
  142.1 1.4 collective-permute-start.36
  142.3 1.6 collective-permute-start.35
  142.9 7.1 %collective-permute-start.18 = (bf16[2,192,384]{2,1,0:T(8,128)(2,1)S(1)}, bf16[2,192,384]{2,1,0:T(8,128)(2,1)S(1)}, u32[]{:S(2)}, u32[]{:S(2)}) collective-permute-start(bf16[2,192,384]{2,1,0:T(8,128)(2,1)S(1)} %get-tuple-element.48), channel_id=1, source_target_pairs={{0,1},{1,0},{2,3},{3,2},{4,5},{5,4},{6,7},{7,6},{8,9},{9,8},{10,11... | collective-permute-start | bytes 884744 | tf_op jit(solution)/shard_map/ppermute | solution.py:489
  143.0 7.0 %collective-permute-start.17 = (bf16[2,192,384]{2,1,0:T(8,128)(2,1)S(1)}, bf16[2,192,384]{2,1,0:T(8,128)(2,1)S(1)}, u32[]{:S(2)}, u32[]{:S(2)}) collective-permute-start(bf16[2,192,384]{2,1,0:T(8,128)(2,1)S(1)} %get-tuple-element.47), channel_id=1, source_target_pairs={{0,1},{1,0},{2,3},{3,2},{4,5},{5,4},{6,7},{7,6},{8,9},{9,8},{10,11... | collective-permute-start | bytes 884744 | tf_op jit(solution)/shard_map/ppermute | solution.py:489
  144.6 1.2 collective-permute-start.37
  145.8 3.7 %collective-permute-start.38 = (f32[16,128]{1,0:T(8,128)S(1)}, f32[16,128]{1,0:T(8,128)S(1)}, u32[]{:S(2)}, u32[]{:S(2)}) collective-permute-start(f32[16,128]{1,0:T(8,128)S(1)} %add.295), channel_id=1, source_target_pairs={{0,2},{1,3},{2,0},{3,1},{4,6},{5,7},{6,4},{7,5},{8,10},{9,11},{10,... | collective-permute-start | bytes 24584 | tf_op jit(solution)/shard_map/ppermute | solution.py:547
  149.5 3.7 %collective-permute-start.39 = (f32[16,128]{1,0:T(8,128)S(1)}, f32[16,128]{1,0:T(8,128)S(1)}, u32[]{:S(2)}, u32[]{:S(2)}) collective-permute-start(f32[16,128]{1,0:T(8,128)S(1)} %add.296), channel_id=1, source_target_pairs={{0,4},{1,5},{2,6},{3,7},{4,0},{5,1},{6,2},{7,3},{8,12},{9,13},{10,... | collective-permute-start | bytes 24584 | tf_op jit(solution)/shard_map/ppermute | solution.py:547
  153.2 8.7 %collective-permute-start.40 = (f32[16,128]{1,0:T(8,128)S(1)}, f32[16,128]{1,0:T(8,128)S(1)}, u32[]{:S(2)}, u32[]{:S(2)}) collective-permute-start(f32[16,128]{1,0:T(8,128)S(1)} %add.297), channel_id=1, source_target_pairs={{0,8},{1,9},{2,10},{3,11},{4,12},{5,13},{6,14},{7,15},{8,0},{9,1},... | collective-permute-start | bytes 24584 | tf_op jit(solution)/shard_map/ppermute | solution.py:547
  (10 other events, 42.7 us)
where the time goes:
time: 163 us; the launch traced here: 162 us
  Pallas kernels  72 us (44%)
  starting transfers between devices  43.2 us (27%)
  waiting for transfers between devices  38.2 us (23%)
  local copies, waits for them, and re-layouts  6.94 us (4%)
    pallas_call x2, Pallas kernels, attention_call(): pl.pallas_call(functools.partial(attention_kernel, za, yb, head_width), g...  43.4 us
    ppermute x30, starting transfers between devices, shift(): return lax.ppermute(x, 'smp', perm)  39.1 us
    ppermute x30, waiting for transfers between devices, shift(): return lax.ppermute(x, 'smp', perm)  31.6 us
    pallas_call x2, Pallas kernels, project_call(): pl.pallas_call(project_kernel, grid_spec=pltpu.PrefetchScalarGridSpec(num...  8.97 us
    pallas_call x2, Pallas kernels, final_call(): pl.pallas_call(functools.partial(kernel, parts), in_specs=[pl.BlockSpec(m...  8.21 us
    pallas_call x1, Pallas kernels, bias_call(): pl.pallas_call(bias_kernel, out_shape=[jax.ShapeDtypeStruct((half, rows,...  7.1 us
    unnamed x35, local copies, waits for them, and re-layouts  5.27 us
    ppermute x4, waiting for transfers between devices, per_device_tiled(): lax.ppermute(projection, 'smp', [(d, d ^ step) for d in range(devices)])  5.12 us
  transfers between devices with their start and end apart: 41, of which 14 were waited for; matrix products, arithmetic and copies ran while one was open for 1% of the time, Pallas kernels for 44%

commit v1 on v0

v1 whole, which is shorter than its diff:
```python
import functools
import math

import jax
import jax.numpy as jnp
from jax import lax
from jax.experimental import pallas as pl
from jax.experimental.pallas import tpu as pltpu
from jax.sharding import Mesh
from jax.sharding import PartitionSpec as P

F32 = jnp.float32
BF16 = jnp.bfloat16
LOG2E = math.log2(math.e)
NT = (((1,), (1,)), ((), ()))
TN = (((0,), (0,)), ((), ()))
VMEM_LIMIT = 48 * 1024 * 1024
CHUNKS = ((4, True), (4, True))


def normalize(pair_rep, pair_gain):
    values_f = pair_rep.astype(F32)
    centre = jnp.mean(values_f, axis=-1, keepdims=True)
    spread = jnp.mean((values_f - centre) ** 2, axis=-1, keepdims=True)
    rstd = lax.rsqrt(spread + 1e-05)
    centred = (values_f - centre) * rstd
    return (centred * pair_gain, centred, rstd)


def per_device_plain(
    activations, cotangent, pair_rep, pair_gain, w_pair, w_query, w_key, w_value, w_out, token_mask
):
    head_count = w_pair.shape[1]
    model_width = w_query.shape[0]
    head_width = model_width // head_count
    tok_count = token_mask.shape[0]
    normed, centred, rstd = normalize(pair_rep, pair_gain)
    bias_rows = jnp.einsum(
        "rjc,ch->rhj", normed, w_pair.astype(F32), precision=lax.Precision.HIGHEST
    ).astype(BF16)
    bias_full = lax.all_gather(bias_rows, "smp", axis=0, tiled=True).astype(F32)
    live_keys = token_mask > 0
    outputs = []
    grad_total = None
    for sample_index in range(activations.shape[0]):
        sample_act = activations[sample_index]

        def project(weight):
            return (
                jnp.dot(sample_act, weight, preferred_element_type=F32)
                .astype(BF16)
                .reshape(tok_count, head_count, head_width)
            )

        queries, keys_proj, values_proj = project(w_query), project(w_key), project(w_value)
        scores = (
            jnp.einsum("ihd,jhd->ihj", queries, keys_proj, preferred_element_type=F32)
            * head_width ** (-0.5)
            + bias_full
        )
        scores = jnp.where(live_keys[None, None, :], scores, -1e30)
        exps = jnp.exp(scores - jnp.max(scores, axis=-1, keepdims=True))
        probs = exps / jnp.sum(exps, axis=-1, keepdims=True)
        mixed = (
            jnp.einsum("ihj,jhd->ihd", probs.astype(BF16), values_proj, preferred_element_type=F32)
            .astype(BF16)
            .reshape(tok_count, model_width)
        )
        output = jnp.dot(mixed, w_out, preferred_element_type=F32)
        outputs.append(jnp.where(live_keys[:, None], output, 0.0).astype(BF16))
        sample_cot = cotangent[sample_index]
        masked_cot = jnp.where(live_keys[:, None], sample_cot, jnp.zeros_like(sample_cot))
        d_mixed = (
            jnp.dot(masked_cot, w_out.T, preferred_element_type=F32)
            .astype(BF16)
            .reshape(tok_count, head_count, head_width)
        )
        d_probs = jnp.einsum("ihd,jhd->ihj", d_mixed, values_proj, preferred_element_type=F32)
        d_scores = probs * (d_probs - jnp.sum(probs * d_probs, axis=-1, keepdims=True))
        grad_total = d_scores if grad_total is None else grad_total + d_scores
    bias_grad = lax.psum_scatter(grad_total, "smp", scatter_dimension=0, tiled=True)
    proj_local = jnp.einsum("rjc,rhj->ch", normed, bias_grad, precision=lax.Precision.HIGHEST)
    grad_projection = lax.psum(proj_local, "smp")
    d_normed = (
        jnp.einsum("rhj,ch->rjc", bias_grad, w_pair.astype(F32), precision=lax.Precision.HIGHEST)
        * pair_gain
    )
    first_mean = jnp.mean(d_normed, axis=-1, keepdims=True)
    second_mean = jnp.mean(d_normed * centred, axis=-1, keepdims=True)
    grad_pair = (rstd * (d_normed - first_mean - centred * second_mean)).astype(BF16)
    return (jnp.stack(outputs), grad_pair, grad_projection)


def dot(left, right, dims=None):
    if dims is None:
        return jnp.dot(left, right, preferred_element_type=F32)
    return lax.dot_general(left, right, dims, preferred_element_type=F32)


def pieces3(value):
    high = value.astype(BF16)
    rest = value - high.astype(F32)
    mid = rest.astype(BF16)
    low = (rest - mid.astype(F32)).astype(BF16)
    return high, mid, low


def bias_kernel(core_ref, pair_ref, gain_ref, wt_ref, mask_ref, own_ref, other_ref, mean_ref, rstd_ref, held):
    rows, tok, chan = pair_ref.shape
    heads = wt_ref.shape[0]
    half = heads // 2
    scaled = wt_ref[...] * gain_ref[...]
    total = jnp.sum(scaled, axis=1, keepdims=True)
    left = jnp.concatenate([*pieces3(scaled), jnp.ones((16, chan), BF16)], axis=0)
    lane = lax.broadcasted_iota(jnp.int32, (tok, 128), 1)
    spreads = jnp.zeros((tok, 128), F32)
    for i in range(rows):
        values = pair_ref[i].astype(F32)
        diff = values - jnp.sum(values, axis=1, keepdims=True) * (1.0 / chan)
        spread = jnp.sum(diff * diff, axis=1, keepdims=True) * (1.0 / chan)
        spreads = jnp.where(lane == i, spread, spreads)
    rstd = lax.rsqrt(spreads.T[:rows] + 1e-05)
    rstd_ref[...] = rstd
    for i in range(rows):
        sums = dot(left, pair_ref[i], NT)
        mean_row = sums[3 * heads : 3 * heads + 1] * (1.0 / chan)
        raw = sums[0:heads] + (sums[heads : 2 * heads] + sums[2 * heads : 3 * heads])
        held[:, i, :] = (raw - total * mean_row) * rstd[i : i + 1]
        mean_ref[i : i + 1, :] = mean_row
    core = core_ref[0]
    live = (mask_ref[...] > 0)[None]
    own_ref[...] = jnp.where(live, held[pl.ds(core * half, half)], -1e30).astype(BF16)
    other_ref[...] = jnp.where(live, held[pl.ds((1 - core) * half, half)], -1e30).astype(BF16)


def bias_call(core, pair_rep, gain, w_t, mask_row):
    rows, tok, chan = pair_rep.shape
    heads = w_t.shape[0]
    half = heads // 2
    vm = pl.BlockSpec(memory_space=pltpu.VMEM)
    return pl.pallas_call(
        bias_kernel,
        out_shape=[
            jax.ShapeDtypeStruct((half, rows, tok), BF16),
            jax.ShapeDtypeStruct((half, rows, tok), BF16),
            jax.ShapeDtypeStruct((rows, tok), F32),
            jax.ShapeDtypeStruct((rows, tok), F32),
            jax.ShapeDtypeStruct((heads, rows, tok), F32),
        ],
        in_specs=[pl.BlockSpec(memory_space=pltpu.SMEM)] + [vm] * 4,
        out_specs=[vm] * 5,
        compiler_params=pltpu.CompilerParams(vmem_limit_bytes=VMEM_LIMIT),
        cost_estimate=pl.CostEstimate(flops=int(3e9), bytes_accessed=int(4e6), transcendentals=0),
        name="pair_bias",
    )(core, pair_rep, gain, w_t, mask_row)


def project_kernel(core_ref, act_ref, cot_ref, wq_ref, wk_ref, wv_ref, wo_ref, mask_ref, q_ref, k_ref, v_ref, d_ref):
    act = act_ref[0]
    for weight, out in ((wq_ref, q_ref), (wk_ref, k_ref), (wv_ref, v_ref)):
        out[0] = dot(act, weight[...]).T.astype(BF16)
    live = mask_ref[...] > 0
    d_ref[0] = jnp.where(live, dot(wo_ref[...], cot_ref[0], NT), 0.0).astype(BF16)


def project_call(core, act, cot, w_query, w_key, w_value, w_out, mask_row):
    samples, tok, width = act.shape
    half = width // 2
    columns = pl.BlockSpec((width, half), lambda s, c: (0, c[0]))
    per_sample = pl.BlockSpec((1, tok, width), lambda s, c: (s, 0, 0))
    out = pl.BlockSpec((1, half, tok), lambda s, c: (s, 0, 0))
    return pl.pallas_call(
        project_kernel,
        grid_spec=pltpu.PrefetchScalarGridSpec(
            num_scalar_prefetch=1,
            grid=(samples,),
            in_specs=[per_sample, per_sample, columns, columns, columns,
                      pl.BlockSpec((half, width), lambda s, c: (c[0], 0)),
                      pl.BlockSpec((1, tok), lambda s, c: (0, 0))],
            out_specs=[out] * 4,
        ),
        out_shape=[jax.ShapeDtypeStruct((samples, half, tok), BF16)] * 4,
        compiler_params=pltpu.CompilerParams(vmem_limit_bytes=VMEM_LIMIT),
        cost_estimate=pl.CostEstimate(
            flops=8 * samples * tok * width * half, bytes_accessed=int(6e6), transcendentals=0
        ),
        name="projections",
    )(core, act, cot, w_query, w_key, w_value, w_out, mask_row)


def code16(block):
    top = jnp.max(jnp.abs(block), axis=0, keepdims=True)
    level = jnp.ceil(jnp.log2(jnp.maximum(top, 1.2e-38)) * 64.0) + 1.0
    unit = block * jnp.exp2(level * (-1.0 / 64.0))
    return jnp.round(unit * 32766.0).astype(jnp.int32).astype(jnp.int16), level


def decode16(codes, levels):
    scale = jnp.exp2(levels * (1.0 / 64.0)) * (1.0 / 32766.0)
    return codes.astype(jnp.int32).astype(F32) * scale


def pack_levels(levels):
    block = jnp.concatenate(levels, axis=0)
    if block.shape[0] < 8:
        block = jnp.concatenate([block, jnp.zeros((8 - block.shape[0], block.shape[1]), F32)], axis=0)
    return jnp.concatenate([block, block], axis=0).astype(jnp.int32).astype(jnp.int16)


def attention_kernel(arrays, head_width, offs_ref, *refs):
    bias_refs = refs[:arrays]
    q0, k0, v0, d0, q1, k1, v1, d1 = refs[arrays : arrays + 8]
    mixed0, mixed1, own_ref, code_ref, bias_f, grad, held = refs[arrays + 8 :]
    stay, _, rows, _ = own_ref.shape
    part = rows // 2
    head, chunk = pl.program_id(0), pl.num_programs(0)
    at = 0
    for ref in bias_refs:
        for b in range(ref.shape[0]):
            block = ref[b, 0].astype(F32) * LOG2E
            for side in range(2):
                start = pl.multiple_of(offs_ref[at], 8)
                bias_f[pl.ds(start, part), :] = block[side * part : (side + 1) * part]
                at += 1
    factor = head_width ** (-0.5) * LOG2E
    count = q0.shape[0]

    def products(s):
        qr, kr, vr, dr = (q0, k0, v0, d0) if s < count else (q1, k1, v1, d1)
        at = s % count
        return dot(qr[at].T, kr[at]), dot(dr[at].T, vr[at]), vr[at].T

    total = None
    ahead = products(0)
    for s in range(2 * count):
        scores, d_probs, value = ahead
        if s + 1 < 2 * count:
            ahead = products(s + 1)
        scores = scores * factor + bias_f[...]
        exps = jnp.exp2(scores - jnp.max(scores, axis=1, keepdims=True))
        probs = exps * (1.0 / jnp.sum(exps, axis=1, keepdims=True))
        mixed = mixed0 if s < count else mixed1
        mixed[s % count] = dot(probs.astype(BF16), value).T.astype(BF16)
        delta = jnp.sum(probs * d_probs, axis=1, keepdims=True)
        d_scores = probs * (d_probs - delta)
        total = d_scores if total is None else total + d_scores
    grad[...] = total

    @pl.when(head == 0)
    def _():
        held[...] = jnp.zeros_like(held)

    for b in range(2 * stay):
        starts = [pl.multiple_of(offs_ref[4 * stay + 2 * b + side], 8) for side in range(2)]
        block = jnp.concatenate([grad[pl.ds(start, part), :] for start in starts], axis=0)
        if b < stay:
            own_ref[b, 0] = block
        else:
            codes, level = code16(block)
            code_ref[b - stay, pl.ds(pl.multiple_of(head * rows, 16), rows), :] = codes
            held[b - stay, pl.ds(head, 1), :] = level

    @pl.when(head == chunk - 1)
    def _():
        last = code_ref.shape[1] - 16
        for b in range(stay):
            code_ref[b, last:, :] = pack_levels([held[b]])


def attention_call(head_width, offsets, bias_arrays, first, own_proj, sib_proj):
    blocks = sum(array.shape[0] for array in bias_arrays)
    _, chunk, rows, tok = bias_arrays[0].shape
    count = own_proj[0].shape[0]
    stay = blocks // 2
    head = pl.BlockSpec((count, head_width, tok), lambda h, o: (0, first + h, 0))
    mixed = pl.BlockSpec((count, head_width, tok), lambda h, o: (0, h, 0))
    coded = (stay, chunk * rows + 16, tok)
    tiles = 2 * count * chunk
    return pl.pallas_call(
        functools.partial(attention_kernel, len(bias_arrays), head_width),
        grid_spec=pltpu.PrefetchScalarGridSpec(
            num_scalar_prefetch=1,
            grid=(chunk,),
            in_specs=[
                pl.BlockSpec((array.shape[0], 1, rows, tok), lambda h, o: (0, h, 0, 0)) for array in bias_arrays
            ]
            + [head] * 8,
            out_specs=[
                mixed,
                mixed,
                pl.BlockSpec((stay, 1, rows, tok), lambda h, o: (0, h, 0, 0)),
                pl.BlockSpec(coded, lambda h, o: (0, 0, 0)),
            ],
            scratch_shapes=[
                pltpu.VMEM((tok, tok), F32),
                pltpu.VMEM((tok, tok), F32),
                pltpu.VMEM((stay, 8, tok), F32),
            ],
        ),
        out_shape=[
            jax.ShapeDtypeStruct((count, chunk * head_width, tok), BF16),
            jax.ShapeDtypeStruct((count, chunk * head_width, tok), BF16),
            jax.ShapeDtypeStruct((stay, chunk, rows, tok), F32),
            jax.ShapeDtypeStruct(coded, jnp.int16),
        ],
        compiler_params=pltpu.CompilerParams(vmem_limit_bytes=VMEM_LIMIT),
        cost_estimate=pl.CostEstimate(
            flops=tiles * 6 * tok * tok * 256, bytes_accessed=int(4e6), transcendentals=tiles * tok * tok
        ),
        name="attention",
    )(offsets, *bias_arrays, *own_proj, *sib_proj)


def plain_call(kernel, name, out_shape, *operands):
    vm = pl.BlockSpec(memory_space=pltpu.VMEM)
    return pl.pallas_call(
        kernel,
        in_specs=[vm] * len(operands),
        out_specs=[vm] * len(out_shape),
        out_shape=out_shape,
        compiler_params=pltpu.CompilerParams(vmem_limit_bytes=VMEM_LIMIT),
        cost_estimate=pl.CostEstimate(flops=int(4e6), bytes_accessed=int(3e6), transcendentals=0),
        name=name,
    )(*operands)


def join_kernel(own_ref, code_ref, stay_ref, next_ref):
    blocks, chunk, rows, _ = own_ref.shape
    last = chunk * rows
    stay = blocks // 2
    for b in range(blocks):
        levels = code_ref[b, last:, :].astype(jnp.int32).astype(F32)
        held = []
        for h in range(chunk):
            span = slice(h * rows, (h + 1) * rows)
            block = own_ref[b, h] + decode16(code_ref[b, span, :], levels[h : h + 1])
            if b < stay:
                stay_ref[b, h] = block
            else:
                codes, level = code16(block)
                next_ref[b - stay, span, :] = codes
                held.append(level)
        if held:
            next_ref[b - stay, last:, :] = pack_levels(held)


def join_call(own, codes):
    blocks, chunk, rows, tok = own.shape
    return plain_call(
        join_kernel,
        "join",
        [
            jax.ShapeDtypeStruct((blocks // 2, chunk, rows, tok), F32),
            jax.ShapeDtypeStruct((blocks // 2, chunk * rows + 16, tok), jnp.int16),
        ],
        own, codes,
    )


def total_kernel(own_ref, code_ref, here_ref, there_ref):
    _, chunk, rows, _ = own_ref.shape
    part = rows // 2
    levels = code_ref[0, chunk * rows :, :].astype(jnp.int32).astype(F32)
    for h in range(chunk):
        block = own_ref[0, h] + decode16(code_ref[0, h * rows : (h + 1) * rows, :], levels[h : h + 1])
        here_ref[h] = block[:part]
        there_ref[h] = block[part:]


def total_call(own, codes):
    _, chunk, rows, tok = own.shape
    return plain_call(
        total_kernel, "last_join", [jax.ShapeDtypeStruct((chunk, rows // 2, tok), F32)] * 2, own, codes
    )


def output_kernel(parts, core_ref, *refs):
    own_refs, other_refs = refs[:parts], refs[parts : 2 * parts]
    w_own, w_other, mask_ref, out_ref = refs[2 * parts :]
    live = mask_ref[...] > 0
    total = None
    for group, weight in ((own_refs, w_own), (other_refs, w_other)):
        start = 0
        for ref in group:
            size = ref.shape[1]
            mixed = ref[0]
            mixed = jnp.where(live, mixed.astype(F32), 0.0).T.astype(BF16)
            term = dot(mixed, weight[start : start + size, :])
            total = term if total is None else total + term
            start += size
    out_ref[0] = total.astype(BF16)


def output_call(core, own, other, w_out, mask_row):
    samples, size, tok = own[0].shape
    parts = len(own)
    width = w_out.shape[0]
    half = width // 2
    block = pl.BlockSpec((1, size, tok), lambda s, c: (s, 0, 0))
    return pl.pallas_call(
        functools.partial(output_kernel, parts),
        grid_spec=pltpu.PrefetchScalarGridSpec(
            num_scalar_prefetch=1,
            grid=(samples,),
            in_specs=[block] * (2 * parts)
            + [
                pl.BlockSpec((half, width), lambda s, c: (c[0], 0)),
                pl.BlockSpec((half, width), lambda s, c: (1 - c[0], 0)),
                pl.BlockSpec((1, tok), lambda s, c: (0, 0)),
            ],
            out_specs=pl.BlockSpec((1, tok, width), lambda s, c: (s, 0, 0)),
        ),
        out_shape=jax.ShapeDtypeStruct((samples, tok, width), BF16),
        compiler_params=pltpu.CompilerParams(vmem_limit_bytes=VMEM_LIMIT),
        cost_estimate=pl.CostEstimate(
            flops=2 * samples * tok * width * width, bytes_accessed=int(4e6), transcendentals=0
        ),
        name="output",
    )(core, *own, *other, w_out, w_out, mask_row)


def load_rows(refs, i):
    return jnp.concatenate([ref[:, i, :] for ref in refs], axis=0)


def projection_kernel(parts, core_ref, *refs):
    own_refs, other_refs = refs[:parts], refs[parts : 2 * parts]
    pair_ref, gain_ref, mean_ref, rstd_ref, out_ref = refs[2 * parts :]
    rows, tok, chan = pair_ref.shape
    heads = out_ref.shape[0]
    half = heads // 2
    total = jnp.zeros((3 * heads, chan), F32)
    means = jnp.zeros((heads, tok), F32)
    for i in range(rows):
        grads = load_rows([*own_refs, *other_refs], i) * rstd_ref[i : i + 1, :]
        means = means + grads * mean_ref[i : i + 1, :]
        total = total + dot(jnp.concatenate(pieces3(grads), axis=0), pair_ref[i])
    raw = total[:heads] + (total[heads : 2 * heads] + total[2 * heads :])
    result = (raw - jnp.sum(means, axis=1, keepdims=True)) * gain_ref[...]
    core = core_ref[0]
    out_ref[pl.ds(pl.multiple_of(core * half, half), half), :] = result[:half]
    out_ref[pl.ds(pl.multiple_of((1 - core) * half, half), half), :] = result[half:]


def pair_grad_kernel(parts, core_ref, *refs):
    own_refs, other_refs = refs[:parts], refs[parts : 2 * parts]
    pair_ref, gain_ref, wt_ref, mean_ref, rstd_ref, bias_ref, out_ref = refs[2 * parts :]
    rows, tok, chan = pair_ref.shape
    half = wt_ref.shape[0] // 2
    core = core_ref[0]

    def own_first(take):
        return jnp.concatenate([take(core * half), take((1 - core) * half)], axis=0)

    scaled = own_first(lambda at: wt_ref[pl.ds(pl.multiple_of(at, half), half), :]) * gain_ref[...]
    scaled = scaled - jnp.mean(scaled, axis=1, keepdims=True)
    wh, wm, wl = pieces3(scaled)
    project = jnp.concatenate([wh, wm, wh, wl, wm, wh], axis=0)
    count = project.shape[0]
    zero, one = jnp.zeros((8, chan), BF16), jnp.ones((8, chan), BF16)
    right = jnp.concatenate(
        [
            jnp.concatenate([project, jnp.zeros_like(project)], axis=1),
            jnp.concatenate([one, zero], axis=1),
            jnp.concatenate([zero, one], axis=1),
        ],
        axis=0,
    )
    fill = jnp.zeros((5, tok), F32)
    for i in range(rows):
        rstd = rstd_ref[i : i + 1, :]
        grads = load_rows([*own_refs, *other_refs], i) * rstd
        bias = own_first(lambda at: bias_ref[pl.ds(at, half), i, :])
        along = jnp.sum(grads * bias, axis=0, keepdims=True) * rstd * (1.0 / chan)
        gh, gm, gl = pieces3(grads)
        back = [piece.astype(F32) for piece in pieces3(along * mean_ref[i : i + 1, :])]
        slope = [piece.astype(F32) for piece in pieces3(along)]
        extra = jnp.concatenate([*back, fill, *slope, fill], axis=0).astype(BF16)
        left = jnp.concatenate([gh, gh, gm, gh, gm, gl, extra], axis=0)
        both = dot(left, right, TN)
        out_ref[i] = (both[:, :chan] - pair_ref[i].astype(F32) * both[:, chan:]).astype(BF16)


def final_call(kernel, name, core, own, other, operands, out_shape):
    vm = pl.BlockSpec(memory_space=pltpu.VMEM)
    parts = len(own)
    return pl.pallas_call(
        functools.partial(kernel, parts),
        in_specs=[pl.BlockSpec(memory_space=pltpu.SMEM)] + [vm] * (2 * parts + len(operands)),
        out_specs=vm,
        out_shape=out_shape,
        compiler_params=pltpu.CompilerParams(vmem_limit_bytes=VMEM_LIMIT),
        cost_estimate=pl.CostEstimate(flops=int(4e9), bytes_accessed=int(8e6), transcendentals=0),
        name=name,
    )(core, *own, *other, *operands)


def per_device_tiled(
    chips, activations, cotangent, pair_rep, pair_gain, w_pair, w_query, w_key, w_value, w_out, token_mask
):
    rows, tok, chan = pair_rep.shape
    heads = w_pair.shape[1]
    half = heads // 2
    head_width = w_query.shape[0] // heads
    core = lax.axis_index("core")
    chip = lax.axis_index("chip")
    bits = [1 << b for b in reversed(range(chips.bit_length() - 1))]

    def swap_core(x):
        return lax.ppermute(x, "core", [(0, 1), (1, 0)])

    def swap(x, bit):
        return lax.ppermute(x, "chip", [(c, c ^ bit) for c in range(chips)])

    masks = [0]
    for bit in bits:
        masks = masks + [m ^ bit for m in masks]
    places = [jnp.stack([chip ^ m for m in masks]), jnp.stack([chip * 0 + c for c in range(chips)])]
    sides = jnp.stack([core, 1 - core])

    def offsets_of(places_in):
        both = jnp.concatenate([places_in, places[0]])
        return (both[:, None] * (2 * rows) + sides[None, :] * rows).reshape(-1).astype(jnp.int32)

    doubled, gathered = [offsets_of(p) for p in places]
    core_1 = core.reshape(1).astype(jnp.int32)
    gain = pair_gain.reshape(1, chan)
    w_t = w_pair.T.astype(F32)
    mask_row = token_mask.reshape(1, tok)

    sib_act, sib_cot = swap_core(activations), swap_core(cotangent)
    bias_own, bias_other, mean_rows, rstd_rows, bias_rows = bias_call(core_1, pair_rep, gain, w_t, mask_row)
    bias_chip = jnp.concatenate([bias_own, swap_core(bias_other)], axis=1)[None]

    weights = (w_query, w_key, w_value, w_out)
    own_proj = project_call(core_1, activations, cotangent, *weights, mask_row)
    sib_proj = project_call(core_1, sib_act, sib_cot, *weights, mask_row)

    mixed_own, mixed_other, grads_own, grads_other = [], [], [], []
    first = 0
    for size, by_permute in CHUNKS:
        mine = bias_chip[:, first : first + size]
        if by_permute:
            for bit in bits[:-1]:
                mine = jnp.concatenate([mine, swap(mine, bit)], axis=0)
            arrays, offsets = [mine, swap(mine, bits[-1])], doubled
        else:
            arrays, offsets = [lax.all_gather(mine, "chip", axis=0, tiled=True)], gathered
        mixed0, mixed1, stay, codes = attention_call(head_width, offsets, arrays, first, own_proj, sib_proj)
        mixed_own.append(mixed0)
        mixed_other.append(swap_core(mixed1))
        for bit in reversed(bits[1:]):
            stay, codes = join_call(stay, swap(codes, bit))
        here, there = total_call(stay, swap(codes, bits[0]))
        grads_own.append(here)
        grads_other.append(swap_core(there))
        first += size

    attended = output_call(core_1, mixed_own, mixed_other, w_out, mask_row)
    projection = final_call(
        projection_kernel, "pair_projection", core_1, grads_own, grads_other,
        (pair_rep, gain, mean_rows, rstd_rows), jax.ShapeDtypeStruct((heads, chan), F32),
    )
    projection = projection + swap_core(projection)
    for bit in reversed(bits):
        projection = projection + swap(projection, bit)
    grad_pair = final_call(
        pair_grad_kernel, "pair_gradient", core_1, grads_own, grads_other,
        (pair_rep, gain, w_t, mean_rows, rstd_rows, bias_rows), jax.ShapeDtypeStruct(pair_rep.shape, BF16),
    )
    return (attended, grad_pair, projection.T)


def solution(mesh):
    split = P(("grp", "smp"), None, None)
    devices = mesh.shape["smp"]

    def run(activations, cotangent, pair_rep, pair_gain, w_pair, *rest):
        parts = mesh.shape["grp"]
        rows, heads, tok = pair_rep.shape[0] // (parts * devices), w_pair.shape[1], pair_rep.shape[1]
        power = devices >= 8 and devices & (devices - 1) == 0
        if power and rows % 8 == 0 and rows <= 128 and heads == 2 * sum(size for size, _ in CHUNKS) and tok % 128 == 0:
            inner = Mesh(mesh.devices.reshape(parts, devices // 2, 2), ("grp", "chip", "core"))
            whole = P(("grp", "chip", "core"), None, None)
            body = functools.partial(per_device_tiled, devices // 2)
        else:
            inner, whole, body = mesh, split, per_device_plain
        return jax.shard_map(
            body,
            mesh=inner,
            in_specs=(whole, whole, whole, P(), P(), P(), P(), P(), P(), P("grp")),
            out_specs=(whole, whole, P("grp", None)),
            check_vma=False,
        )(activations, cotangent, pair_rep, pair_gain, w_pair, *rest)

    return run
```

time: 163 us -> 134 us (0.82)
  Pallas kernels: 72 us -> 41.5 us
  starting transfers between devices: 43.2 us -> 25.5 us
  waiting for transfers between devices: 38.2 us -> 49.9 us
  other arithmetic: 1.3 us -> 7.23 us
  local copies, waits for them, and re-layouts: 6.94 us -> 8.76 us
    pallas_call x6 -> x8, Pallas kernels: 45.1 us -> 22.4 us  [the longest x2 21.3 us: attention_call(): pl.pallas_call(functools.partial(attention_kernel, len(bias_arrays), head...]
    ppermute x41 -> x23, starting transfers between devices: 43.2 us -> 25.5 us  [the longest x15 23.6 us: swap(): return lax.ppermute(x, 'chip', [(c, c ^ bit) for c in range(chips)])]
    ppermute x41 -> x23, waiting for transfers between devices: 38.2 us -> 49.9 us  [the longest x15 47.1 us: swap(): return lax.ppermute(x, 'chip', [(c, c ^ bit) for c in range(chips)])]
    concatenate x0 -> x4, other arithmetic: none -> 4.64 us  [per_device_tiled(): mine = jnp.concatenate([mine, swap(mine, bit)], axis=0)]
    pallas_call x2, Pallas kernels: 8.21 us -> 3.75 us  [final_call(): pl.pallas_call(functools.partial(kernel, parts), in_specs=[pl.BlockSpec(m...]
    pallas_call x1, Pallas kernels: 7.1 us -> 3.6 us  [bias_call(): pl.pallas_call(bias_kernel, out_shape=[jax.ShapeDtypeStruct((half, rows,...]
    unnamed x35 -> x60, local copies, waits for them, and re-layouts: 5.27 us -> 7.17 us
  transfers between devices with their start and end apart: 41 -> 23, of which waited for: 14 -> 13; matrix products, arithmetic and copies ran while one was open for 1% -> 5% of each run, Pallas kernels for 44% -> 28%
where the time goes in v1:
time: 134 us
  waiting for transfers between devices  49.9 us (37%)
  Pallas kernels  41.5 us (31%)
  starting transfers between devices  25.5 us (19%)
  local copies, waits for them, and re-layouts  8.76 us (7%)
  other arithmetic  7.23 us (5%)
    ppermute x15, waiting for transfers between devices, swap(): return lax.ppermute(x, 'chip', [(c, c ^ bit) for c in range(chips)])  47.1 us
    ppermute x15, starting transfers between devices, swap(): return lax.ppermute(x, 'chip', [(c, c ^ bit) for c in range(chips)])  23.6 us
    pallas_call x2, Pallas kernels, attention_call(): pl.pallas_call(functools.partial(attention_kernel, len(bias_arrays), head...  21.3 us
    pallas_call x2, Pallas kernels, project_call(): pl.pallas_call(project_kernel, grid_spec=pltpu.PrefetchScalarGridSpec(num...  9.13 us
    unnamed x60, local copies, waits for them, and re-layouts  7.17 us
    concatenate x4, other arithmetic, per_device_tiled(): mine = jnp.concatenate([mine, swap(mine, bit)], axis=0)  4.64 us
    pallas_call x2, Pallas kernels, final_call(): pl.pallas_call(functools.partial(kernel, parts), in_specs=[pl.BlockSpec(m...  3.75 us
    pallas_call x1, Pallas kernels, bias_call(): pl.pallas_call(bias_kernel, out_shape=[jax.ShapeDtypeStruct((half, rows,...  3.6 us
  transfers between devices with their start and end apart: 23, of which 13 were waited for; matrix products, arithmetic and copies ran while one was open for 5% of the time, Pallas kernels for 28%

profile of v1, /device:TPU:0, one launch (start us, length us, event | category | flops | bytes accessed | tf_op | source)
XLA Modules:
  0.0 133.9 jit_solution(5041590863441140883)
XLA Ops:
  0.6 0.7 reshape.169.mask_ref.refs_6_
  1.3 0.7 convert_bitcast_fusion.wt_ref.refs_6_
  2.0 1.7 %copy-done.6 = bf16[24,384,128]{2,1,0:T(8,128)(2,1)S(1)} copy-done((bf16[24,384,128]{2,1,0:T(8,128)(2,1)S(1)}, bf16[24,384,128]{2,1,0:T(8,128)(2,1)}, u32[]{:S(2)}) %copy-start.6) | copy-done | bytes 2359320
  3.7 0.7 copy-done.17
  4.3 3.6 %pair_bias.1 = (bf16[8,24,384]{2,1,0:T(8,128)(2,1)S(1)}, bf16[8,24,384]{2,1,0:T(8,128)(2,1)S(1)}, f32[24,384]{1,0:T(8,128)S(1)}, f32[24,384]{1,0:T(8,128)S(1)}, f32[16,24,384]{2,1,0:T(8,128)S(1)}) custom-call(s32[1]{0:T(128)} %bitcast.core_ref, bf16[24,384,128]{2,1,0:T(8,128)(2,1)S(1)} %copy-done.6, f32[1,128]{1,0:T(1,128)S(1)} %bitcast.17, ...), custom_call_target="tpu_custom_call" | custom-call | flops 3000000000 | bytes 4000000 | tf_op jit(solution)/shard_map/pair_bias/pallas_call | solution.py:141
  8.5 1.0 collective-permute-done
  9.6 4.0 %collective-permute-start.6 = (bf16[1,4,48,384]{3,2,1,0:T(8,128)(2,1)S(1)}, bf16[1,4,48,384]{3,2,1,0:T(8,128)(2,1)S(1)}, u32[]{:S(2)}, u32[]{:S(2)}) collective-permute-start(bf16[1,4,48,384]{3,2,1,0:T(8,128)(2,1)S(1)} %get-tuple-element.69), channel_id=1, source_target_pairs={{0,8},{2,10},{4,12},{6,14},{8,0},{10,2},{12,4},{14,6},{1,9},{3,11}... | collective-permute-start | bytes 442376 | tf_op jit(solution)/shard_map/ppermute | solution.py:513
  14.4 10.1 %collective-permute-done.6 = bf16[1,4,48,384]{3,2,1,0:T(8,128)(2,1)S(1)} collective-permute-done((bf16[1,4,48,384]{3,2,1,0:T(8,128)(2,1)S(1)}, bf16[1,4,48,384]{3,2,1,0:T(8,128)(2,1)S(1)}, u32[]{:S(2)}, u32[]{:S(2)}) %collective-permute-start.6) | collective-permute-done | bytes 147488 | tf_op jit(solution)/shard_map/ppermute | solution.py:513
  24.6 0.8 pad_maximum_fusion.3
  26.2 1.0 collective-permute-done.1
  27.3 0.7 copy-done.28
  28.0 0.8 collective-permute-start.2
  28.8 6.8 %collective-permute-done.7 = bf16[2,4,48,384]{3,2,1,0:T(8,128)(2,1)} collective-permute-done((bf16[2,4,48,384]{3,2,1,0:T(8,128)(2,1)}, bf16[2,4,48,384]{3,2,1,0:T(8,128)(2,1)}, u32[]{:S(2)}, u32[]{:S(2)}) %collective-permute-start.7) | collective-permute-done | bytes 294944 | tf_op jit(solution)/shard_map/ppermute | solution.py:513
  35.6 2.0 %pad_maximum_fusion.1.refs_0_ = bf16[4,4,48,384]{3,2,1,0:T(8,128)(2,1)} fusion(bf16[2,4,48,384]{3,2,1,0:T(8,128)(2,1)} %collective-permute-done.7, bf16[1,4,48,384]{3,2,1,0:T(8,128)(2,1)} %copy-done.27, bf16[1,4,48,384]{3,2,1,0:T(8,128)(2,1)} %copy-done.26), kind=kLoop, calls=%fused_computation.1 | loop fusion | flops 589824 | bytes 1179648 | tf_op jit(solution)/shard_map/concatenate | solution.py:545
  37.5 1.9 %collective-permute-start.8 = (bf16[4,4,48,384]{3,2,1,0:T(8,128)(2,1)}, bf16[4,4,48,384]{3,2,1,0:T(8,128)(2,1)}, u32[]{:S(2)}, u32[]{:S(2)}) collective-permute-start(bf16[4,4,48,384]{3,2,1,0:T(8,128)(2,1)} %pad_maximum_fusion.1.refs_0_), channel_id=1, source_target_pairs={{0,2},{2,0},{4,6},{6,4},{8,10},{10,8},{12,14},{14,12},{1,3},{3,1},... | collective-permute-start | bytes 1769480 | tf_op jit(solution)/shard_map/ppermute | solution.py:513
  39.4 0.7 broadcast_add_fusion
  40.1 1.9 %pad_maximum_fusion.refs_0_ = bf16[4,4,48,384]{3,2,1,0:T(8,128)(2,1)} fusion(bf16[2,4,48,384]{3,2,1,0:T(8,128)(2,1)S(1)} %collective-permute-done.2, bf16[1,4,48,384]{3,2,1,0:T(8,128)(2,1)} %copy-done.28, bf16[1,4,48,384]{3,2,1,0:T(8,128)(2,1)} %copy-done.25), kind=kLoop, calls=%fused_computation | loop fusion | flops 589824 | bytes 1179648 | tf_op jit(solution)/shard_map/concatenate | solution.py:545
  42.0 1.3 %collective-permute-start.3 = (bf16[4,4,48,384]{3,2,1,0:T(8,128)(2,1)}, bf16[4,4,48,384]{3,2,1,0:T(8,128)(2,1)}, u32[]{:S(2)}, u32[]{:S(2)}) collective-permute-start(bf16[4,4,48,384]{3,2,1,0:T(8,128)(2,1)} %pad_maximum_fusion.refs_0_), channel_id=1, source_target_pairs={{0,2},{2,0},{4,6},{6,4},{8,10},{10,8},{12,14},{14,12},{1,3},{3,1},... | collective-permute-start | bytes 1769480 | tf_op jit(solution)/shard_map/ppermute | solution.py:513
  43.4 4.3 %projections.2 = (bf16[2,384,384]{2,1,0:T(8,128)(2,1)S(1)}, bf16[2,384,384]{2,1,0:T(8,128)(2,1)S(1)}, bf16[2,384,384]{2,1,0:T(8,128)(2,1)S(1)}, bf16[2,384,384]{2,1,0:T(8,128)(2,1)S(1)}) custom-call(s32[1]{0:T(128)} %bitcast.core_ref, bf16[2,384,768]{2,1,0:T(8,128)(2,1)S(1)} %copy-done.4, bf16[2,384,768]{2,1,0:T(8,128)(2,1)S(1)} %copy-done.5, ...), custom_call_target="tpu_custom_call" | custom-call | flops 1811939328 | bytes 6000000 | tf_op jit(solution)/shard_map/projections/pallas_call | solution.py:172
  47.7 0.8 copy-done.8
  48.5 0.8 copy-done.10
  49.3 0.8 copy-done.12
  50.2 0.8 copy-done.14
  51.0 0.8 add.32.offs_ref
  51.8 4.8 %projections.3 = (bf16[2,384,384]{2,1,0:T(8,128)(2,1)S(1)}, bf16[2,384,384]{2,1,0:T(8,128)(2,1)S(1)}, bf16[2,384,384]{2,1,0:T(8,128)(2,1)S(1)}, bf16[2,384,384]{2,1,0:T(8,128)(2,1)S(1)}) custom-call(s32[1]{0:T(128)} %bitcast.core_ref, bf16[2,384,768]{2,1,0:T(8,128)(2,1)} %collective-permute-done.4.act_ref, ...), custom_call_target="tpu_custom_call" | custom-call | flops 1811939328 | bytes 6000000 | tf_op jit(solution)/shard_map/projections/pallas_call | solution.py:172
  56.6 0.8 copy-done.16
  57.5 10.7 %attention.3 = (bf16[2,192,384]{2,1,0:T(8,128)(2,1)S(1)}, bf16[2,192,384]{2,1,0:T(8,128)(2,1)S(1)}, f32[4,4,48,384]{3,2,1,0:T(8,128)}, s16[4,208,384]{2,1,0:T(8,128)(2,1)}) custom-call(s32[32]{0:T(128)S(1)} %add.32.offs_ref, bf16[4,4,48,384]{3,2,1,0:T(8,128)(2,1)} %pad_maximum_fusion.1.refs_0_, bf16[4,4,48,384]{3,2,1,0:T(8,128)(2,1)} %collective-permute-done.8.refs_1_, ...), custom_call_target="tpu_custom_call" | custom-call | flops 3623878656 | bytes 4000000 | tf_op jit(solution)/shard_map/attention/pallas_call | solution.py:279
  68.2 0.7 collective-permute-start.14
  68.9 10.6 %attention.2 = (bf16[2,192,384]{2,1,0:T(8,128)(2,1)S(1)}, bf16[2,192,384]{2,1,0:T(8,128)(2,1)S(1)}, f32[4,4,48,384]{3,2,1,0:T(8,128)}, s16[4,208,384]{2,1,0:T(8,128)(2,1)}) custom-call(s32[32]{0:T(128)S(1)} %add.32.offs_ref, bf16[4,4,48,384]{3,2,1,0:T(8,128)(2,1)} %pad_maximum_fusion.refs_0_, bf16[4,4,48,384]{3,2,1,0:T(8,128)(2,1)} %collective-permute-done.3.refs_1_, ...), custom_call_target="tpu_custom_call" | custom-call | flops 3623878656 | bytes 4000000 | tf_op jit(solution)/shard_map/attention/pallas_call | solution.py:279
  79.5 1.4 %collective-permute-start.11 = (s16[4,208,384]{2,1,0:T(8,128)(2,1)}, s16[4,208,384]{2,1,0:T(8,128)(2,1)S(1)}, u32[]{:S(2)}, u32[]{:S(2)}) collective-permute-start(s16[4,208,384]{2,1,0:T(8,128)(2,1)} %get-tuple-element.51), channel_id=1, source_target_pairs={{0,2},{2,0},{4,6},{6,4},{8,10},{10,8},{12,14},{14,12},{1,3},{3,1},... | collective-permute-start | bytes 1916936 | tf_op jit(solution)/shard_map/ppermute | solution.py:513
  80.9 3.8 %collective-permute-done.14.code_ref = s16[4,208,384]{2,1,0:T(8,128)(2,1)S(1)} collective-permute-done((s16[4,208,384]{2,1,0:T(8,128)(2,1)}, s16[4,208,384]{2,1,0:T(8,128)(2,1)S(1)}, u32[]{:S(2)}, u32[]{:S(2)}) %collective-permute-start.14) | collective-permute-done | bytes 639008 | tf_op jit(solution)/shard_map/ppermute | solution.py:513
  85.0 2.2 %collective-permute-start.15 = (s16[2,208,384]{2,1,0:T(8,128)(2,1)S(1)}, s16[2,208,384]{2,1,0:T(8,128)(2,1)S(1)}, u32[]{:S(2)}, u32[]{:S(2)}) collective-permute-start(s16[2,208,384]{2,1,0:T(8,128)(2,1)S(1)} %get-tuple-element.60), channel_id=1, source_target_pairs={{0,4},{2,6},{4,0},{6,2},{8,12},{10,14},{12,8},{14,10},{1,5},{3,7},... | collective-permute-start | bytes 958472 | tf_op jit(solution)/shard_map/ppermute | solution.py:513
  87.2 8.7 %collective-permute-done.11.code_ref = s16[4,208,384]{2,1,0:T(8,128)(2,1)S(1)} collective-permute-done((s16[4,208,384]{2,1,0:T(8,128)(2,1)}, s16[4,208,384]{2,1,0:T(8,128)(2,1)S(1)}, u32[]{:S(2)}, u32[]{:S(2)}) %collective-permute-start.11) | collective-permute-done | bytes 639008 | tf_op jit(solution)/shard_map/ppermute | solution.py:513
  96.3 2.4 %collective-permute-start.12 = (s16[2,208,384]{2,1,0:T(8,128)(2,1)S(1)}, s16[2,208,384]{2,1,0:T(8,128)(2,1)S(1)}, u32[]{:S(2)}, u32[]{:S(2)}) collective-permute-start(s16[2,208,384]{2,1,0:T(8,128)(2,1)S(1)} %get-tuple-element.53), channel_id=1, source_target_pairs={{0,4},{2,6},{4,0},{6,2},{8,12},{10,14},{12,8},{14,10},{1,5},{3,7},... | collective-permute-start | bytes 958472 | tf_op jit(solution)/shard_map/ppermute | solution.py:513
  98.8 3.5 %collective-permute-start.16 = (s16[1,208,384]{2,1,0:T(8,128)(2,1)S(1)}, s16[1,208,384]{2,1,0:T(8,128)(2,1)S(1)}, u32[]{:S(2)}, u32[]{:S(2)}) collective-permute-start(s16[1,208,384]{2,1,0:T(8,128)(2,1)S(1)} %get-tuple-element.62), channel_id=1, source_target_pairs={{0,8},{2,10},{4,12},{6,14},{8,0},{10,2},{12,4},{14,6},{1,9},{3,11}... | collective-permute-start | bytes 479240 | tf_op jit(solution)/shard_map/ppermute | solution.py:513
  102.3 5.2 %collective-permute-done.12.code_ref = s16[2,208,384]{2,1,0:T(8,128)(2,1)S(1)} collective-permute-done((s16[2,208,384]{2,1,0:T(8,128)(2,1)S(1)}, s16[2,208,384]{2,1,0:T(8,128)(2,1)S(1)}, u32[]{:S(2)}, u32[]{:S(2)}) %collective-permute-start.12) | collective-permute-done | bytes 319520 | tf_op jit(solution)/shard_map/ppermute | solution.py:513
  107.8 2.8 %collective-permute-start.13 = (s16[1,208,384]{2,1,0:T(8,128)(2,1)S(1)}, s16[1,208,384]{2,1,0:T(8,128)(2,1)S(1)}, u32[]{:S(2)}, u32[]{:S(2)}) collective-permute-start(s16[1,208,384]{2,1,0:T(8,128)(2,1)S(1)} %get-tuple-element.55), channel_id=1, source_target_pairs={{0,8},{2,10},{4,12},{6,14},{8,0},{10,2},{12,4},{14,6},{1,9},{3,11}... | collective-permute-start | bytes 479240 | tf_op jit(solution)/shard_map/ppermute | solution.py:513
  110.7 7.2 %collective-permute-done.13.code_ref = s16[1,208,384]{2,1,0:T(8,128)(2,1)S(1)} collective-permute-done((s16[1,208,384]{2,1,0:T(8,128)(2,1)S(1)}, s16[1,208,384]{2,1,0:T(8,128)(2,1)S(1)}, u32[]{:S(2)}, u32[]{:S(2)}) %collective-permute-start.13) | collective-permute-done | bytes 159776 | tf_op jit(solution)/shard_map/ppermute | solution.py:513
  118.7 0.8 collective-permute-done.17.refs_2_
  119.5 0.7 pair_projection.1
  120.4 1.0 collective-permute-done.19
  121.4 0.7 collective-permute-start.20
  122.1 2.9 %collective-permute-done.20 = f32[16,128]{1,0:T(8,128)S(1)} collective-permute-done((f32[16,128]{1,0:T(8,128)S(1)}, f32[16,128]{1,0:T(8,128)S(1)}, u32[]{:S(2)}, u32[]{:S(2)}) %collective-permute-start.20) | collective-permute-done | bytes 8224 | tf_op jit(solution)/shard_map/ppermute | solution.py:513
  125.1 2.6 %output.1 = bf16[2,384,768]{2,1,0:T(8,128)(2,1)} custom-call(s32[1]{0:T(128)} %bitcast.core_ref, bf16[2,192,384]{2,1,0:T(8,128)(2,1)S(1)} %get-tuple-element.46.refs_0_, bf16[2,192,384]{2,1,0:T(8,128)(2,1)S(1)} %get-tuple-element.47.refs_1_, bf16[2,192,384]{2,1,0:T(8,128)(2,1)S(1)} %collective-permute-done.9.refs_2_, ...), custom_call_target="tpu_custom_call" | custom-call | flops 905969664 | bytes 4000000 | tf_op jit(solution)/shard_map/output/pallas_call | solution.py:400
  127.7 1.0 collective-permute-done.21
  128.7 1.4 %collective-permute-start.22 = (f32[16,128]{1,0:T(8,128)S(1)}, f32[16,128]{1,0:T(8,128)S(1)}, u32[]{:S(2)}, u32[]{:S(2)}) collective-permute-start(f32[16,128]{1,0:T(8,128)S(1)} %add.35), channel_id=1, source_target_pairs={{0,8},{2,10},{4,12},{6,14},{8,0},{10,2},{12,4},{14,6},{1,9},{3,11}... | collective-permute-start | bytes 24584 | tf_op jit(solution)/shard_map/ppermute | solution.py:513
  130.1 3.0 %pair_gradient.1 = bf16[24,384,128]{2,1,0:T(8,128)(2,1)} custom-call(s32[1]{0:T(128)} %bitcast.core_ref, f32[4,24,384]{2,1,0:T(8,128)S(1)} %get-tuple-element.56.refs_0_, f32[4,24,384]{2,1,0:T(8,128)S(1)} %get-tuple-element.63.refs_1_, f32[4,24,384]{2,1,0:T(8,128)S(1)} %collective-permute-done.17.refs_2_, f32[4,24,384]{2,1,0:T(8,128)S(1)} %collective-permute-done.18.refs_3_, ...), custom_call_target="tpu_custom_call" | custom-call | flops 4000000000 | bytes 8000000 | tf_op jit(solution)/shard_map/pair_gradient/pallas_call | solution.py:487
  133.3 0.6 add_bitcast_fusion
  (89 shorter events, 4.6 us)
Async XLA Ops:
  2.0 1.7 %copy-start.6 = (bf16[24,384,128]{2,1,0:T(8,128)(2,1)S(1)}, bf16[24,384,128]{2,1,0:T(8,128)(2,1)}, u32[]{:S(2)}) copy-start(bf16[24,384,128]{2,1,0:T(8,128)(2,1)} %refs_4_.5) | copy-start | bytes 7077892
  4.3 9.3 %copy-start.5 = (bf16[2,384,768]{2,1,0:T(8,128)(2,1)S(1)}, bf16[2,384,768]{2,1,0:T(8,128)(2,1)}, u32[]{:S(2)}) copy-start(bf16[2,384,768]{2,1,0:T(8,128)(2,1)} %cot_ref.1) | copy-start | bytes 3538948
  7.9 5.7 %copy-start.19 = (f32[16,24,384]{2,1,0:T(8,128)}, f32[16,24,384]{2,1,0:T(8,128)S(1)}, u32[]{:S(2)}) copy-start(f32[16,24,384]{2,1,0:T(8,128)S(1)} %get-tuple-element.68.refs_9_) | copy-start | bytes 1769476
  7.9 5.7 %copy-start.21 = (f32[24,384]{1,0:T(8,128)}, f32[24,384]{1,0:T(8,128)S(1)}, u32[]{:S(2)}) copy-start(f32[24,384]{1,0:T(8,128)S(1)} %get-tuple-element.66.refs_7_.refs_6_) | copy-start | bytes 110596
  8.0 5.7 %copy-start.23 = (f32[24,384]{1,0:T(8,128)}, f32[24,384]{1,0:T(8,128)S(1)}, u32[]{:S(2)}) copy-start(f32[24,384]{1,0:T(8,128)S(1)} %get-tuple-element.67.refs_8_.refs_7_) | copy-start | bytes 110596
  8.0 5.7 %copy-start.4 = (bf16[2,384,768]{2,1,0:T(8,128)(2,1)S(1)}, bf16[2,384,768]{2,1,0:T(8,128)(2,1)}, u32[]{:S(2)}) copy-start(bf16[2,384,768]{2,1,0:T(8,128)(2,1)} %act_ref.1) | copy-start | bytes 3538948
  8.0 1.5 %collective-permute-start = (bf16[8,24,384]{2,1,0:T(8,128)(2,1)S(1)}, bf16[8,24,384]{2,1,0:T(8,128)(2,1)S(1)}, u32[]{:S(2)}, u32[]{:S(2)}) collective-permute-start(bf16[8,24,384]{2,1,0:T(8,128)(2,1)S(1)} %get-tuple-element.37), channel_id=1, source_target_pairs={{0,1},{1,0},{2,3},{3,2},{4,5},{5,4},{6,7},{7,6},{8,9},{9,8},{10,11... | collective-permute-start | bytes 442376 | tf_op jit(solution)/shard_map/ppermute | solution.py:510
  9.6 17.7 %copy-start.25 = (bf16[1,4,48,384]{3,2,1,0:T(8,128)(2,1)}, bf16[1,4,48,384]{3,2,1,0:T(8,128)(2,1)S(1)}, u32[]{:S(2)}) copy-start(bf16[1,4,48,384]{3,2,1,0:T(8,128)(2,1)S(1)} %get-tuple-element.70) | copy-start | bytes 442372
  9.6 17.7 %copy-start.26 = (bf16[1,4,48,384]{3,2,1,0:T(8,128)(2,1)}, bf16[1,4,48,384]{3,2,1,0:T(8,128)(2,1)S(1)}, u32[]{:S(2)}) copy-start(bf16[1,4,48,384]{3,2,1,0:T(8,128)(2,1)S(1)} %get-tuple-element.69) | copy-start | bytes 442372
  9.6 15.0 %collective-permute-start.6 = (bf16[1,4,48,384]{3,2,1,0:T(8,128)(2,1)S(1)}, bf16[1,4,48,384]{3,2,1,0:T(8,128)(2,1)S(1)}, u32[]{:S(2)}, u32[]{:S(2)}) collective-permute-start(bf16[1,4,48,384]{3,2,1,0:T(8,128)(2,1)S(1)} %get-tuple-element.69), channel_id=1, source_target_pairs={{0,8},{2,10},{4,12},{6,14},{8,0},{10,2},{12,4},{14,6},{1,9},{3,11}... | collective-permute-start | bytes 442376 | tf_op jit(solution)/shard_map/ppermute | solution.py:513
  13.6 38.2 %collective-permute-start.4 = (bf16[2,384,768]{2,1,0:T(8,128)(2,1)S(1)}, bf16[2,384,768]{2,1,0:T(8,128)(2,1)}, u32[]{:S(2)}, u32[]{:S(2)}) collective-permute-start(bf16[2,384,768]{2,1,0:T(8,128)(2,1)S(1)} %copy-done.4), channel_id=1, source_target_pairs={{0,1},{1,0},{2,3},{3,2},{4,5},{5,4},{6,7},{7,6},{8,9},{9,8},{10,11... | collective-permute-start | bytes 3538952 | tf_op jit(solution)/shard_map/ppermute | solution.py:510
  13.7 38.2 %collective-permute-start.5 = (bf16[2,384,768]{2,1,0:T(8,128)(2,1)S(1)}, bf16[2,384,768]{2,1,0:T(8,128)(2,1)}, u32[]{:S(2)}, u32[]{:S(2)}) collective-permute-start(bf16[2,384,768]{2,1,0:T(8,128)(2,1)S(1)} %copy-done.5), channel_id=1, source_target_pairs={{0,1},{1,0},{2,3},{3,2},{4,5},{5,4},{6,7},{7,6},{8,9},{9,8},{10,11... | collective-permute-start | bytes 3538952 | tf_op jit(solution)/shard_map/ppermute | solution.py:510
  14.3 13.0 %collective-permute-start.1 = (bf16[1,4,48,384]{3,2,1,0:T(8,128)(2,1)S(1)}, bf16[1,4,48,384]{3,2,1,0:T(8,128)(2,1)S(1)}, u32[]{:S(2)}, u32[]{:S(2)}) collective-permute-start(bf16[1,4,48,384]{3,2,1,0:T(8,128)(2,1)S(1)} %get-tuple-element.70), channel_id=1, source_target_pairs={{0,8},{2,10},{4,12},{6,14},{8,0},{10,2},{12,4},{14,6},{1,9},{3,11}... | collective-permute-start | bytes 442376 | tf_op jit(solution)/shard_map/ppermute | solution.py:513
  24.6 2.7 %copy-start.27 = (bf16[1,4,48,384]{3,2,1,0:T(8,128)(2,1)}, bf16[1,4,48,384]{3,2,1,0:T(8,128)(2,1)S(1)}, u32[]{:S(2)}) copy-start(bf16[1,4,48,384]{3,2,1,0:T(8,128)(2,1)S(1)} %collective-permute-done.6) | copy-start | bytes 442372
  25.3 10.3 %collective-permute-start.7 = (bf16[2,4,48,384]{3,2,1,0:T(8,128)(2,1)}, bf16[2,4,48,384]{3,2,1,0:T(8,128)(2,1)}, u32[]{:S(2)}, u32[]{:S(2)}) collective-permute-start(bf16[2,4,48,384]{3,2,1,0:T(8,128)(2,1)} %pad_maximum_fusion.3), channel_id=1, source_target_pairs={{0,4},{2,6},{4,0},{6,2},{8,12},{10,14},{12,8},{14,10},{1,5},{3,7},... | collective-permute-start | bytes 884744 | tf_op jit(solution)/shard_map/ppermute | solution.py:513
  26.2 13.3 %copy-start.29 = (s32[16]{0:T(128)S(1)}, s32[16]{0:T(128)}, u32[]{:S(2)}) copy-start(s32[16]{0:T(128)} %broadcast_multiply_fusion) | copy-start | bytes 196
  28.0 15.4 %copy-start.1 = (bf16[768,768]{1,0:T(8,128)(2,1)S(1)}, bf16[768,768]{1,0:T(8,128)(2,1)}, u32[]{:S(2)}) copy-start(bf16[768,768]{1,0:T(8,128)(2,1)} %wq_ref.3) | copy-start | bytes 3538948
  28.0 12.1 %collective-permute-start.2 = (bf16[2,4,48,384]{3,2,1,0:T(8,128)(2,1)S(1)}, bf16[2,4,48,384]{3,2,1,0:T(8,128)(2,1)S(1)}, u32[]{:S(2)}, u32[]{:S(2)}) collective-permute-start(bf16[2,4,48,384]{3,2,1,0:T(8,128)(2,1)S(1)} %pad_maximum_fusion.2), channel_id=1, source_target_pairs={{0,4},{2,6},{4,0},{6,2},{8,12},{10,14},{12,8},{14,10},{1,5},{3,7},... | collective-permute-start | bytes 884744 | tf_op jit(solution)/shard_map/ppermute | solution.py:513
  37.5 19.9 %collective-permute-start.8 = (bf16[4,4,48,384]{3,2,1,0:T(8,128)(2,1)}, bf16[4,4,48,384]{3,2,1,0:T(8,128)(2,1)}, u32[]{:S(2)}, u32[]{:S(2)}) collective-permute-start(bf16[4,4,48,384]{3,2,1,0:T(8,128)(2,1)} %pad_maximum_fusion.1.refs_0_), channel_id=1, source_target_pairs={{0,2},{2,0},{4,6},{6,4},{8,10},{10,8},{12,14},{14,12},{1,3},{3,1},... | collective-permute-start | bytes 1769480 | tf_op jit(solution)/shard_map/ppermute | solution.py:513
  42.0 26.9 %collective-permute-start.3 = (bf16[4,4,48,384]{3,2,1,0:T(8,128)(2,1)}, bf16[4,4,48,384]{3,2,1,0:T(8,128)(2,1)}, u32[]{:S(2)}, u32[]{:S(2)}) collective-permute-start(bf16[4,4,48,384]{3,2,1,0:T(8,128)(2,1)} %pad_maximum_fusion.refs_0_), channel_id=1, source_target_pairs={{0,2},{2,0},{4,6},{6,4},{8,10},{10,8},{12,14},{14,12},{1,3},{3,1},... | collective-permute-start | bytes 1769480 | tf_op jit(solution)/shard_map/ppermute | solution.py:513
  49.3 0.8 copy-start.12
  51.8 5.7 %copy-start.9 = (bf16[2,384,384]{2,1,0:T(8,128)(2,1)S(1)}, bf16[2,384,384]{2,1,0:T(8,128)(2,1)}, u32[]{:S(2)}) copy-start(bf16[2,384,384]{2,1,0:T(8,128)(2,1)} %copy-done.8) | copy-start | bytes 1769476
  51.8 5.7 %copy-start.11 = (bf16[2,384,384]{2,1,0:T(8,128)(2,1)S(1)}, bf16[2,384,384]{2,1,0:T(8,128)(2,1)}, u32[]{:S(2)}) copy-start(bf16[2,384,384]{2,1,0:T(8,128)(2,1)} %copy-done.10) | copy-start | bytes 1769476
  51.8 5.7 %copy-start.13 = (bf16[2,384,384]{2,1,0:T(8,128)(2,1)S(1)}, bf16[2,384,384]{2,1,0:T(8,128)(2,1)}, u32[]{:S(2)}) copy-start(bf16[2,384,384]{2,1,0:T(8,128)(2,1)} %copy-done.12) | copy-start | bytes 1769476
  51.8 5.7 %copy-start.15 = (bf16[2,384,384]{2,1,0:T(8,128)(2,1)S(1)}, bf16[2,384,384]{2,1,0:T(8,128)(2,1)}, u32[]{:S(2)}) copy-start(bf16[2,384,384]{2,1,0:T(8,128)(2,1)} %copy-done.14) | copy-start | bytes 1769476
  56.6 0.8 copy-start.16
  68.2 16.5 %copy-start.2 = (f32[4,4,48,384]{3,2,1,0:T(8,128)S(1)}, f32[4,4,48,384]{3,2,1,0:T(8,128)}, u32[]{:S(2)}) copy-start(f32[4,4,48,384]{3,2,1,0:T(8,128)} %get-tuple-element.57.own_ref) | copy-start | bytes 3538948
  68.2 16.5 %collective-permute-start.14 = (s16[4,208,384]{2,1,0:T(8,128)(2,1)}, s16[4,208,384]{2,1,0:T(8,128)(2,1)S(1)}, u32[]{:S(2)}, u32[]{:S(2)}) collective-permute-start(s16[4,208,384]{2,1,0:T(8,128)(2,1)} %get-tuple-element.58), channel_id=1, source_target_pairs={{0,2},{2,0},{4,6},{6,4},{8,10},{10,8},{12,14},{14,12},{1,3},{3,1},... | collective-permute-start | bytes 1916936 | tf_op jit(solution)/shard_map/ppermute | solution.py:513
  79.5 16.4 %copy-start.3 = (f32[4,4,48,384]{3,2,1,0:T(8,128)S(1)}, f32[4,4,48,384]{3,2,1,0:T(8,128)}, u32[]{:S(2)}) copy-start(f32[4,4,48,384]{3,2,1,0:T(8,128)} %get-tuple-element.50.own_ref) | copy-start | bytes 3538948
  79.5 16.4 %collective-permute-start.11 = (s16[4,208,384]{2,1,0:T(8,128)(2,1)}, s16[4,208,384]{2,1,0:T(8,128)(2,1)S(1)}, u32[]{:S(2)}, u32[]{:S(2)}) collective-permute-start(s16[4,208,384]{2,1,0:T(8,128)(2,1)} %get-tuple-element.51), channel_id=1, source_target_pairs={{0,2},{2,0},{4,6},{6,4},{8,10},{10,8},{12,14},{14,12},{1,3},{3,1},... | collective-permute-start | bytes 1916936 | tf_op jit(solution)/shard_map/ppermute | solution.py:513
  85.0 13.7 %collective-permute-start.15 = (s16[2,208,384]{2,1,0:T(8,128)(2,1)S(1)}, s16[2,208,384]{2,1,0:T(8,128)(2,1)S(1)}, u32[]{:S(2)}, u32[]{:S(2)}) collective-permute-start(s16[2,208,384]{2,1,0:T(8,128)(2,1)S(1)} %get-tuple-element.60), channel_id=1, source_target_pairs={{0,4},{2,6},{4,0},{6,2},{8,12},{10,14},{12,8},{14,10},{1,5},{3,7},... | collective-permute-start | bytes 958472 | tf_op jit(solution)/shard_map/ppermute | solution.py:513
  96.3 11.3 %collective-permute-start.12 = (s16[2,208,384]{2,1,0:T(8,128)(2,1)S(1)}, s16[2,208,384]{2,1,0:T(8,128)(2,1)S(1)}, u32[]{:S(2)}, u32[]{:S(2)}) collective-permute-start(s16[2,208,384]{2,1,0:T(8,128)(2,1)S(1)} %get-tuple-element.53), channel_id=1, source_target_pairs={{0,4},{2,6},{4,0},{6,2},{8,12},{10,14},{12,8},{14,10},{1,5},{3,7},... | collective-permute-start | bytes 958472 | tf_op jit(solution)/shard_map/ppermute | solution.py:513
  98.6 20.8 %copy-start.7 = (bf16[24,384,128]{2,1,0:T(8,128)(2,1)S(1)}, bf16[24,384,128]{2,1,0:T(8,128)(2,1)}, u32[]{:S(2)}) copy-start(bf16[24,384,128]{2,1,0:T(8,128)(2,1)} %refs_4_.5) | copy-start | bytes 7077892
  98.6 20.8 %copy-start.18 = (f32[128]{0:T(128)S(1)}, f32[128]{0:T(128)}, u32[]{:S(2)}) copy-start(f32[128]{0:T(128)} %param.13) | copy-start | bytes 1540
  98.6 20.8 %copy-start.22 = (f32[24,384]{1,0:T(8,128)S(1)}, f32[24,384]{1,0:T(8,128)}, u32[]{:S(2)}) copy-start(f32[24,384]{1,0:T(8,128)} %copy-done.21) | copy-start | bytes 110596
  98.6 20.8 %copy-start.24 = (f32[24,384]{1,0:T(8,128)S(1)}, f32[24,384]{1,0:T(8,128)}, u32[]{:S(2)}) copy-start(f32[24,384]{1,0:T(8,128)} %copy-done.23) | copy-start | bytes 110596
  98.8 11.7 %collective-permute-start.16 = (s16[1,208,384]{2,1,0:T(8,128)(2,1)S(1)}, s16[1,208,384]{2,1,0:T(8,128)(2,1)S(1)}, u32[]{:S(2)}, u32[]{:S(2)}) collective-permute-start(s16[1,208,384]{2,1,0:T(8,128)(2,1)S(1)} %get-tuple-element.62), channel_id=1, source_target_pairs={{0,8},{2,10},{4,12},{6,14},{8,0},{10,2},{12,4},{14,6},{1,9},{3,11}... | collective-permute-start | bytes 479240 | tf_op jit(solution)/shard_map/ppermute | solution.py:513
  107.8 10.2 %collective-permute-start.13 = (s16[1,208,384]{2,1,0:T(8,128)(2,1)S(1)}, s16[1,208,384]{2,1,0:T(8,128)(2,1)S(1)}, u32[]{:S(2)}, u32[]{:S(2)}) collective-permute-start(s16[1,208,384]{2,1,0:T(8,128)(2,1)S(1)} %get-tuple-element.55), channel_id=1, source_target_pairs={{0,8},{2,10},{4,12},{6,14},{8,0},{10,2},{12,4},{14,6},{1,9},{3,11}... | collective-permute-start | bytes 479240 | tf_op jit(solution)/shard_map/ppermute | solution.py:513
  110.6 8.0 %collective-permute-start.18 = (f32[4,24,384]{2,1,0:T(8,128)S(1)}, f32[4,24,384]{2,1,0:T(8,128)S(1)}, u32[]{:S(2)}, u32[]{:S(2)}) collective-permute-start(f32[4,24,384]{2,1,0:T(8,128)S(1)} %get-tuple-element.65), channel_id=1, source_target_pairs={{0,1},{1,0},{2,3},{3,2},{4,5},{5,4},{6,7},{7,6},{8,9},{9,8},{10,11... | collective-permute-start | bytes 442376 | tf_op jit(solution)/shard_map/ppermute | solution.py:510
  118.0 1.4 %collective-permute-start.17 = (f32[4,24,384]{2,1,0:T(8,128)S(1)}, f32[4,24,384]{2,1,0:T(8,128)S(1)}, u32[]{:S(2)}, u32[]{:S(2)}) collective-permute-start(f32[4,24,384]{2,1,0:T(8,128)S(1)} %get-tuple-element.64), channel_id=1, source_target_pairs={{0,1},{1,0},{2,3},{3,2},{4,5},{5,4},{6,7},{7,6},{8,9},{9,8},{10,11... | collective-permute-start | bytes 442376 | tf_op jit(solution)/shard_map/ppermute | solution.py:510
  118.1 7.0 %collective-permute-start.10 = (bf16[2,192,384]{2,1,0:T(8,128)(2,1)S(1)}, bf16[2,192,384]{2,1,0:T(8,128)(2,1)S(1)}, u32[]{:S(2)}, u32[]{:S(2)}) collective-permute-start(bf16[2,192,384]{2,1,0:T(8,128)(2,1)S(1)} %get-tuple-element.49), channel_id=1, source_target_pairs={{0,1},{1,0},{2,3},{3,2},{4,5},{5,4},{6,7},{7,6},{8,9},{9,8},{10,11... | collective-permute-start | bytes 884744 | tf_op jit(solution)/shard_map/ppermute | solution.py:510
  118.6 6.5 %collective-permute-start.9 = (bf16[2,192,384]{2,1,0:T(8,128)(2,1)S(1)}, bf16[2,192,384]{2,1,0:T(8,128)(2,1)S(1)}, u32[]{:S(2)}, u32[]{:S(2)}) collective-permute-start(bf16[2,192,384]{2,1,0:T(8,128)(2,1)S(1)} %get-tuple-element.48), channel_id=1, source_target_pairs={{0,1},{1,0},{2,3},{3,2},{4,5},{5,4},{6,7},{7,6},{8,9},{9,8},{10,11... | collective-permute-start | bytes 884744 | tf_op jit(solution)/shard_map/ppermute | solution.py:510
  119.4 5.6 %copy-start = (bf16[768,768]{1,0:T(8,128)(2,1)S(1)}, bf16[768,768]{1,0:T(8,128)(2,1)}, u32[]{:S(2)}) copy-start(bf16[768,768]{1,0:T(8,128)(2,1)} %refs_5_.1) | copy-start | bytes 3538948
  120.2 1.2 collective-permute-start.19
  121.4 3.7 %collective-permute-start.20 = (f32[16,128]{1,0:T(8,128)S(1)}, f32[16,128]{1,0:T(8,128)S(1)}, u32[]{:S(2)}, u32[]{:S(2)}) collective-permute-start(f32[16,128]{1,0:T(8,128)S(1)} %add.33), channel_id=1, source_target_pairs={{0,2},{2,0},{4,6},{6,4},{8,10},{10,8},{12,14},{14,12},{1,3},{3,1},... | collective-permute-start | bytes 24584 | tf_op jit(solution)/shard_map/ppermute | solution.py:513
  125.0 3.7 %collective-permute-start.21 = (f32[16,128]{1,0:T(8,128)S(1)}, f32[16,128]{1,0:T(8,128)S(1)}, u32[]{:S(2)}, u32[]{:S(2)}) collective-permute-start(f32[16,128]{1,0:T(8,128)S(1)} %add.34), channel_id=1, source_target_pairs={{0,4},{2,6},{4,0},{6,2},{8,12},{10,14},{12,8},{14,10},{1,5},{3,7},... | collective-permute-start | bytes 24584 | tf_op jit(solution)/shard_map/ppermute | solution.py:513
  125.1 5.0 %copy-start.20 = (f32[16,24,384]{2,1,0:T(8,128)S(1)}, f32[16,24,384]{2,1,0:T(8,128)}, u32[]{:S(2)}) copy-start(f32[16,24,384]{2,1,0:T(8,128)} %copy-done.19) | copy-start | bytes 1769476
  128.7 4.5 %collective-permute-start.22 = (f32[16,128]{1,0:T(8,128)S(1)}, f32[16,128]{1,0:T(8,128)S(1)}, u32[]{:S(2)}, u32[]{:S(2)}) collective-permute-start(f32[16,128]{1,0:T(8,128)S(1)} %add.35), channel_id=1, source_target_pairs={{0,8},{2,10},{4,12},{6,14},{8,0},{10,2},{12,4},{14,6},{1,9},{3,11}... | collective-permute-start | bytes 24584 | tf_op jit(solution)/shard_map/ppermute | solution.py:513
  (5 other events, 3.8 us)

commit v2 on v1

--- a/solution.py
+++ b/solution.py
@@ -14,8 +14,14 @@
 LOG2E = math.log2(math.e)
 NT = (((1,), (1,)), ((), ()))
 TN = (((0,), (0,)), ((), ()))
+COST = pl.CostEstimate(flops=1000, bytes_accessed=1000, transcendentals=0)
 VMEM_LIMIT = 48 * 1024 * 1024
-CHUNKS = ((4, True), (4, True))
+VMEM_WIDE = 60 * 1024 * 1024
+CHUNKS = (3, 3, 2)
+GATHER_OTHER = (2,)
+SCATTER_OTHER = (0,)
+EARLY = 9
+LATE = False
 
 
 def normalize(pair_rep, pair_gain):
@@ -107,9 +113,9 @@
 
 def bias_kernel(core_ref, pair_ref, gain_ref, wt_ref, mask_ref, own_ref, other_ref, mean_ref, rstd_ref, held):
     rows, tok, chan = pair_ref.shape
-    heads = wt_ref.shape[0]
+    heads = wt_ref.shape[1]
     half = heads // 2
-    scaled = wt_ref[...] * gain_ref[...]
+    scaled = wt_ref[...].astype(F32).T * gain_ref[...]
     total = jnp.sum(scaled, axis=1, keepdims=True)
     left = jnp.concatenate([*pieces3(scaled), jnp.ones((16, chan), BF16)], axis=0)
     lane = lax.broadcasted_iota(jnp.int32, (tok, 128), 1)
@@ -128,14 +134,14 @@
         held[:, i, :] = (raw - total * mean_row) * rstd[i : i + 1]
         mean_ref[i : i + 1, :] = mean_row
     core = core_ref[0]
-    live = (mask_ref[...] > 0)[None]
+    live = (mask_ref[...].reshape(1, 1, tok) > 0)
     own_ref[...] = jnp.where(live, held[pl.ds(core * half, half)], -1e30).astype(BF16)
     other_ref[...] = jnp.where(live, held[pl.ds((1 - core) * half, half)], -1e30).astype(BF16)
 
 
-def bias_call(core, pair_rep, gain, w_t, mask_row):
+def bias_call(core, pair_rep, gain, w_pair, mask_row):
     rows, tok, chan = pair_rep.shape
-    heads = w_t.shape[0]
+    heads = w_pair.shape[1]
     half = heads // 2
     vm = pl.BlockSpec(memory_space=pltpu.VMEM)
     return pl.pallas_call(
@@ -150,9 +156,9 @@
         in_specs=[pl.BlockSpec(memory_space=pltpu.SMEM)] + [vm] * 4,
         out_specs=[vm] * 5,
         compiler_params=pltpu.CompilerParams(vmem_limit_bytes=VMEM_LIMIT),
-        cost_estimate=pl.CostEstimate(flops=int(3e9), bytes_accessed=int(4e6), transcendentals=0),
+        cost_estimate=COST,
         name="pair_bias",
-    )(core, pair_rep, gain, w_t, mask_row)
+    )(core, pair_rep, gain, w_pair, mask_row)
 
 
 def project_kernel(core_ref, act_ref, cot_ref, wq_ref, wk_ref, wv_ref, wo_ref, mask_ref, q_ref, k_ref, v_ref, d_ref):
@@ -180,10 +186,8 @@
             out_specs=[out] * 4,
         ),
         out_shape=[jax.ShapeDtypeStruct((samples, half, tok), BF16)] * 4,
-        compiler_params=pltpu.CompilerParams(vmem_limit_bytes=VMEM_LIMIT),
-        cost_estimate=pl.CostEstimate(
-            flops=8 * samples * tok * width * half, bytes_accessed=int(6e6), transcendentals=0
-        ),
+        compiler_params=pltpu.CompilerParams(vmem_limit_bytes=VMEM_WIDE),
+        cost_estimate=COST,
         name="projections",
     )(core, act, cot, w_query, w_key, w_value, w_out, mask_row)
 
@@ -207,21 +211,24 @@
     return jnp.concatenate([block, block], axis=0).astype(jnp.int32).astype(jnp.int16)
 
 
-def attention_kernel(arrays, head_width, offs_ref, *refs):
+def attention_kernel(arrays, head_width, masks, out_masks, place_ref, *refs):
     bias_refs = refs[:arrays]
     q0, k0, v0, d0, q1, k1, v1, d1 = refs[arrays : arrays + 8]
     mixed0, mixed1, own_ref, code_ref, bias_f, grad, held = refs[arrays + 8 :]
     stay, _, rows, _ = own_ref.shape
     part = rows // 2
     head, chunk = pl.program_id(0), pl.num_programs(0)
-    at = 0
-    for ref in bias_refs:
-        for b in range(ref.shape[0]):
-            block = ref[b, 0].astype(F32) * LOG2E
-            for side in range(2):
-                start = pl.multiple_of(offs_ref[at], 8)
-                bias_f[pl.ds(start, part), :] = block[side * part : (side + 1) * part]
-                at += 1
+    chip, core = place_ref[0], place_ref[1]
+
+    def starts(mask):
+        first = (chip ^ mask) * rows
+        return [pl.multiple_of(first + side * part, 8) for side in (core, 1 - core)]
+
+    blocks = [(ref, b) for ref in bias_refs for b in range(ref.shape[0])]
+    for mask, (ref, b) in zip(masks, blocks):
+        block = ref[b, 0].astype(F32) * LOG2E
+        for side, start in enumerate(starts(mask)):
+            bias_f[pl.ds(start, part), :] = block[side * part : (side + 1) * part]
     factor = head_width ** (-0.5) * LOG2E
     count = q0.shape[0]
 
@@ -250,9 +257,8 @@
     def _():
         held[...] = jnp.zeros_like(held)
 
-    for b in range(2 * stay):
-        starts = [pl.multiple_of(offs_ref[4 * stay + 2 * b + side], 8) for side in range(2)]
-        block = jnp.concatenate([grad[pl.ds(start, part), :] for start in starts], axis=0)
+    for b, mask in enumerate(out_masks):
+        block = jnp.concatenate([grad[pl.ds(start, part), :] for start in starts(mask)], axis=0)
         if b < stay:
             own_ref[b, 0] = block
         else:
@@ -267,17 +273,17 @@
             code_ref[b, last:, :] = pack_levels([held[b]])
 
 
-def attention_call(head_width, offsets, bias_arrays, first, own_proj, sib_proj):
-    blocks = sum(array.shape[0] for array in bias_arrays)
+def attention_call(head_width, masks, out_masks, place, bias_arrays, first, own_proj, sib_proj):
+    blocks = len(masks)
     _, chunk, rows, tok = bias_arrays[0].shape
     count = own_proj[0].shape[0]
     stay = blocks // 2
-    head = pl.BlockSpec((count, head_width, tok), lambda h, o: (0, first + h, 0))
+    head = pl.BlockSpec((count, head_width, tok), lambda h, _: (0, first + h, 0))
     mixed = pl.BlockSpec((count, head_width, tok), lambda h, o: (0, h, 0))
     coded = (stay, chunk * rows + 16, tok)
     tiles = 2 * count * chunk
     return pl.pallas_call(
-        functools.partial(attention_kernel, len(bias_arrays), head_width),
+        functools.partial(attention_kernel, len(bias_arrays), head_width, masks, out_masks),
         grid_spec=pltpu.PrefetchScalarGridSpec(
             num_scalar_prefetch=1,
             grid=(chunk,),
@@ -303,12 +309,10 @@
             jax.ShapeDtypeStruct((stay, chunk, rows, tok), F32),
             jax.ShapeDtypeStruct(coded, jnp.int16),
         ],
-        compiler_params=pltpu.CompilerParams(vmem_limit_bytes=VMEM_LIMIT),
-        cost_estimate=pl.CostEstimate(
-            flops=tiles * 6 * tok * tok * 256, bytes_accessed=int(4e6), transcendentals=tiles * tok * tok
-        ),
+        compiler_params=pltpu.CompilerParams(vmem_limit_bytes=VMEM_WIDE),
+        cost_estimate=COST,
         name="attention",
-    )(offsets, *bias_arrays, *own_proj, *sib_proj)
+    )(place, *bias_arrays, *own_proj, *sib_proj)
 
 
 def plain_call(kernel, name, out_shape, *operands):
@@ -319,9 +323,21 @@
         out_specs=[vm] * len(out_shape),
         out_shape=out_shape,
         compiler_params=pltpu.CompilerParams(vmem_limit_bytes=VMEM_LIMIT),
-        cost_estimate=pl.CostEstimate(flops=int(4e6), bytes_accessed=int(3e6), transcendentals=0),
+        cost_estimate=COST,
         name=name,
     )(*operands)
+
+
+def concat_kernel(*refs):
+    out_ref, at = refs[-1], 0
+    for ref in refs[:-1]:
+        out_ref[at : at + ref.shape[0]] = ref[...]
+        at += ref.shape[0]
+
+
+def concat_call(*arrays):
+    blocks = sum(x.shape[0] for x in arrays)
+    return plain_call(concat_kernel, "concat", [jax.ShapeDtypeStruct((blocks, *arrays[0].shape[1:]), BF16)], *arrays)[0]
 
 
 def join_kernel(own_ref, code_ref, stay_ref, next_ref):
@@ -392,17 +408,17 @@
 
 
 def output_call(core, own, other, w_out, mask_row):
-    samples, size, tok = own[0].shape
+    samples, _, tok = own[0].shape
     parts = len(own)
     width = w_out.shape[0]
     half = width // 2
-    block = pl.BlockSpec((1, size, tok), lambda s, c: (s, 0, 0))
+    blocks = [pl.BlockSpec((1, x.shape[1], tok), lambda s, c: (s, 0, 0)) for x in (*own, *other)]
     return pl.pallas_call(
         functools.partial(output_kernel, parts),
         grid_spec=pltpu.PrefetchScalarGridSpec(
             num_scalar_prefetch=1,
             grid=(samples,),
-            in_specs=[block] * (2 * parts)
+            in_specs=blocks
             + [
                 pl.BlockSpec((half, width), lambda s, c: (c[0], 0)),
                 pl.BlockSpec((half, width), lambda s, c: (1 - c[0], 0)),
@@ -411,10 +427,8 @@
             out_specs=pl.BlockSpec((1, tok, width), lambda s, c: (s, 0, 0)),
         ),
         out_shape=jax.ShapeDtypeStruct((samples, tok, width), BF16),
-        compiler_params=pltpu.CompilerParams(vmem_limit_bytes=VMEM_LIMIT),
-        cost_estimate=pl.CostEstimate(
-            flops=2 * samples * tok * width * width, bytes_accessed=int(4e6), transcendentals=0
-        ),
+        compiler_params=pltpu.CompilerParams(vmem_limit_bytes=VMEM_WIDE),
+        cost_estimate=COST,
         name="output",
     )(core, *own, *other, w_out, w_out, mask_row)
 
@@ -444,15 +458,16 @@
 
 def pair_grad_kernel(parts, core_ref, *refs):
     own_refs, other_refs = refs[:parts], refs[parts : 2 * parts]
-    pair_ref, gain_ref, wt_ref, mean_ref, rstd_ref, bias_ref, out_ref = refs[2 * parts :]
+    pair_ref, gain_ref, wt_ref, mean_ref, rstd_ref, bias_ref, out_ref, turned = refs[2 * parts :]
     rows, tok, chan = pair_ref.shape
-    half = wt_ref.shape[0] // 2
+    half = wt_ref.shape[1] // 2
     core = core_ref[0]
+    turned[...] = wt_ref[...].astype(F32).T
 
     def own_first(take):
         return jnp.concatenate([take(core * half), take((1 - core) * half)], axis=0)
 
-    scaled = own_first(lambda at: wt_ref[pl.ds(pl.multiple_of(at, half), half), :]) * gain_ref[...]
+    scaled = own_first(lambda at: turned[pl.ds(pl.multiple_of(at, half), half), :]) * gain_ref[...]
     scaled = scaled - jnp.mean(scaled, axis=1, keepdims=True)
     wh, wm, wl = pieces3(scaled)
     project = jnp.concatenate([wh, wm, wh, wl, wm, wh], axis=0)
@@ -481,7 +496,7 @@
         out_ref[i] = (both[:, :chan] - pair_ref[i].astype(F32) * both[:, chan:]).astype(BF16)
 
 
-def final_call(kernel, name, core, own, other, operands, out_shape):
+def final_call(kernel, name, core, own, other, operands, out_shape, scratch=()):
     vm = pl.BlockSpec(memory_space=pltpu.VMEM)
     parts = len(own)
     return pl.pallas_call(
@@ -489,8 +504,9 @@
         in_specs=[pl.BlockSpec(memory_space=pltpu.SMEM)] + [vm] * (2 * parts + len(operands)),
         out_specs=vm,
         out_shape=out_shape,
+        scratch_shapes=scratch,
         compiler_params=pltpu.CompilerParams(vmem_limit_bytes=VMEM_LIMIT),
-        cost_estimate=pl.CostEstimate(flops=int(4e9), bytes_accessed=int(8e6), transcendentals=0),
+        cost_estimate=COST,
         name=name,
     )(core, *own, *other, *operands)
 
@@ -512,62 +528,97 @@
     def swap(x, bit):
         return lax.ppermute(x, "chip", [(c, c ^ bit) for c in range(chips)])
 
-    masks = [0]
-    for bit in bits:
-        masks = masks + [m ^ bit for m in masks]
-    places = [jnp.stack([chip ^ m for m in masks]), jnp.stack([chip * 0 + c for c in range(chips)])]
-    sides = jnp.stack([core, 1 - core])
-
-    def offsets_of(places_in):
-        both = jnp.concatenate([places_in, places[0]])
-        return (both[:, None] * (2 * rows) + sides[None, :] * rows).reshape(-1).astype(jnp.int32)
-
-    doubled, gathered = [offsets_of(p) for p in places]
+    tie = lax.optimization_barrier
+    place = jnp.stack([chip, core]).astype(jnp.int32)
     core_1 = core.reshape(1).astype(jnp.int32)
     gain = pair_gain.reshape(1, chan)
-    w_t = w_pair.T.astype(F32)
+    normal, other = bits, [*bits[:-2], bits[-1], bits[-2]]
+    count, levels = len(CHUNKS), len(bits)
+    gather_bits = [other if n in GATHER_OTHER else normal for n in range(count)]
+    scatter_bits = [list(reversed(other if n in SCATTER_OTHER else normal)) for n in range(count)]
+
+    def masks_of(order):
+        masks = [0]
+        for bit in order:
+            masks = masks + [m ^ bit for m in masks]
+        return masks
+
+    sib_act, sib_cot = swap_core(activations), swap_core(cotangent)
+    bias_own, bias_other, mean_rows, rstd_rows, bias_rows = bias_call(core_1, pair_rep, gain, w_pair, token_mask)
+    bias_chip = jnp.concatenate([bias_own, swap_core(bias_other)], axis=1)[None]
     mask_row = token_mask.reshape(1, tok)
-
-    sib_act, sib_cot = swap_core(activations), swap_core(cotangent)
-    bias_own, bias_other, mean_rows, rstd_rows, bias_rows = bias_call(core_1, pair_rep, gain, w_t, mask_row)
-    bias_chip = jnp.concatenate([bias_own, swap_core(bias_other)], axis=1)[None]
-
     weights = (w_query, w_key, w_value, w_out)
     own_proj = project_call(core_1, activations, cotangent, *weights, mask_row)
     sib_proj = project_call(core_1, sib_act, sib_cot, *weights, mask_row)
 
+    firsts = [sum(CHUNKS[:n]) for n in range(count)]
+    arrays = []
+    for n, size in enumerate(CHUNKS):
+        mine = bias_chip[:, firsts[n] : firsts[n] + size]
+        for level, bit in enumerate(gather_bits[n][:-1]):
+            coming = swap(mine, bit)
+            if n == 0 and level == 0:
+                coming, own_proj = tie((coming, own_proj))
+            if n == 0 and level == 1:
+                coming, sib_proj = tie((coming, sib_proj))
+            mine = concat_call(mine, coming)
+        arrays.append([mine, swap(mine, gather_bits[n][-1])])
+
     mixed_own, mixed_other, grads_own, grads_other = [], [], [], []
-    first = 0
-    for size, by_permute in CHUNKS:
-        mine = bias_chip[:, first : first + size]
-        if by_permute:
-            for bit in bits[:-1]:
-                mine = jnp.concatenate([mine, swap(mine, bit)], axis=0)
-            arrays, offsets = [mine, swap(mine, bits[-1])], doubled
-        else:
-            arrays, offsets = [lax.all_gather(mine, "chip", axis=0, tiled=True)], gathered
-        mixed0, mixed1, stay, codes = attention_call(head_width, offsets, arrays, first, own_proj, sib_proj)
+    far = [None] * count
+    stays = [None] * count
+    level_of = [0] * count
+
+    def join(n):
+        level_of[n] += 1
+        stays[n], codes = join_call(stays[n], far[n])
+        return codes
+
+    for n in range(count):
+        if n == count - 1 and n >= EARLY:
+            for k in range(n - EARLY + 1):
+                codes = join(k)
+                codes, place = tie((codes, place))
+                far[k] = swap(codes, scatter_bits[k][1])
+        mixed0, mixed1, stays[n], codes = attention_call(
+            head_width, masks_of(gather_bits[n]), masks_of(reversed(scatter_bits[n])),
+            place, arrays[n], firsts[n], own_proj, sib_proj,
+        )
         mixed_own.append(mixed0)
-        mixed_other.append(swap_core(mixed1))
-        for bit in reversed(bits[1:]):
-            stay, codes = join_call(stay, swap(codes, bit))
-        here, there = total_call(stay, swap(codes, bits[0]))
+        mixed_other.append(mixed1)
+        far[n] = swap(codes, scatter_bits[n][0])
+    if LATE:
+        first_join = join(1)
+        first_join, *mixed_other = tie((first_join, *mixed_other))
+        far[1] = swap(first_join, scatter_bits[1][1])
+    mixed_other = [swap_core(mixed1) for mixed1 in mixed_other]
+    attended = output_call(core_1, mixed_own, mixed_other, w_out, mask_row)
+    for n in range(count):
+        while level_of[n] < levels - 1:
+            if n == count - 1 and level_of[n] == 1:
+                far[n], attended = tie((far[n], attended))
+            codes = join(n)
+            far[n] = swap(codes, scatter_bits[n][level_of[n]])
+        here, there = total_call(stays[n], far[n])
         grads_own.append(here)
         grads_other.append(swap_core(there))
-        first += size
-
-    attended = output_call(core_1, mixed_own, mixed_other, w_out, mask_row)
+
     projection = final_call(
         projection_kernel, "pair_projection", core_1, grads_own, grads_other,
         (pair_rep, gain, mean_rows, rstd_rows), jax.ShapeDtypeStruct((heads, chan), F32),
     )
+    rstd_rows, projection = tie((rstd_rows, projection))
+    grad_pair = final_call(
+        pair_grad_kernel, "pair_gradient", core_1, grads_own, grads_other,
+        (pair_rep, gain, w_pair, mean_rows, rstd_rows, bias_rows), jax.ShapeDtypeStruct(pair_rep.shape, BF16),
+        (pltpu.VMEM((heads, chan), F32),),
+    )
     projection = projection + swap_core(projection)
     for bit in reversed(bits):
-        projection = projection + swap(projection, bit)
-    grad_pair = final_call(
-        pair_grad_kernel, "pair_gradient", core_1, grads_own, grads_other,
-        (pair_rep, gain, w_t, mean_rows, rstd_rows, bias_rows), jax.ShapeDtypeStruct(pair_rep.shape, BF16),
-    )
+        other = swap(projection, bit)
+        if bit == bits[-1]:
+            other, grad_pair = tie((other, grad_pair))
+        projection = projection + other
     return (attended, grad_pair, projection.T)
 
 
@@ -579,7 +630,7 @@
         parts = mesh.shape["grp"]
         rows, heads, tok = pair_rep.shape[0] // (parts * devices), w_pair.shape[1], pair_rep.shape[1]
         power = devices >= 8 and devices & (devices - 1) == 0
-        if power and rows % 8 == 0 and rows <= 128 and heads == 2 * sum(size for size, _ in CHUNKS) and tok % 128 == 0:
+        if power and rows % 8 == 0 and rows <= 128 and heads == 2 * sum(CHUNKS) and tok % 128 == 0:
             inner = Mesh(mesh.devices.reshape(parts, devices // 2, 2), ("grp", "chip", "core"))
             whole = P(("grp", "chip", "core"), None, None)
             body = functools.partial(per_device_tiled, devices // 2)

time: 134 us -> 124 us (0.925)
  waiting for transfers between devices: 49.9 us -> 30.4 us
  Pallas kernels: 41.5 us -> 52.4 us
  starting transfers between devices: 25.5 us -> 31.5 us
  other arithmetic: 7.23 us -> 1.31 us
  local copies, waits for them, and re-layouts: 8.76 us -> 6.97 us
    ppermute x15 -> x21, waiting for transfers between devices: 47.1 us -> 27.2 us  [swap(): return lax.ppermute(x, 'chip', [(c, c ^ bit) for c in range(chips)])]
    ppermute x15 -> x21, starting transfers between devices: 23.6 us -> 29.5 us  [swap(): return lax.ppermute(x, 'chip', [(c, c ^ bit) for c in range(chips)])]
    concatenate x4 -> x0, other arithmetic: 4.64 us -> none  [per_device_tiled(): mine = jnp.concatenate([mine, swap(mine, bit)], axis=0)]
    pallas_call x2 -> x3, Pallas kernels: 21.3 us -> 24.7 us  [attention_call(): pl.pallas_call(functools.partial(attention_kernel, len(bias_arrays), head...]
    pallas_call x6 -> x15, Pallas kernels: 1.08 us -> 4.16 us  [plain_call(): pl.pallas_call(kernel, in_specs=[vm] * len(operands), out_specs=[vm] * le...]
    pallas_call x1, Pallas kernels: 2.58 us -> 4.91 us  [output_call(): pl.pallas_call(functools.partial(output_kernel, parts), grid_spec=pltpu.P...]
    pallas_call x2, Pallas kernels: 9.13 us -> 11.1 us  [project_call(): pl.pallas_call(project_kernel, grid_spec=pltpu.PrefetchScalarGridSpec(num...]
    unnamed x60 -> x39, local copies, waits for them, and re-layouts: 7.17 us -> 6.37 us
  transfers between devices with their start and end apart: 23 -> 31, of which waited for: 13 -> 11; matrix products, arithmetic and copies ran while one was open for 5% -> 2% of each run, Pallas kernels for 28% -> 42%
where the time goes in v2:
time: 124 us
  Pallas kernels  52.4 us (42%)
  starting transfers between devices  31.5 us (25%)
  waiting for transfers between devices  30.4 us (25%)
  local copies, waits for them, and re-layouts  6.97 us (6%)
  other arithmetic  1.31 us (1%)
    ppermute x21, starting transfers between devices, swap(): return lax.ppermute(x, 'chip', [(c, c ^ bit) for c in range(chips)])  29.5 us
    ppermute x21, waiting for transfers between devices, swap(): return lax.ppermute(x, 'chip', [(c, c ^ bit) for c in range(chips)])  27.2 us
    pallas_call x3, Pallas kernels, attention_call(): pl.pallas_call(functools.partial(attention_kernel, len(bias_arrays), head...  24.7 us
    pallas_call x2, Pallas kernels, project_call(): pl.pallas_call(project_kernel, grid_spec=pltpu.PrefetchScalarGridSpec(num...  11.1 us
    unnamed x39, local copies, waits for them, and re-layouts  6.37 us
    pallas_call x1, Pallas kernels, output_call(): pl.pallas_call(functools.partial(output_kernel, parts), grid_spec=pltpu.P...  4.91 us
    pallas_call x15, Pallas kernels, plain_call(): pl.pallas_call(kernel, in_specs=[vm] * len(operands), out_specs=[vm] * le...  4.16 us
    pallas_call x2, Pallas kernels, final_call(): pl.pallas_call(functools.partial(kernel, parts), in_specs=[pl.BlockSpec(m...  3.85 us
  transfers between devices with their start and end apart: 31, of which 11 were waited for; matrix products, arithmetic and copies ran while one was open for 2% of the time, Pallas kernels for 42%

profile of v2, /device:TPU:0, one launch (start us, length us, event | category | flops | bytes accessed | tf_op | source)
XLA Modules:
  0.0 123.6 jit_solution(16063028903073651899)
XLA Ops:
  0.6 0.5 collective-permute-start.6
  1.2 0.8 copy.13.wt_ref.refs_8_
  2.0 1.7 %copy-done = bf16[24,384,128]{2,1,0:T(8,128)(2,1)S(1)} copy-done((bf16[24,384,128]{2,1,0:T(8,128)(2,1)S(1)}, bf16[24,384,128]{2,1,0:T(8,128)(2,1)}, u32[]{:S(2)}) %copy-start) | copy-done | bytes 2359320
  3.7 0.7 copy-done.8
  4.4 0.7 copy-done.9
  5.0 3.7 %pair_bias.1 = (bf16[8,24,384]{2,1,0:T(8,128)(2,1)S(1)}, bf16[8,24,384]{2,1,0:T(8,128)(2,1)S(1)}, f32[24,384]{1,0:T(8,128)S(1)}, f32[24,384]{1,0:T(8,128)S(1)}, f32[16,24,384]{2,1,0:T(8,128)S(1)}) custom-call(s32[1]{0:T(128)} %bitcast.1.core_ref, bf16[24,384,128]{2,1,0:T(8,128)(2,1)S(1)} %copy-done, f32[1,128]{1,0:T(1,128)S(1)} %bitcast.7, ...), custom_call_target="tpu_custom_call" | custom-call | flops 1000 | bytes 1000 | tf_op jit(solution)/shard_map/pair_bias/pallas_call | solution.py:147
  8.7 0.5 collective-permute-start
  9.2 1.0 collective-permute-done
  10.3 4.0 %collective-permute-start.11 = (bf16[1,3,48,384]{3,2,1,0:T(8,128)(2,1)S(1)}, bf16[1,3,48,384]{3,2,1,0:T(8,128)(2,1)S(1)}, u32[]{:S(2)}, u32[]{:S(2)}) collective-permute-start(bf16[1,3,48,384]{3,2,1,0:T(8,128)(2,1)S(1)} %get-tuple-element.121.refs_0_), channel_id=1, source_target_pairs={{0,8},{2,10},{4,12},{6,14},{8,0},{10,2},{12,4},{14,6},{1,9},{3,11}... | collective-permute-start | bytes 331784 | tf_op jit(solution)/shard_map/ppermute | solution.py:529
  14.4 8.5 %collective-permute-done.11.refs_1_ = bf16[1,3,48,384]{3,2,1,0:T(8,128)(2,1)S(1)} collective-permute-done((bf16[1,3,48,384]{3,2,1,0:T(8,128)(2,1)S(1)}, bf16[1,3,48,384]{3,2,1,0:T(8,128)(2,1)S(1)}, u32[]{:S(2)}, u32[]{:S(2)}) %collective-permute-start.11) | collective-permute-done | bytes 110624 | tf_op jit(solution)/shard_map/ppermute | solution.py:529
  23.3 0.6 reshape.14.mask_ref.refs_8_
  23.9 5.6 %projections.2 = (bf16[2,384,384]{2,1,0:T(8,128)(2,1)}, bf16[2,384,384]{2,1,0:T(8,128)(2,1)}, bf16[2,384,384]{2,1,0:T(8,128)(2,1)}, bf16[2,384,384]{2,1,0:T(8,128)(2,1)}) custom-call(s32[1]{0:T(128)} %bitcast.1.core_ref, bf16[2,384,768]{2,1,0:T(8,128)(2,1)} %act_ref.1, bf16[2,384,768]{2,1,0:T(8,128)(2,1)} %cot_ref.1, bf16[768,768]{1,0:T(8,128)(2,1)} %wq_ref.3, ...), custom_call_target="tpu_custom_call" | custom-call | flops 1000 | bytes 1000 | tf_op jit(solution)/shard_map/projections/pallas_call | solution.py:178
  29.4 1.8 %collective-permute-start.5 = (bf16[2,3,48,384]{3,2,1,0:T(8,128)(2,1)S(1)}, bf16[2,3,48,384]{3,2,1,0:T(8,128)(2,1)S(1)}, u32[]{:S(2)}, u32[]{:S(2)}) collective-permute-start(bf16[2,3,48,384]{3,2,1,0:T(8,128)(2,1)S(1)} %concat.8.refs_0_), channel_id=1, source_target_pairs={{0,4},{2,6},{4,0},{6,2},{8,12},{10,14},{12,8},{14,10},{1,5},{3,7},... | collective-permute-start | bytes 663560 | tf_op jit(solution)/shard_map/ppermute | solution.py:529
  31.3 1.9 %collective-permute-start.13 = (bf16[4,3,48,384]{3,2,1,0:T(8,128)(2,1)S(1)}, bf16[4,3,48,384]{3,2,1,0:T(8,128)(2,1)}, u32[]{:S(2)}, u32[]{:S(2)}) collective-permute-start(bf16[4,3,48,384]{3,2,1,0:T(8,128)(2,1)S(1)} %concat.11.refs_0_), channel_id=1, source_target_pairs={{0,2},{2,0},{4,6},{6,4},{8,10},{10,8},{12,14},{14,12},{1,3},{3,1},... | collective-permute-start | bytes 1327112 | tf_op jit(solution)/shard_map/ppermute | solution.py:529
  33.2 1.0 copy-done.11
  34.2 5.6 %projections.3 = (bf16[2,384,384]{2,1,0:T(8,128)(2,1)}, bf16[2,384,384]{2,1,0:T(8,128)(2,1)}, bf16[2,384,384]{2,1,0:T(8,128)(2,1)}, bf16[2,384,384]{2,1,0:T(8,128)(2,1)}) custom-call(s32[1]{0:T(128)} %bitcast.1.core_ref, bf16[2,384,768]{2,1,0:T(8,128)(2,1)} %copy-done.11, bf16[2,384,768]{2,1,0:T(8,128)(2,1)} %collective-permute-done.7.cot_ref, ...), custom_call_target="tpu_custom_call" | custom-call | flops 1000 | bytes 1000 | tf_op jit(solution)/shard_map/projections/pallas_call | solution.py:178
  40.1 1.8 %collective-permute-start.1 = (bf16[1,2,48,384]{3,2,1,0:T(8,128)(2,1)S(1)}, bf16[1,2,48,384]{3,2,1,0:T(8,128)(2,1)S(1)}, u32[]{:S(2)}, u32[]{:S(2)}) collective-permute-start(bf16[1,2,48,384]{3,2,1,0:T(8,128)(2,1)S(1)} %slice.12.refs_0_), channel_id=1, source_target_pairs={{0,8},{2,10},{4,12},{6,14},{8,0},{10,2},{12,4},{14,6},{1,9},{3,11}... | collective-permute-start | bytes 221192 | tf_op jit(solution)/shard_map/ppermute | solution.py:529
  41.9 4.3 %collective-permute-done.1.refs_1_ = bf16[1,2,48,384]{3,2,1,0:T(8,128)(2,1)S(1)} collective-permute-done((bf16[1,2,48,384]{3,2,1,0:T(8,128)(2,1)S(1)}, bf16[1,2,48,384]{3,2,1,0:T(8,128)(2,1)S(1)}, u32[]{:S(2)}, u32[]{:S(2)}) %collective-permute-start.1) | collective-permute-done | bytes 73760 | tf_op jit(solution)/shard_map/ppermute | solution.py:529
  46.2 1.8 %collective-permute-start.2 = (bf16[2,2,48,384]{3,2,1,0:T(8,128)(2,1)S(1)}, bf16[2,2,48,384]{3,2,1,0:T(8,128)(2,1)S(1)}, u32[]{:S(2)}, u32[]{:S(2)}) collective-permute-start(bf16[2,2,48,384]{3,2,1,0:T(8,128)(2,1)S(1)} %concat.6.refs_0_), channel_id=1, source_target_pairs={{0,2},{2,0},{4,6},{6,4},{8,10},{10,8},{12,14},{14,12},{1,3},{3,1},... | collective-permute-start | bytes 442376 | tf_op jit(solution)/shard_map/ppermute | solution.py:529
  48.0 0.7 pad_add_fusion.place_ref
  48.7 8.9 %attention.5 = (bf16[2,144,384]{2,1,0:T(8,128)(2,1)}, bf16[2,144,384]{2,1,0:T(8,128)(2,1)}, f32[4,3,48,384]{3,2,1,0:T(8,128)}, s16[4,160,384]{2,1,0:T(8,128)(2,1)}) custom-call(s32[2]{0:T(128)} %pad_add_fusion.place_ref, bf16[4,3,48,384]{3,2,1,0:T(8,128)(2,1)} %copy-done.2, bf16[4,3,48,384]{3,2,1,0:T(8,128)(2,1)} %collective-permute-done.13.refs_1_, ...), custom_call_target="tpu_custom_call" | custom-call | flops 1000 | bytes 1000 | tf_op jit(solution)/shard_map/attention/pallas_call | solution.py:285
  58.2 8.9 %attention.4 = (bf16[2,144,384]{2,1,0:T(8,128)(2,1)}, bf16[2,144,384]{2,1,0:T(8,128)(2,1)}, f32[4,3,48,384]{3,2,1,0:T(8,128)}, s16[4,160,384]{2,1,0:T(8,128)(2,1)}) custom-call(s32[2]{0:T(128)} %pad_add_fusion.place_ref, bf16[4,3,48,384]{3,2,1,0:T(8,128)(2,1)} %copy-done.3, bf16[4,3,48,384]{3,2,1,0:T(8,128)(2,1)} %collective-permute-done.10.refs_1_, ...), custom_call_target="tpu_custom_call" | custom-call | flops 1000 | bytes 1000 | tf_op jit(solution)/shard_map/attention/pallas_call | solution.py:285
  67.1 2.0 %collective-permute-start.17 = (s16[4,160,384]{2,1,0:T(8,128)(2,1)}, s16[4,160,384]{2,1,0:T(8,128)(2,1)S(1)}, u32[]{:S(2)}, u32[]{:S(2)}) collective-permute-start(s16[4,160,384]{2,1,0:T(8,128)(2,1)} %get-tuple-element.94), channel_id=1, source_target_pairs={{0,4},{2,6},{4,0},{6,2},{8,12},{10,14},{12,8},{14,10},{1,5},{3,7},... | collective-permute-start | bytes 1474568 | tf_op jit(solution)/shard_map/ppermute | solution.py:529
  69.2 0.7 copy-done.12
  69.9 6.8 %attention.3 = (bf16[2,96,384]{2,1,0:T(8,128)(2,1)}, bf16[2,96,384]{2,1,0:T(8,128)(2,1)}, f32[4,2,48,384]{3,2,1,0:T(8,128)}, s16[4,112,384]{2,1,0:T(8,128)(2,1)}) custom-call(s32[2]{0:T(128)} %pad_add_fusion.place_ref, bf16[4,2,48,384]{3,2,1,0:T(8,128)(2,1)} %copy-done.4, bf16[4,2,48,384]{3,2,1,0:T(8,128)(2,1)} %copy-done.12, ...), custom_call_target="tpu_custom_call" | custom-call | flops 1000 | bytes 1000 | tf_op jit(solution)/shard_map/attention/pallas_call | solution.py:285
  76.8 1.8 %collective-permute-start.8 = (s16[4,112,384]{2,1,0:T(8,128)(2,1)}, s16[4,112,384]{2,1,0:T(8,128)(2,1)S(1)}, u32[]{:S(2)}, u32[]{:S(2)}) collective-permute-start(s16[4,112,384]{2,1,0:T(8,128)(2,1)} %get-tuple-element.82), channel_id=1, source_target_pairs={{0,2},{2,0},{4,6},{6,4},{8,10},{10,8},{12,14},{14,12},{1,3},{3,1},... | collective-permute-start | bytes 1032200 | tf_op jit(solution)/shard_map/ppermute | solution.py:529
  79.3 2.5 %collective-permute-start.18 = (s16[2,160,384]{2,1,0:T(8,128)(2,1)S(1)}, s16[2,160,384]{2,1,0:T(8,128)(2,1)S(1)}, u32[]{:S(2)}, u32[]{:S(2)}) collective-permute-start(s16[2,160,384]{2,1,0:T(8,128)(2,1)S(1)} %get-tuple-element.96), channel_id=1, source_target_pairs={{0,2},{2,0},{4,6},{6,4},{8,10},{10,8},{12,14},{14,12},{1,3},{3,1},... | collective-permute-start | bytes 737288 | tf_op jit(solution)/shard_map/ppermute | solution.py:529
  82.4 2.4 %collective-permute-done.8.code_ref = s16[4,112,384]{2,1,0:T(8,128)(2,1)S(1)} collective-permute-done((s16[4,112,384]{2,1,0:T(8,128)(2,1)}, s16[4,112,384]{2,1,0:T(8,128)(2,1)S(1)}, u32[]{:S(2)}, u32[]{:S(2)}) %collective-permute-start.8) | collective-permute-done | bytes 344096 | tf_op jit(solution)/shard_map/ppermute | solution.py:529
  84.8 0.8 join.6
  85.7 1.7 %collective-permute-start.9 = (s16[2,112,384]{2,1,0:T(8,128)(2,1)}, s16[2,112,384]{2,1,0:T(8,128)(2,1)S(1)}, u32[]{:S(2)}, u32[]{:S(2)}) collective-permute-start(s16[2,112,384]{2,1,0:T(8,128)(2,1)} %get-tuple-element.83), channel_id=1, source_target_pairs={{0,4},{2,6},{4,0},{6,2},{8,12},{10,14},{12,8},{14,10},{1,5},{3,7},... | collective-permute-start | bytes 516104 | tf_op jit(solution)/shard_map/ppermute | solution.py:529
  87.4 0.8 join.10
  88.2 3.1 %collective-permute-start.22 = (s16[1,160,384]{2,1,0:T(8,128)(2,1)}, s16[1,160,384]{2,1,0:T(8,128)(2,1)S(1)}, u32[]{:S(2)}, u32[]{:S(2)}) collective-permute-start(s16[1,160,384]{2,1,0:T(8,128)(2,1)} %get-tuple-element.105), channel_id=1, source_target_pairs={{0,8},{2,10},{4,12},{6,14},{8,0},{10,2},{12,4},{14,6},{1,9},{3,11}... | collective-permute-start | bytes 368648 | tf_op jit(solution)/shard_map/ppermute | solution.py:529
  91.3 0.8 join.8
  92.1 0.6 copy-done.15
  92.9 4.9 %output.1 = bf16[2,384,768]{2,1,0:T(8,128)(2,1)} custom-call(s32[1]{0:T(128)} %bitcast.1.core_ref, bf16[2,144,384]{2,1,0:T(8,128)(2,1)} %get-tuple-element.85.refs_0_, bf16[2,144,384]{2,1,0:T(8,128)(2,1)} %get-tuple-element.86.refs_1_, bf16[2,96,384]{2,1,0:T(8,128)(2,1)} %get-tuple-element.87.refs_2_, bf16[2,144,384]{2,1,0:T(8,128)(2,1)} %copy-done.14, ...), custom_call_target="tpu_custom_call" | custom-call | flops 1000 | bytes 1000 | tf_op jit(solution)/shard_map/output/pallas_call | solution.py:416
  97.9 2.9 %collective-permute-start.23 = (s16[1,112,384]{2,1,0:T(8,128)(2,1)S(1)}, s16[1,112,384]{2,1,0:T(8,128)(2,1)S(1)}, u32[]{:S(2)}, u32[]{:S(2)}) collective-permute-start(s16[1,112,384]{2,1,0:T(8,128)(2,1)S(1)} %get-tuple-element.110), channel_id=1, source_target_pairs={{0,8},{2,10},{4,12},{6,14},{8,0},{10,2},{12,4},{14,6},{1,9},{3,11}... | collective-permute-start | bytes 258056 | tf_op jit(solution)/shard_map/ppermute | solution.py:529
  101.0 4.2 %collective-permute-done.19.code_ref = s16[1,160,384]{2,1,0:T(8,128)(2,1)} collective-permute-done((s16[1,160,384]{2,1,0:T(8,128)(2,1)}, s16[1,160,384]{2,1,0:T(8,128)(2,1)}, u32[]{:S(2)}, u32[]{:S(2)}) %collective-permute-start.19) | collective-permute-done | bytes 122912 | tf_op jit(solution)/shard_map/ppermute | solution.py:529
  105.1 0.9 last_join.3
  106.2 0.7 collective-permute-done.23.code_ref
  107.0 1.2 collective-permute-done.26.refs_5_
  108.2 0.7 pair_projection.1
  109.1 1.0 collective-permute-done.27
  110.1 1.5 %collective-permute-start.28 = (f32[16,128]{1,0:T(8,128)S(1)}, f32[16,128]{1,0:T(8,128)S(1)}, u32[]{:S(2)}, u32[]{:S(2)}) collective-permute-start(f32[16,128]{1,0:T(8,128)S(1)} %add.12), channel_id=1, source_target_pairs={{0,2},{2,0},{4,6},{6,4},{8,10},{10,8},{12,14},{14,12},{1,3},{3,1},... | collective-permute-start | bytes 24584 | tf_op jit(solution)/shard_map/ppermute | solution.py:529
  111.6 3.2 %pair_gradient.1 = bf16[24,384,128]{2,1,0:T(8,128)(2,1)} custom-call(s32[1]{0:T(128)} %bitcast.1.core_ref, f32[3,24,384]{2,1,0:T(8,128)S(1)} %get-tuple-element.99.refs_0_, f32[3,24,384]{2,1,0:T(8,128)S(1)} %get-tuple-element.106.refs_1_, f32[2,24,384]{2,1,0:T(8,128)S(1)} %get-tuple-element.111.refs_2_, f32[3,24,384]{2,1,0:T(8,128)S(1)} %collective-permute-done.24.refs_3_, ...), custom_call_target="tpu_custom_call" | custom-call | flops 1000 | bytes 1000 | tf_op jit(solution)/shard_map/pair_gradient/pallas_call | solution.py:502
  114.8 3.6 %collective-permute-done.29 = f32[16,128]{1,0:T(8,128)S(1)} collective-permute-done((f32[16,128]{1,0:T(8,128)S(1)}, f32[16,128]{1,0:T(8,128)S(1)}, u32[]{:S(2)}, u32[]{:S(2)}) %collective-permute-start.29) | collective-permute-done | bytes 8224 | tf_op jit(solution)/shard_map/ppermute | solution.py:529
  118.4 1.3 %collective-permute-start.30 = (f32[16,128]{1,0:T(8,128)S(1)}, f32[16,128]{1,0:T(8,128)S(1)}, u32[]{:S(2)}, u32[]{:S(2)}) collective-permute-start(f32[16,128]{1,0:T(8,128)S(1)} %add.14), channel_id=1, source_target_pairs={{0,8},{2,10},{4,12},{6,14},{8,0},{10,2},{12,4},{14,6},{1,9},{3,11}... | collective-permute-start | bytes 24584 | tf_op jit(solution)/shard_map/ppermute | solution.py:529
  119.7 3.3 %collective-permute-done.30 = f32[16,128]{1,0:T(8,128)S(1)} collective-permute-done((f32[16,128]{1,0:T(8,128)S(1)}, f32[16,128]{1,0:T(8,128)S(1)}, u32[]{:S(2)}, u32[]{:S(2)}) %collective-permute-start.30) | collective-permute-done | bytes 8224 | tf_op jit(solution)/shard_map/ppermute | solution.py:529
  123.0 0.6 add_bitcast_fusion
  (86 shorter events, 3.6 us)
Async XLA Ops:
  0.6 32.6 %collective-permute-start.6 = (bf16[2,384,768]{2,1,0:T(8,128)(2,1)}, bf16[2,384,768]{2,1,0:T(8,128)(2,1)S(1)}, u32[]{:S(2)}, u32[]{:S(2)}) collective-permute-start(bf16[2,384,768]{2,1,0:T(8,128)(2,1)} %act_ref.1), channel_id=1, source_target_pairs={{0,1},{1,0},{2,3},{3,2},{4,5},{5,4},{6,7},{7,6},{8,9},{9,8},{10,11... | collective-permute-start | bytes 3538952 | tf_op jit(solution)/shard_map/ppermute | solution.py:526
  1.1 32.1 %collective-permute-start.7 = (bf16[2,384,768]{2,1,0:T(8,128)(2,1)}, bf16[2,384,768]{2,1,0:T(8,128)(2,1)}, u32[]{:S(2)}, u32[]{:S(2)}) collective-permute-start(bf16[2,384,768]{2,1,0:T(8,128)(2,1)} %cot_ref.1), channel_id=1, source_target_pairs={{0,1},{1,0},{2,3},{3,2},{4,5},{5,4},{6,7},{7,6},{8,9},{9,8},{10,11... | collective-permute-start | bytes 3538952 | tf_op jit(solution)/shard_map/ppermute | solution.py:526
  2.0 1.7 %copy-start = (bf16[24,384,128]{2,1,0:T(8,128)(2,1)S(1)}, bf16[24,384,128]{2,1,0:T(8,128)(2,1)}, u32[]{:S(2)}) copy-start(bf16[24,384,128]{2,1,0:T(8,128)(2,1)} %refs_6_.5) | copy-start | bytes 7077892
  3.7 0.7 copy-start.8
  8.7 1.5 %collective-permute-start = (bf16[8,24,384]{2,1,0:T(8,128)(2,1)S(1)}, bf16[8,24,384]{2,1,0:T(8,128)(2,1)S(1)}, u32[]{:S(2)}, u32[]{:S(2)}) collective-permute-start(bf16[8,24,384]{2,1,0:T(8,128)(2,1)S(1)} %get-tuple-element.63), channel_id=1, source_target_pairs={{0,1},{1,0},{2,3},{3,2},{4,5},{5,4},{6,7},{7,6},{8,9},{9,8},{10,11... | collective-permute-start | bytes 442376 | tf_op jit(solution)/shard_map/ppermute | solution.py:526
  10.3 12.6 %collective-permute-start.11 = (bf16[1,3,48,384]{3,2,1,0:T(8,128)(2,1)S(1)}, bf16[1,3,48,384]{3,2,1,0:T(8,128)(2,1)S(1)}, u32[]{:S(2)}, u32[]{:S(2)}) collective-permute-start(bf16[1,3,48,384]{3,2,1,0:T(8,128)(2,1)S(1)} %get-tuple-element.121.refs_0_), channel_id=1, source_target_pairs={{0,8},{2,10},{4,12},{6,14},{8,0},{10,2},{12,4},{14,6},{1,9},{3,11}... | collective-permute-start | bytes 331784 | tf_op jit(solution)/shard_map/ppermute | solution.py:529
  14.3 15.1 %collective-permute-start.4 = (bf16[1,3,48,384]{3,2,1,0:T(8,128)(2,1)S(1)}, bf16[1,3,48,384]{3,2,1,0:T(8,128)(2,1)S(1)}, u32[]{:S(2)}, u32[]{:S(2)}) collective-permute-start(bf16[1,3,48,384]{3,2,1,0:T(8,128)(2,1)S(1)} %get-tuple-element.122.refs_0_), channel_id=1, source_target_pairs={{0,8},{2,10},{4,12},{6,14},{8,0},{10,2},{12,4},{14,6},{1,9},{3,11}... | collective-permute-start | bytes 331784 | tf_op jit(solution)/shard_map/ppermute | solution.py:529
  22.9 8.3 %collective-permute-start.12 = (bf16[2,3,48,384]{3,2,1,0:T(8,128)(2,1)S(1)}, bf16[2,3,48,384]{3,2,1,0:T(8,128)(2,1)S(1)}, u32[]{:S(2)}, u32[]{:S(2)}) collective-permute-start(bf16[2,3,48,384]{3,2,1,0:T(8,128)(2,1)S(1)} %concat.10.refs_0_), channel_id=1, source_target_pairs={{0,4},{2,6},{4,0},{6,2},{8,12},{10,14},{12,8},{14,10},{1,5},{3,7},... | collective-permute-start | bytes 663560 | tf_op jit(solution)/shard_map/ppermute | solution.py:529
  29.4 10.4 %collective-permute-start.5 = (bf16[2,3,48,384]{3,2,1,0:T(8,128)(2,1)S(1)}, bf16[2,3,48,384]{3,2,1,0:T(8,128)(2,1)S(1)}, u32[]{:S(2)}, u32[]{:S(2)}) collective-permute-start(bf16[2,3,48,384]{3,2,1,0:T(8,128)(2,1)S(1)} %concat.8.refs_0_), channel_id=1, source_target_pairs={{0,4},{2,6},{4,0},{6,2},{8,12},{10,14},{12,8},{14,10},{1,5},{3,7},... | collective-permute-start | bytes 663560 | tf_op jit(solution)/shard_map/ppermute | solution.py:529
  31.3 8.5 %copy-start.2 = (bf16[4,3,48,384]{3,2,1,0:T(8,128)(2,1)}, bf16[4,3,48,384]{3,2,1,0:T(8,128)(2,1)S(1)}, u32[]{:S(2)}) copy-start(bf16[4,3,48,384]{3,2,1,0:T(8,128)(2,1)S(1)} %concat.11.refs_0_) | copy-start | bytes 1327108
  31.3 17.4 %collective-permute-start.13 = (bf16[4,3,48,384]{3,2,1,0:T(8,128)(2,1)S(1)}, bf16[4,3,48,384]{3,2,1,0:T(8,128)(2,1)}, u32[]{:S(2)}, u32[]{:S(2)}) collective-permute-start(bf16[4,3,48,384]{3,2,1,0:T(8,128)(2,1)S(1)} %concat.11.refs_0_), channel_id=1, source_target_pairs={{0,2},{2,0},{4,6},{6,4},{8,10},{10,8},{12,14},{14,12},{1,3},{3,1},... | collective-permute-start | bytes 1327112 | tf_op jit(solution)/shard_map/ppermute | solution.py:529
  33.2 1.0 copy-start.11
  39.9 17.8 %copy-start.3 = (bf16[4,3,48,384]{3,2,1,0:T(8,128)(2,1)}, bf16[4,3,48,384]{3,2,1,0:T(8,128)(2,1)S(1)}, u32[]{:S(2)}) copy-start(bf16[4,3,48,384]{3,2,1,0:T(8,128)(2,1)S(1)} %concat.9.refs_0_) | copy-start | bytes 1327108
  39.9 18.3 %collective-permute-start.10 = (bf16[4,3,48,384]{3,2,1,0:T(8,128)(2,1)S(1)}, bf16[4,3,48,384]{3,2,1,0:T(8,128)(2,1)}, u32[]{:S(2)}, u32[]{:S(2)}) collective-permute-start(bf16[4,3,48,384]{3,2,1,0:T(8,128)(2,1)S(1)} %concat.9.refs_0_), channel_id=1, source_target_pairs={{0,2},{2,0},{4,6},{6,4},{8,10},{10,8},{12,14},{14,12},{1,3},{3,1},... | collective-permute-start | bytes 1327112 | tf_op jit(solution)/shard_map/ppermute | solution.py:529
  40.1 6.1 %collective-permute-start.1 = (bf16[1,2,48,384]{3,2,1,0:T(8,128)(2,1)S(1)}, bf16[1,2,48,384]{3,2,1,0:T(8,128)(2,1)S(1)}, u32[]{:S(2)}, u32[]{:S(2)}) collective-permute-start(bf16[1,2,48,384]{3,2,1,0:T(8,128)(2,1)S(1)} %slice.12.refs_0_), channel_id=1, source_target_pairs={{0,8},{2,10},{4,12},{6,14},{8,0},{10,2},{12,4},{14,6},{1,9},{3,11}... | collective-permute-start | bytes 221192 | tf_op jit(solution)/shard_map/ppermute | solution.py:529
  46.2 11.8 %collective-permute-start.2 = (bf16[2,2,48,384]{3,2,1,0:T(8,128)(2,1)S(1)}, bf16[2,2,48,384]{3,2,1,0:T(8,128)(2,1)S(1)}, u32[]{:S(2)}, u32[]{:S(2)}) collective-permute-start(bf16[2,2,48,384]{3,2,1,0:T(8,128)(2,1)S(1)} %concat.6.refs_0_), channel_id=1, source_target_pairs={{0,2},{2,0},{4,6},{6,4},{8,10},{10,8},{12,14},{14,12},{1,3},{3,1},... | collective-permute-start | bytes 442376 | tf_op jit(solution)/shard_map/ppermute | solution.py:529
  57.7 20.9 %collective-permute-start.20 = (s16[4,160,384]{2,1,0:T(8,128)(2,1)}, s16[4,160,384]{2,1,0:T(8,128)(2,1)S(1)}, u32[]{:S(2)}, u32[]{:S(2)}) collective-permute-start(s16[4,160,384]{2,1,0:T(8,128)(2,1)} %get-tuple-element.101), channel_id=1, source_target_pairs={{0,2},{2,0},{4,6},{6,4},{8,10},{10,8},{12,14},{14,12},{1,3},{3,1},... | collective-permute-start | bytes 1474568 | tf_op jit(solution)/shard_map/ppermute | solution.py:529
  58.1 9.1 %copy-start.4 = (bf16[4,2,48,384]{3,2,1,0:T(8,128)(2,1)}, bf16[4,2,48,384]{3,2,1,0:T(8,128)(2,1)S(1)}, u32[]{:S(2)}) copy-start(bf16[4,2,48,384]{3,2,1,0:T(8,128)(2,1)S(1)} %concat.7.refs_0_) | copy-start | bytes 884740
  58.1 11.1 %collective-permute-start.3 = (bf16[4,2,48,384]{3,2,1,0:T(8,128)(2,1)S(1)}, bf16[4,2,48,384]{3,2,1,0:T(8,128)(2,1)S(1)}, u32[]{:S(2)}, u32[]{:S(2)}) collective-permute-start(bf16[4,2,48,384]{3,2,1,0:T(8,128)(2,1)S(1)} %concat.7.refs_0_), channel_id=1, source_target_pairs={{0,4},{2,6},{4,0},{6,2},{8,12},{10,14},{12,8},{14,10},{1,5},{3,7},... | collective-permute-start | bytes 884744 | tf_op jit(solution)/shard_map/ppermute | solution.py:529
  67.1 11.4 %copy-start.5 = (f32[4,3,48,384]{3,2,1,0:T(8,128)S(1)}, f32[4,3,48,384]{3,2,1,0:T(8,128)}, u32[]{:S(2)}) copy-start(f32[4,3,48,384]{3,2,1,0:T(8,128)} %get-tuple-element.100.own_ref) | copy-start | bytes 2654212
  67.1 11.9 %collective-permute-start.17 = (s16[4,160,384]{2,1,0:T(8,128)(2,1)}, s16[4,160,384]{2,1,0:T(8,128)(2,1)S(1)}, u32[]{:S(2)}, u32[]{:S(2)}) collective-permute-start(s16[4,160,384]{2,1,0:T(8,128)(2,1)} %get-tuple-element.94), channel_id=1, source_target_pairs={{0,4},{2,6},{4,0},{6,2},{8,12},{10,14},{12,8},{14,10},{1,5},{3,7},... | collective-permute-start | bytes 1474568 | tf_op jit(solution)/shard_map/ppermute | solution.py:529
  69.2 0.7 copy-start.12
  76.7 2.3 %copy-start.6 = (f32[4,3,48,384]{3,2,1,0:T(8,128)S(1)}, f32[4,3,48,384]{3,2,1,0:T(8,128)}, u32[]{:S(2)}) copy-start(f32[4,3,48,384]{3,2,1,0:T(8,128)} %get-tuple-element.93.own_ref) | copy-start | bytes 2654212
  76.8 8.1 %collective-permute-start.8 = (s16[4,112,384]{2,1,0:T(8,128)(2,1)}, s16[4,112,384]{2,1,0:T(8,128)(2,1)S(1)}, u32[]{:S(2)}, u32[]{:S(2)}) collective-permute-start(s16[4,112,384]{2,1,0:T(8,128)(2,1)} %get-tuple-element.82), channel_id=1, source_target_pairs={{0,2},{2,0},{4,6},{6,4},{8,10},{10,8},{12,14},{14,12},{1,3},{3,1},... | collective-permute-start | bytes 1032200 | tf_op jit(solution)/shard_map/ppermute | solution.py:529
  78.6 3.3 %copy-start.16 = (bf16[2,144,384]{2,1,0:T(8,128)(2,1)S(1)}, bf16[2,144,384]{2,1,0:T(8,128)(2,1)}, u32[]{:S(2)}) copy-start(bf16[2,144,384]{2,1,0:T(8,128)(2,1)} %get-tuple-element.89) | copy-start | bytes 663556
  78.6 3.3 %copy-start.17 = (bf16[2,144,384]{2,1,0:T(8,128)(2,1)S(1)}, bf16[2,144,384]{2,1,0:T(8,128)(2,1)}, u32[]{:S(2)}) copy-start(bf16[2,144,384]{2,1,0:T(8,128)(2,1)} %get-tuple-element.88) | copy-start | bytes 663556
  78.6 6.2 %copy-start.18 = (bf16[2,96,384]{2,1,0:T(8,128)(2,1)S(1)}, bf16[2,96,384]{2,1,0:T(8,128)(2,1)}, u32[]{:S(2)}) copy-start(bf16[2,96,384]{2,1,0:T(8,128)(2,1)} %get-tuple-element.90) | copy-start | bytes 442372
  78.6 6.2 %copy-start.7 = (f32[4,2,48,384]{3,2,1,0:T(8,128)S(1)}, f32[4,2,48,384]{3,2,1,0:T(8,128)}, u32[]{:S(2)}) copy-start(f32[4,2,48,384]{3,2,1,0:T(8,128)} %get-tuple-element.81.own_ref) | copy-start | bytes 1769476
  78.8 6.8 %collective-permute-start.21 = (s16[2,160,384]{2,1,0:T(8,128)(2,1)S(1)}, s16[2,160,384]{2,1,0:T(8,128)(2,1)S(1)}, u32[]{:S(2)}, u32[]{:S(2)}) collective-permute-start(s16[2,160,384]{2,1,0:T(8,128)(2,1)S(1)} %get-tuple-element.103), channel_id=1, source_target_pairs={{0,4},{2,6},{4,0},{6,2},{8,12},{10,14},{12,8},{14,10},{1,5},{3,7},... | collective-permute-start | bytes 737288 | tf_op jit(solution)/shard_map/ppermute | solution.py:529
  79.3 8.9 %collective-permute-start.18 = (s16[2,160,384]{2,1,0:T(8,128)(2,1)S(1)}, s16[2,160,384]{2,1,0:T(8,128)(2,1)S(1)}, u32[]{:S(2)}, u32[]{:S(2)}) collective-permute-start(s16[2,160,384]{2,1,0:T(8,128)(2,1)S(1)} %get-tuple-element.96), channel_id=1, source_target_pairs={{0,2},{2,0},{4,6},{6,4},{8,10},{10,8},{12,14},{14,12},{1,3},{3,1},... | collective-permute-start | bytes 737288 | tf_op jit(solution)/shard_map/ppermute | solution.py:529
  81.9 10.2 %collective-permute-start.15 = (bf16[2,144,384]{2,1,0:T(8,128)(2,1)S(1)}, bf16[2,144,384]{2,1,0:T(8,128)(2,1)S(1)}, u32[]{:S(2)}, u32[]{:S(2)}) collective-permute-start(bf16[2,144,384]{2,1,0:T(8,128)(2,1)S(1)} %copy-done.16), channel_id=1, source_target_pairs={{0,1},{1,0},{2,3},{3,2},{4,5},{5,4},{6,7},{7,6},{8,9},{9,8},{10,11... | collective-permute-start | bytes 663560 | tf_op jit(solution)/shard_map/ppermute | solution.py:526
  81.9 10.2 %collective-permute-start.14 = (bf16[2,144,384]{2,1,0:T(8,128)(2,1)S(1)}, bf16[2,144,384]{2,1,0:T(8,128)(2,1)S(1)}, u32[]{:S(2)}, u32[]{:S(2)}) collective-permute-start(bf16[2,144,384]{2,1,0:T(8,128)(2,1)S(1)} %copy-done.17), channel_id=1, source_target_pairs={{0,1},{1,0},{2,3},{3,2},{4,5},{5,4},{6,7},{7,6},{8,9},{9,8},{10,11... | collective-permute-start | bytes 663560 | tf_op jit(solution)/shard_map/ppermute | solution.py:526
  84.8 7.2 %collective-permute-start.16 = (bf16[2,96,384]{2,1,0:T(8,128)(2,1)S(1)}, bf16[2,96,384]{2,1,0:T(8,128)(2,1)S(1)}, u32[]{:S(2)}, u32[]{:S(2)}) collective-permute-start(bf16[2,96,384]{2,1,0:T(8,128)(2,1)S(1)} %copy-done.18), channel_id=1, source_target_pairs={{0,1},{1,0},{2,3},{3,2},{4,5},{5,4},{6,7},{7,6},{8,9},{9,8},{10,11... | collective-permute-start | bytes 442376 | tf_op jit(solution)/shard_map/ppermute | solution.py:526
  85.7 12.1 %collective-permute-start.9 = (s16[2,112,384]{2,1,0:T(8,128)(2,1)}, s16[2,112,384]{2,1,0:T(8,128)(2,1)S(1)}, u32[]{:S(2)}, u32[]{:S(2)}) collective-permute-start(s16[2,112,384]{2,1,0:T(8,128)(2,1)} %get-tuple-element.83), channel_id=1, source_target_pairs={{0,4},{2,6},{4,0},{6,2},{8,12},{10,14},{12,8},{14,10},{1,5},{3,7},... | collective-permute-start | bytes 516104 | tf_op jit(solution)/shard_map/ppermute | solution.py:529
  88.2 12.7 %collective-permute-start.22 = (s16[1,160,384]{2,1,0:T(8,128)(2,1)}, s16[1,160,384]{2,1,0:T(8,128)(2,1)S(1)}, u32[]{:S(2)}, u32[]{:S(2)}) collective-permute-start(s16[1,160,384]{2,1,0:T(8,128)(2,1)} %get-tuple-element.105), channel_id=1, source_target_pairs={{0,8},{2,10},{4,12},{6,14},{8,0},{10,2},{12,4},{14,6},{1,9},{3,11}... | collective-permute-start | bytes 368648 | tf_op jit(solution)/shard_map/ppermute | solution.py:529
  92.1 13.1 %collective-permute-start.19 = (s16[1,160,384]{2,1,0:T(8,128)(2,1)}, s16[1,160,384]{2,1,0:T(8,128)(2,1)}, u32[]{:S(2)}, u32[]{:S(2)}) collective-permute-start(s16[1,160,384]{2,1,0:T(8,128)(2,1)} %get-tuple-element.98), channel_id=1, source_target_pairs={{0,8},{2,10},{4,12},{6,14},{8,0},{10,2},{12,4},{14,6},{1,9},{3,11}... | collective-permute-start | bytes 368648 | tf_op jit(solution)/shard_map/ppermute | solution.py:529
  92.1 0.7 copy-start.13
  92.1 0.8 copy-start.14
  92.9 15.3 %copy-start.1 = (bf16[24,384,128]{2,1,0:T(8,128)(2,1)S(1)}, bf16[24,384,128]{2,1,0:T(8,128)(2,1)}, u32[]{:S(2)}) copy-start(bf16[24,384,128]{2,1,0:T(8,128)(2,1)} %refs_6_.5) | copy-start | bytes 7077892
  97.8 10.4 %copy-start.10 = (f32[128]{0:T(128)S(1)}, f32[128]{0:T(128)}, u32[]{:S(2)}) copy-start(f32[128]{0:T(128)} %param.13) | copy-start | bytes 1540
  97.9 8.9 %collective-permute-start.23 = (s16[1,112,384]{2,1,0:T(8,128)(2,1)S(1)}, s16[1,112,384]{2,1,0:T(8,128)(2,1)S(1)}, u32[]{:S(2)}, u32[]{:S(2)}) collective-permute-start(s16[1,112,384]{2,1,0:T(8,128)(2,1)S(1)} %get-tuple-element.110), channel_id=1, source_target_pairs={{0,8},{2,10},{4,12},{6,14},{8,0},{10,2},{12,4},{14,6},{1,9},{3,11}... | collective-permute-start | bytes 258056 | tf_op jit(solution)/shard_map/ppermute | solution.py:529
  100.9 7.3 %collective-permute-start.25 = (f32[3,24,384]{2,1,0:T(8,128)S(1)}, f32[3,24,384]{2,1,0:T(8,128)S(1)}, u32[]{:S(2)}, u32[]{:S(2)}) collective-permute-start(f32[3,24,384]{2,1,0:T(8,128)S(1)} %get-tuple-element.113), channel_id=1, source_target_pairs={{0,1},{1,0},{2,3},{3,2},{4,5},{5,4},{6,7},{7,6},{8,9},{9,8},{10,11... | collective-permute-start | bytes 331784 | tf_op jit(solution)/shard_map/ppermute | solution.py:526
  106.1 2.1 %collective-permute-start.24 = (f32[3,24,384]{2,1,0:T(8,128)S(1)}, f32[3,24,384]{2,1,0:T(8,128)S(1)}, u32[]{:S(2)}, u32[]{:S(2)}) collective-permute-start(f32[3,24,384]{2,1,0:T(8,128)S(1)} %get-tuple-element.112), channel_id=1, source_target_pairs={{0,1},{1,0},{2,3},{3,2},{4,5},{5,4},{6,7},{7,6},{8,9},{9,8},{10,11... | collective-permute-start | bytes 331784 | tf_op jit(solution)/shard_map/ppermute | solution.py:526
  106.8 1.3 %collective-permute-start.26 = (f32[2,24,384]{2,1,0:T(8,128)S(1)}, f32[2,24,384]{2,1,0:T(8,128)S(1)}, u32[]{:S(2)}, u32[]{:S(2)}) collective-permute-start(f32[2,24,384]{2,1,0:T(8,128)S(1)} %get-tuple-element.114), channel_id=1, source_target_pairs={{0,1},{1,0},{2,3},{3,2},{4,5},{5,4},{6,7},{7,6},{8,9},{9,8},{10,11... | collective-permute-start | bytes 221192 | tf_op jit(solution)/shard_map/ppermute | solution.py:526
  108.9 1.2 collective-permute-start.27
  110.1 4.7 %collective-permute-start.28 = (f32[16,128]{1,0:T(8,128)S(1)}, f32[16,128]{1,0:T(8,128)S(1)}, u32[]{:S(2)}, u32[]{:S(2)}) collective-permute-start(f32[16,128]{1,0:T(8,128)S(1)} %add.12), channel_id=1, source_target_pairs={{0,2},{2,0},{4,6},{6,4},{8,10},{10,8},{12,14},{14,12},{1,3},{3,1},... | collective-permute-start | bytes 24584 | tf_op jit(solution)/shard_map/ppermute | solution.py:529
  114.8 3.7 %collective-permute-start.29 = (f32[16,128]{1,0:T(8,128)S(1)}, f32[16,128]{1,0:T(8,128)S(1)}, u32[]{:S(2)}, u32[]{:S(2)}) collective-permute-start(f32[16,128]{1,0:T(8,128)S(1)} %add.13), channel_id=1, source_target_pairs={{0,4},{2,6},{4,0},{6,2},{8,12},{10,14},{12,8},{14,10},{1,5},{3,7},... | collective-permute-start | bytes 24584 | tf_op jit(solution)/shard_map/ppermute | solution.py:529
  118.4 4.5 %collective-permute-start.30 = (f32[16,128]{1,0:T(8,128)S(1)}, f32[16,128]{1,0:T(8,128)S(1)}, u32[]{:S(2)}, u32[]{:S(2)}) collective-permute-start(f32[16,128]{1,0:T(8,128)S(1)} %add.14), channel_id=1, source_target_pairs={{0,8},{2,10},{4,12},{6,14},{8,0},{10,2},{12,4},{14,6},{1,9},{3,11}... | collective-permute-start | bytes 24584 | tf_op jit(solution)/shard_map/ppermute | solution.py:529
  (2 other events, 1.3 us)

commit v3 on v2

--- a/solution.py
+++ b/solution.py
@@ -18,7 +18,7 @@
 VMEM_LIMIT = 48 * 1024 * 1024
 VMEM_WIDE = 60 * 1024 * 1024
 CHUNKS = (3, 3, 2)
-GATHER_OTHER = (2,)
+GATHER_OTHER = ()
 SCATTER_OTHER = (0,)
 EARLY = 9
 LATE = False
@@ -595,10 +595,10 @@
     attended = output_call(core_1, mixed_own, mixed_other, w_out, mask_row)
     for n in range(count):
         while level_of[n] < levels - 1:
-            if n == count - 1 and level_of[n] == 1:
-                far[n], attended = tie((far[n], attended))
             codes = join(n)
             far[n] = swap(codes, scatter_bits[n][level_of[n]])
+    far, attended = tie((far, attended))
+    for n in range(count):
         here, there = total_call(stays[n], far[n])
         grads_own.append(here)
         grads_other.append(swap_core(there))

time: 124 us -> 129 us (1.040)
  waiting for transfers between devices: 30.4 us -> 37.6 us
  Pallas kernels: 52.4 us -> 50.8 us
    ppermute x21, waiting for transfers between devices: 27.2 us -> 34.3 us  [swap(): return lax.ppermute(x, 'chip', [(c, c ^ bit) for c in range(chips)])]
    pallas_call x15, Pallas kernels: 4.16 us -> 2.59 us  [plain_call(): pl.pallas_call(kernel, in_specs=[vm] * len(operands), out_specs=[vm] * le...]
    ppermute x21, starting transfers between devices: 29.5 us -> 28.1 us  [swap(): return lax.ppermute(x, 'chip', [(c, c ^ bit) for c in range(chips)])]
    unnamed x39 -> x41, local copies, waits for them, and re-layouts: 6.37 us -> 6.92 us
  transfers between devices with their start and end apart: 31 -> 31, of which waited for: 11 -> 11; matrix products, arithmetic and copies ran while one was open for 2% -> 2% of each run, Pallas kernels for 42% -> 39%
where the time goes in v3:
time: 129 us
  Pallas kernels  50.8 us (39%)
  waiting for transfers between devices  37.6 us (29%)
  starting transfers between devices  30.8 us (24%)
  local copies, waits for them, and re-layouts  7.52 us (6%)
    ppermute x21, waiting for transfers between devices, swap(): return lax.ppermute(x, 'chip', [(c, c ^ bit) for c in range(chips)])  34.3 us
    ppermute x21, starting transfers between devices, swap(): return lax.ppermute(x, 'chip', [(c, c ^ bit) for c in range(chips)])  28.1 us
    pallas_call x3, Pallas kernels, attention_call(): pl.pallas_call(functools.partial(attention_kernel, len(bias_arrays), head...  24.7 us
    pallas_call x2, Pallas kernels, project_call(): pl.pallas_call(project_kernel, grid_spec=pltpu.PrefetchScalarGridSpec(num...  11.1 us
    unnamed x41, local copies, waits for them, and re-layouts  6.92 us
    pallas_call x1, Pallas kernels, output_call(): pl.pallas_call(functools.partial(output_kernel, parts), grid_spec=pltpu.P...  4.91 us
    pallas_call x2, Pallas kernels, final_call(): pl.pallas_call(functools.partial(kernel, parts), in_specs=[pl.BlockSpec(m...  3.86 us
    pallas_call x1, Pallas kernels, bias_call(): pl.pallas_call(bias_kernel, out_shape=[jax.ShapeDtypeStruct((half, rows,...  3.67 us
  transfers between devices with their start and end apart: 31, of which 11 were waited for; matrix products, arithmetic and copies ran while one was open for 2% of the time, Pallas kernels for 39%

profile of v3, /device:TPU:0, one launch (start us, length us, event | category | flops | bytes accessed | tf_op | source)
XLA Modules:
  0.0 128.9 jit_solution(7964329108850395443)
XLA Ops:
  0.6 0.5 collective-permute-start.3
  1.2 0.8 copy.13.wt_ref.refs_8_
  2.0 1.7 %copy-done = bf16[24,384,128]{2,1,0:T(8,128)(2,1)S(1)} copy-done((bf16[24,384,128]{2,1,0:T(8,128)(2,1)S(1)}, bf16[24,384,128]{2,1,0:T(8,128)(2,1)}, u32[]{:S(2)}) %copy-start) | copy-done | bytes 2359320
  3.7 0.7 copy-done.8
  4.4 0.7 copy-done.9
  5.0 3.7 %pair_bias.1 = (bf16[8,24,384]{2,1,0:T(8,128)(2,1)S(1)}, bf16[8,24,384]{2,1,0:T(8,128)(2,1)S(1)}, f32[24,384]{1,0:T(8,128)S(1)}, f32[24,384]{1,0:T(8,128)S(1)}, f32[16,24,384]{2,1,0:T(8,128)S(1)}) custom-call(s32[1]{0:T(128)} %bitcast.1.core_ref, bf16[24,384,128]{2,1,0:T(8,128)(2,1)S(1)} %copy-done, f32[1,128]{1,0:T(1,128)S(1)} %bitcast.7, ...), custom_call_target="tpu_custom_call" | custom-call | flops 1000 | bytes 1000 | tf_op jit(solution)/shard_map/pair_bias/pallas_call | solution.py:147
  9.2 1.0 collective-permute-done
  10.3 4.0 %collective-permute-start.9 = (bf16[1,3,48,384]{3,2,1,0:T(8,128)(2,1)S(1)}, bf16[1,3,48,384]{3,2,1,0:T(8,128)(2,1)S(1)}, u32[]{:S(2)}, u32[]{:S(2)}) collective-permute-start(bf16[1,3,48,384]{3,2,1,0:T(8,128)(2,1)S(1)} %get-tuple-element.125.refs_0_), channel_id=1, source_target_pairs={{0,8},{2,10},{4,12},{6,14},{8,0},{10,2},{12,4},{14,6},{1,9},{3,11}... | collective-permute-start | bytes 331784 | tf_op jit(solution)/shard_map/ppermute | solution.py:529
  14.4 8.5 %collective-permute-done.9.refs_1_ = bf16[1,3,48,384]{3,2,1,0:T(8,128)(2,1)S(1)} collective-permute-done((bf16[1,3,48,384]{3,2,1,0:T(8,128)(2,1)S(1)}, bf16[1,3,48,384]{3,2,1,0:T(8,128)(2,1)S(1)}, u32[]{:S(2)}, u32[]{:S(2)}) %collective-permute-start.9) | collective-permute-done | bytes 110624 | tf_op jit(solution)/shard_map/ppermute | solution.py:529
  23.3 0.6 reshape.14.mask_ref.refs_8_
  23.9 5.6 %projections.2 = (bf16[2,384,384]{2,1,0:T(8,128)(2,1)}, bf16[2,384,384]{2,1,0:T(8,128)(2,1)}, bf16[2,384,384]{2,1,0:T(8,128)(2,1)}, bf16[2,384,384]{2,1,0:T(8,128)(2,1)}) custom-call(s32[1]{0:T(128)} %bitcast.1.core_ref, bf16[2,384,768]{2,1,0:T(8,128)(2,1)} %act_ref.1, bf16[2,384,768]{2,1,0:T(8,128)(2,1)} %cot_ref.1, bf16[768,768]{1,0:T(8,128)(2,1)} %wq_ref.3, ...), custom_call_target="tpu_custom_call" | custom-call | flops 1000 | bytes 1000 | tf_op jit(solution)/shard_map/projections/pallas_call | solution.py:178
  29.5 1.8 %collective-permute-start.2 = (bf16[2,3,48,384]{3,2,1,0:T(8,128)(2,1)S(1)}, bf16[2,3,48,384]{3,2,1,0:T(8,128)(2,1)S(1)}, u32[]{:S(2)}, u32[]{:S(2)}) collective-permute-start(bf16[2,3,48,384]{3,2,1,0:T(8,128)(2,1)S(1)} %concat.6.refs_0_), channel_id=1, source_target_pairs={{0,4},{2,6},{4,0},{6,2},{8,12},{10,14},{12,8},{14,10},{1,5},{3,7},... | collective-permute-start | bytes 663560 | tf_op jit(solution)/shard_map/ppermute | solution.py:529
  31.3 1.9 %collective-permute-start.11 = (bf16[4,3,48,384]{3,2,1,0:T(8,128)(2,1)S(1)}, bf16[4,3,48,384]{3,2,1,0:T(8,128)(2,1)S(1)}, u32[]{:S(2)}, u32[]{:S(2)}) collective-permute-start(bf16[4,3,48,384]{3,2,1,0:T(8,128)(2,1)S(1)} %concat.9.refs_0_), channel_id=1, source_target_pairs={{0,2},{2,0},{4,6},{6,4},{8,10},{10,8},{12,14},{14,12},{1,3},{3,1},... | collective-permute-start | bytes 1327112 | tf_op jit(solution)/shard_map/ppermute | solution.py:529
  33.2 5.6 %projections.3 = (bf16[2,384,384]{2,1,0:T(8,128)(2,1)}, bf16[2,384,384]{2,1,0:T(8,128)(2,1)}, bf16[2,384,384]{2,1,0:T(8,128)(2,1)}, bf16[2,384,384]{2,1,0:T(8,128)(2,1)}) custom-call(s32[1]{0:T(128)} %bitcast.1.core_ref, bf16[2,384,768]{2,1,0:T(8,128)(2,1)} %collective-permute-done.3.act_ref, bf16[2,384,768]{2,1,0:T(8,128)(2,1)} %collective-permute-done.4.cot_ref, ...), custom_call_target="tpu_custom_call" | custom-call | flops 1000 | bytes 1000 | tf_op jit(solution)/shard_map/projections/pallas_call | solution.py:178
  39.1 2.5 %collective-permute-start.15 = (bf16[1,2,48,384]{3,2,1,0:T(8,128)(2,1)S(1)}, bf16[1,2,48,384]{3,2,1,0:T(8,128)(2,1)S(1)}, u32[]{:S(2)}, u32[]{:S(2)}) collective-permute-start(bf16[1,2,48,384]{3,2,1,0:T(8,128)(2,1)S(1)} %slice.14.refs_0_), channel_id=1, source_target_pairs={{0,8},{2,10},{4,12},{6,14},{8,0},{10,2},{12,4},{14,6},{1,9},{3,11}... | collective-permute-start | bytes 221192 | tf_op jit(solution)/shard_map/ppermute | solution.py:529
  41.6 3.7 %collective-permute-done.15.refs_1_ = bf16[1,2,48,384]{3,2,1,0:T(8,128)(2,1)S(1)} collective-permute-done((bf16[1,2,48,384]{3,2,1,0:T(8,128)(2,1)S(1)}, bf16[1,2,48,384]{3,2,1,0:T(8,128)(2,1)S(1)}, u32[]{:S(2)}, u32[]{:S(2)}) %collective-permute-start.15) | collective-permute-done | bytes 73760 | tf_op jit(solution)/shard_map/ppermute | solution.py:529
  45.6 0.6 pad_add_fusion.place_ref
  46.3 0.8 copy-done.11
  47.0 8.9 %attention.4 = (bf16[2,144,384]{2,1,0:T(8,128)(2,1)}, bf16[2,144,384]{2,1,0:T(8,128)(2,1)}, f32[4,3,48,384]{3,2,1,0:T(8,128)}, s16[4,160,384]{2,1,0:T(8,128)(2,1)}) custom-call(s32[2]{0:T(128)} %pad_add_fusion.place_ref, bf16[4,3,48,384]{3,2,1,0:T(8,128)(2,1)} %copy-done.2, bf16[4,3,48,384]{3,2,1,0:T(8,128)(2,1)} %copy-done.11, ...), custom_call_target="tpu_custom_call" | custom-call | flops 1000 | bytes 1000 | tf_op jit(solution)/shard_map/attention/pallas_call | solution.py:285
  56.0 1.6 %collective-permute-start.12 = (s16[4,160,384]{2,1,0:T(8,128)(2,1)}, s16[4,160,384]{2,1,0:T(8,128)(2,1)S(1)}, u32[]{:S(2)}, u32[]{:S(2)}) collective-permute-start(s16[4,160,384]{2,1,0:T(8,128)(2,1)} %get-tuple-element.90), channel_id=1, source_target_pairs={{0,2},{2,0},{4,6},{6,4},{8,10},{10,8},{12,14},{14,12},{1,3},{3,1},... | collective-permute-start | bytes 1474568 | tf_op jit(solution)/shard_map/ppermute | solution.py:529
  57.6 0.6 collective-permute-start.17
  58.2 0.8 copy-done.12
  59.0 8.9 %attention.3 = (bf16[2,144,384]{2,1,0:T(8,128)(2,1)}, bf16[2,144,384]{2,1,0:T(8,128)(2,1)}, f32[4,3,48,384]{3,2,1,0:T(8,128)}, s16[4,160,384]{2,1,0:T(8,128)(2,1)}) custom-call(s32[2]{0:T(128)} %pad_add_fusion.place_ref, bf16[4,3,48,384]{3,2,1,0:T(8,128)(2,1)} %copy-done.3, bf16[4,3,48,384]{3,2,1,0:T(8,128)(2,1)} %copy-done.12, ...), custom_call_target="tpu_custom_call" | custom-call | flops 1000 | bytes 1000 | tf_op jit(solution)/shard_map/attention/pallas_call | solution.py:285
  67.9 1.8 %collective-permute-start.6 = (s16[4,160,384]{2,1,0:T(8,128)(2,1)}, s16[4,160,384]{2,1,0:T(8,128)(2,1)S(1)}, u32[]{:S(2)}, u32[]{:S(2)}) collective-permute-start(s16[4,160,384]{2,1,0:T(8,128)(2,1)} %get-tuple-element.85), channel_id=1, source_target_pairs={{0,4},{2,6},{4,0},{6,2},{8,12},{10,14},{12,8},{14,10},{1,5},{3,7},... | collective-permute-start | bytes 1474568 | tf_op jit(solution)/shard_map/ppermute | solution.py:529
  69.8 3.5 %collective-permute-done.17.refs_1_ = bf16[4,2,48,384]{3,2,1,0:T(8,128)(2,1)S(1)} collective-permute-done((bf16[4,2,48,384]{3,2,1,0:T(8,128)(2,1)S(1)}, bf16[4,2,48,384]{3,2,1,0:T(8,128)(2,1)S(1)}, u32[]{:S(2)}, u32[]{:S(2)}) %collective-permute-start.17) | collective-permute-done | bytes 294944 | tf_op jit(solution)/shard_map/ppermute | solution.py:529
  73.3 0.7 copy-done.13
  74.0 6.8 %attention.5 = (bf16[2,96,384]{2,1,0:T(8,128)(2,1)}, bf16[2,96,384]{2,1,0:T(8,128)(2,1)}, f32[4,2,48,384]{3,2,1,0:T(8,128)}, s16[4,112,384]{2,1,0:T(8,128)(2,1)}) custom-call(s32[2]{0:T(128)} %pad_add_fusion.place_ref, bf16[4,2,48,384]{3,2,1,0:T(8,128)(2,1)} %copy-done.4, bf16[4,2,48,384]{3,2,1,0:T(8,128)(2,1)} %copy-done.13, ...), custom_call_target="tpu_custom_call" | custom-call | flops 1000 | bytes 1000 | tf_op jit(solution)/shard_map/attention/pallas_call | solution.py:285
  80.9 1.5 %collective-permute-start.18 = (s16[4,112,384]{2,1,0:T(8,128)(2,1)}, s16[4,112,384]{2,1,0:T(8,128)(2,1)S(1)}, u32[]{:S(2)}, u32[]{:S(2)}) collective-permute-start(s16[4,112,384]{2,1,0:T(8,128)(2,1)} %get-tuple-element.95), channel_id=1, source_target_pairs={{0,2},{2,0},{4,6},{6,4},{8,10},{10,8},{12,14},{14,12},{1,3},{3,1},... | collective-permute-start | bytes 1032200 | tf_op jit(solution)/shard_map/ppermute | solution.py:529
  83.2 0.7 collective-permute-start.7
  83.9 6.4 %collective-permute-done.18.code_ref = s16[4,112,384]{2,1,0:T(8,128)(2,1)S(1)} collective-permute-done((s16[4,112,384]{2,1,0:T(8,128)(2,1)}, s16[4,112,384]{2,1,0:T(8,128)(2,1)S(1)}, u32[]{:S(2)}, u32[]{:S(2)}) %collective-permute-start.18) | collective-permute-done | bytes 344096 | tf_op jit(solution)/shard_map/ppermute | solution.py:529
  91.3 0.8 join.9
  92.1 0.9 collective-permute-done.7.code_ref
  93.0 2.9 %collective-permute-start.14 = (s16[1,160,384]{2,1,0:T(8,128)(2,1)}, s16[1,160,384]{2,1,0:T(8,128)(2,1)S(1)}, u32[]{:S(2)}, u32[]{:S(2)}) collective-permute-start(s16[1,160,384]{2,1,0:T(8,128)(2,1)} %get-tuple-element.93), channel_id=1, source_target_pairs={{0,8},{2,10},{4,12},{6,14},{8,0},{10,2},{12,4},{14,6},{1,9},{3,11}... | collective-permute-start | bytes 368648 | tf_op jit(solution)/shard_map/ppermute | solution.py:529
  95.8 0.8 join.7
  96.6 2.7 %collective-permute-start.8 = (s16[1,160,384]{2,1,0:T(8,128)(2,1)}, s16[1,160,384]{2,1,0:T(8,128)(2,1)S(1)}, u32[]{:S(2)}, u32[]{:S(2)}) collective-permute-start(s16[1,160,384]{2,1,0:T(8,128)(2,1)} %get-tuple-element.88), channel_id=1, source_target_pairs={{0,8},{2,10},{4,12},{6,14},{8,0},{10,2},{12,4},{14,6},{1,9},{3,11}... | collective-permute-start | bytes 368648 | tf_op jit(solution)/shard_map/ppermute | solution.py:529
  100.5 4.9 %output.1 = bf16[2,384,768]{2,1,0:T(8,128)(2,1)} custom-call(s32[1]{0:T(128)} %bitcast.1.core_ref, bf16[2,144,384]{2,1,0:T(8,128)(2,1)} %get-tuple-element.99.refs_0_, bf16[2,144,384]{2,1,0:T(8,128)(2,1)} %get-tuple-element.100.refs_1_, bf16[2,96,384]{2,1,0:T(8,128)(2,1)} %get-tuple-element.101.refs_2_, bf16[2,144,384]{2,1,0:T(8,128)(2,1)} %copy-done.15, ...), custom_call_target="tpu_custom_call" | custom-call | flops 1000 | bytes 1000 | tf_op jit(solution)/shard_map/output/pallas_call | solution.py:416
  105.4 5.8 %collective-permute-done.20.code_ref = s16[1,112,384]{2,1,0:T(8,128)(2,1)S(1)} collective-permute-done((s16[1,112,384]{2,1,0:T(8,128)(2,1)S(1)}, s16[1,112,384]{2,1,0:T(8,128)(2,1)S(1)}, u32[]{:S(2)}, u32[]{:S(2)}) %collective-permute-start.20) | collective-permute-done | bytes 86048 | tf_op jit(solution)/shard_map/ppermute | solution.py:529
  111.3 0.6 collective-permute-start.25
  112.0 1.2 collective-permute-done.26.refs_5_
  113.3 0.7 pair_projection.1
  114.1 1.0 collective-permute-done.27
  115.2 1.7 %collective-permute-start.28 = (f32[16,128]{1,0:T(8,128)S(1)}, f32[16,128]{1,0:T(8,128)S(1)}, u32[]{:S(2)}, u32[]{:S(2)}) collective-permute-start(f32[16,128]{1,0:T(8,128)S(1)} %add.12), channel_id=1, source_target_pairs={{0,2},{2,0},{4,6},{6,4},{8,10},{10,8},{12,14},{14,12},{1,3},{3,1},... | collective-permute-start | bytes 24584 | tf_op jit(solution)/shard_map/ppermute | solution.py:529
  116.9 3.2 %pair_gradient.1 = bf16[24,384,128]{2,1,0:T(8,128)(2,1)} custom-call(s32[1]{0:T(128)} %bitcast.1.core_ref, f32[3,24,384]{2,1,0:T(8,128)S(1)} %get-tuple-element.109.refs_0_, f32[3,24,384]{2,1,0:T(8,128)S(1)} %get-tuple-element.112.refs_1_, f32[2,24,384]{2,1,0:T(8,128)S(1)} %get-tuple-element.115.refs_2_, f32[3,24,384]{2,1,0:T(8,128)S(1)} %collective-permute-done.24.refs_3_, ...), custom_call_target="tpu_custom_call" | custom-call | flops 1000 | bytes 1000 | tf_op jit(solution)/shard_map/pair_gradient/pallas_call | solution.py:502
  120.1 0.7 collective-permute-start.29
  120.8 3.0 %collective-permute-done.29 = f32[16,128]{1,0:T(8,128)S(1)} collective-permute-done((f32[16,128]{1,0:T(8,128)S(1)}, f32[16,128]{1,0:T(8,128)S(1)}, u32[]{:S(2)}, u32[]{:S(2)}) %collective-permute-start.29) | collective-permute-done | bytes 8224 | tf_op jit(solution)/shard_map/ppermute | solution.py:529
  123.7 2.0 %collective-permute-start.30 = (f32[16,128]{1,0:T(8,128)S(1)}, f32[16,128]{1,0:T(8,128)S(1)}, u32[]{:S(2)}, u32[]{:S(2)}) collective-permute-start(f32[16,128]{1,0:T(8,128)S(1)} %add.14), channel_id=1, source_target_pairs={{0,8},{2,10},{4,12},{6,14},{8,0},{10,2},{12,4},{14,6},{1,9},{3,11}... | collective-permute-start | bytes 24584 | tf_op jit(solution)/shard_map/ppermute | solution.py:529
  125.8 2.5 %collective-permute-done.30 = f32[16,128]{1,0:T(8,128)S(1)} collective-permute-done((f32[16,128]{1,0:T(8,128)S(1)}, f32[16,128]{1,0:T(8,128)S(1)}, u32[]{:S(2)}, u32[]{:S(2)}) %collective-permute-start.30) | collective-permute-done | bytes 8224 | tf_op jit(solution)/shard_map/ppermute | solution.py:529
  128.3 0.6 add_bitcast_fusion
  (88 shorter events, 5.2 us)
Async XLA Ops:
  0.6 32.6 %collective-permute-start.3 = (bf16[2,384,768]{2,1,0:T(8,128)(2,1)}, bf16[2,384,768]{2,1,0:T(8,128)(2,1)}, u32[]{:S(2)}, u32[]{:S(2)}) collective-permute-start(bf16[2,384,768]{2,1,0:T(8,128)(2,1)} %act_ref.1), channel_id=1, source_target_pairs={{0,1},{1,0},{2,3},{3,2},{4,5},{5,4},{6,7},{7,6},{8,9},{9,8},{10,11... | collective-permute-start | bytes 3538952 | tf_op jit(solution)/shard_map/ppermute | solution.py:526
  1.1 32.1 %collective-permute-start.4 = (bf16[2,384,768]{2,1,0:T(8,128)(2,1)}, bf16[2,384,768]{2,1,0:T(8,128)(2,1)}, u32[]{:S(2)}, u32[]{:S(2)}) collective-permute-start(bf16[2,384,768]{2,1,0:T(8,128)(2,1)} %cot_ref.1), channel_id=1, source_target_pairs={{0,1},{1,0},{2,3},{3,2},{4,5},{5,4},{6,7},{7,6},{8,9},{9,8},{10,11... | collective-permute-start | bytes 3538952 | tf_op jit(solution)/shard_map/ppermute | solution.py:526
  2.0 1.7 %copy-start = (bf16[24,384,128]{2,1,0:T(8,128)(2,1)S(1)}, bf16[24,384,128]{2,1,0:T(8,128)(2,1)}, u32[]{:S(2)}) copy-start(bf16[24,384,128]{2,1,0:T(8,128)(2,1)} %refs_6_.5) | copy-start | bytes 7077892
  8.7 1.5 %collective-permute-start = (bf16[8,24,384]{2,1,0:T(8,128)(2,1)S(1)}, bf16[8,24,384]{2,1,0:T(8,128)(2,1)S(1)}, u32[]{:S(2)}, u32[]{:S(2)}) collective-permute-start(bf16[8,24,384]{2,1,0:T(8,128)(2,1)S(1)} %get-tuple-element.65), channel_id=1, source_target_pairs={{0,1},{1,0},{2,3},{3,2},{4,5},{5,4},{6,7},{7,6},{8,9},{9,8},{10,11... | collective-permute-start | bytes 442376 | tf_op jit(solution)/shard_map/ppermute | solution.py:526
  10.3 12.6 %collective-permute-start.9 = (bf16[1,3,48,384]{3,2,1,0:T(8,128)(2,1)S(1)}, bf16[1,3,48,384]{3,2,1,0:T(8,128)(2,1)S(1)}, u32[]{:S(2)}, u32[]{:S(2)}) collective-permute-start(bf16[1,3,48,384]{3,2,1,0:T(8,128)(2,1)S(1)} %get-tuple-element.125.refs_0_), channel_id=1, source_target_pairs={{0,8},{2,10},{4,12},{6,14},{8,0},{10,2},{12,4},{14,6},{1,9},{3,11}... | collective-permute-start | bytes 331784 | tf_op jit(solution)/shard_map/ppermute | solution.py:529
  14.3 15.1 %collective-permute-start.1 = (bf16[1,3,48,384]{3,2,1,0:T(8,128)(2,1)S(1)}, bf16[1,3,48,384]{3,2,1,0:T(8,128)(2,1)S(1)}, u32[]{:S(2)}, u32[]{:S(2)}) collective-permute-start(bf16[1,3,48,384]{3,2,1,0:T(8,128)(2,1)S(1)} %get-tuple-element.126.refs_0_), channel_id=1, source_target_pairs={{0,8},{2,10},{4,12},{6,14},{8,0},{10,2},{12,4},{14,6},{1,9},{3,11}... | collective-permute-start | bytes 331784 | tf_op jit(solution)/shard_map/ppermute | solution.py:529
  22.9 8.3 %collective-permute-start.10 = (bf16[2,3,48,384]{3,2,1,0:T(8,128)(2,1)S(1)}, bf16[2,3,48,384]{3,2,1,0:T(8,128)(2,1)S(1)}, u32[]{:S(2)}, u32[]{:S(2)}) collective-permute-start(bf16[2,3,48,384]{3,2,1,0:T(8,128)(2,1)S(1)} %concat.8.refs_0_), channel_id=1, source_target_pairs={{0,4},{2,6},{4,0},{6,2},{8,12},{10,14},{12,8},{14,10},{1,5},{3,7},... | collective-permute-start | bytes 663560 | tf_op jit(solution)/shard_map/ppermute | solution.py:529
  29.5 9.4 %collective-permute-start.2 = (bf16[2,3,48,384]{3,2,1,0:T(8,128)(2,1)S(1)}, bf16[2,3,48,384]{3,2,1,0:T(8,128)(2,1)S(1)}, u32[]{:S(2)}, u32[]{:S(2)}) collective-permute-start(bf16[2,3,48,384]{3,2,1,0:T(8,128)(2,1)S(1)} %concat.6.refs_0_), channel_id=1, source_target_pairs={{0,4},{2,6},{4,0},{6,2},{8,12},{10,14},{12,8},{14,10},{1,5},{3,7},... | collective-permute-start | bytes 663560 | tf_op jit(solution)/shard_map/ppermute | solution.py:529
  31.3 7.5 %copy-start.2 = (bf16[4,3,48,384]{3,2,1,0:T(8,128)(2,1)}, bf16[4,3,48,384]{3,2,1,0:T(8,128)(2,1)S(1)}, u32[]{:S(2)}) copy-start(bf16[4,3,48,384]{3,2,1,0:T(8,128)(2,1)S(1)} %concat.9.refs_0_) | copy-start | bytes 1327108
  31.3 15.0 %collective-permute-start.11 = (bf16[4,3,48,384]{3,2,1,0:T(8,128)(2,1)S(1)}, bf16[4,3,48,384]{3,2,1,0:T(8,128)(2,1)S(1)}, u32[]{:S(2)}, u32[]{:S(2)}) collective-permute-start(bf16[4,3,48,384]{3,2,1,0:T(8,128)(2,1)S(1)} %concat.9.refs_0_), channel_id=1, source_target_pairs={{0,2},{2,0},{4,6},{6,4},{8,10},{10,8},{12,14},{14,12},{1,3},{3,1},... | collective-permute-start | bytes 1327112 | tf_op jit(solution)/shard_map/ppermute | solution.py:529
  38.9 17.1 %copy-start.3 = (bf16[4,3,48,384]{3,2,1,0:T(8,128)(2,1)}, bf16[4,3,48,384]{3,2,1,0:T(8,128)(2,1)S(1)}, u32[]{:S(2)}) copy-start(bf16[4,3,48,384]{3,2,1,0:T(8,128)(2,1)S(1)} %concat.7.refs_0_) | copy-start | bytes 1327108
  38.9 19.3 %collective-permute-start.5 = (bf16[4,3,48,384]{3,2,1,0:T(8,128)(2,1)S(1)}, bf16[4,3,48,384]{3,2,1,0:T(8,128)(2,1)S(1)}, u32[]{:S(2)}, u32[]{:S(2)}) collective-permute-start(bf16[4,3,48,384]{3,2,1,0:T(8,128)(2,1)S(1)} %concat.7.refs_0_), channel_id=1, source_target_pairs={{0,2},{2,0},{4,6},{6,4},{8,10},{10,8},{12,14},{14,12},{1,3},{3,1},... | collective-permute-start | bytes 1327112 | tf_op jit(solution)/shard_map/ppermute | solution.py:529
  39.1 6.2 %collective-permute-start.15 = (bf16[1,2,48,384]{3,2,1,0:T(8,128)(2,1)S(1)}, bf16[1,2,48,384]{3,2,1,0:T(8,128)(2,1)S(1)}, u32[]{:S(2)}, u32[]{:S(2)}) collective-permute-start(bf16[1,2,48,384]{3,2,1,0:T(8,128)(2,1)S(1)} %slice.14.refs_0_), channel_id=1, source_target_pairs={{0,8},{2,10},{4,12},{6,14},{8,0},{10,2},{12,4},{14,6},{1,9},{3,11}... | collective-permute-start | bytes 221192 | tf_op jit(solution)/shard_map/ppermute | solution.py:529
  45.3 12.2 %collective-permute-start.16 = (bf16[2,2,48,384]{3,2,1,0:T(8,128)(2,1)S(1)}, bf16[2,2,48,384]{3,2,1,0:T(8,128)(2,1)S(1)}, u32[]{:S(2)}, u32[]{:S(2)}) collective-permute-start(bf16[2,2,48,384]{3,2,1,0:T(8,128)(2,1)S(1)} %concat.10.refs_0_), channel_id=1, source_target_pairs={{0,4},{2,6},{4,0},{6,2},{8,12},{10,14},{12,8},{14,10},{1,5},{3,7},... | collective-permute-start | bytes 442376 | tf_op jit(solution)/shard_map/ppermute | solution.py:529
  46.3 0.8 copy-start.11
  56.0 26.3 %collective-permute-start.12 = (s16[4,160,384]{2,1,0:T(8,128)(2,1)}, s16[4,160,384]{2,1,0:T(8,128)(2,1)S(1)}, u32[]{:S(2)}, u32[]{:S(2)}) collective-permute-start(s16[4,160,384]{2,1,0:T(8,128)(2,1)} %get-tuple-element.90), channel_id=1, source_target_pairs={{0,2},{2,0},{4,6},{6,4},{8,10},{10,8},{12,14},{14,12},{1,3},{3,1},... | collective-permute-start | bytes 1474568 | tf_op jit(solution)/shard_map/ppermute | solution.py:529
  57.6 10.3 %copy-start.4 = (bf16[4,2,48,384]{3,2,1,0:T(8,128)(2,1)}, bf16[4,2,48,384]{3,2,1,0:T(8,128)(2,1)S(1)}, u32[]{:S(2)}) copy-start(bf16[4,2,48,384]{3,2,1,0:T(8,128)(2,1)S(1)} %concat.11.refs_0_) | copy-start | bytes 884740
  57.6 15.6 %collective-permute-start.17 = (bf16[4,2,48,384]{3,2,1,0:T(8,128)(2,1)S(1)}, bf16[4,2,48,384]{3,2,1,0:T(8,128)(2,1)S(1)}, u32[]{:S(2)}, u32[]{:S(2)}) collective-permute-start(bf16[4,2,48,384]{3,2,1,0:T(8,128)(2,1)S(1)} %concat.11.refs_0_), channel_id=1, source_target_pairs={{0,2},{2,0},{4,6},{6,4},{8,10},{10,8},{12,14},{14,12},{1,3},{3,1},... | collective-permute-start | bytes 884744 | tf_op jit(solution)/shard_map/ppermute | solution.py:529
  58.2 0.8 copy-start.12
  67.9 14.4 %copy-start.5 = (f32[4,3,48,384]{3,2,1,0:T(8,128)S(1)}, f32[4,3,48,384]{3,2,1,0:T(8,128)}, u32[]{:S(2)}) copy-start(f32[4,3,48,384]{3,2,1,0:T(8,128)} %get-tuple-element.89.own_ref) | copy-start | bytes 2654212
  67.9 15.0 %collective-permute-start.6 = (s16[4,160,384]{2,1,0:T(8,128)(2,1)}, s16[4,160,384]{2,1,0:T(8,128)(2,1)S(1)}, u32[]{:S(2)}, u32[]{:S(2)}) collective-permute-start(s16[4,160,384]{2,1,0:T(8,128)(2,1)} %get-tuple-element.85), channel_id=1, source_target_pairs={{0,4},{2,6},{4,0},{6,2},{8,12},{10,14},{12,8},{14,10},{1,5},{3,7},... | collective-permute-start | bytes 1474568 | tf_op jit(solution)/shard_map/ppermute | solution.py:529
  73.3 0.7 copy-start.13
  80.8 2.1 %copy-start.6 = (f32[4,3,48,384]{3,2,1,0:T(8,128)S(1)}, f32[4,3,48,384]{3,2,1,0:T(8,128)}, u32[]{:S(2)}) copy-start(f32[4,3,48,384]{3,2,1,0:T(8,128)} %get-tuple-element.84.own_ref) | copy-start | bytes 2654212
  80.9 9.5 %collective-permute-start.18 = (s16[4,112,384]{2,1,0:T(8,128)(2,1)}, s16[4,112,384]{2,1,0:T(8,128)(2,1)S(1)}, u32[]{:S(2)}, u32[]{:S(2)}) collective-permute-start(s16[4,112,384]{2,1,0:T(8,128)(2,1)} %get-tuple-element.95), channel_id=1, source_target_pairs={{0,2},{2,0},{4,6},{6,4},{8,10},{10,8},{12,14},{14,12},{1,3},{3,1},... | collective-permute-start | bytes 1032200 | tf_op jit(solution)/shard_map/ppermute | solution.py:529
  82.3 8.0 %copy-start.7 = (f32[4,2,48,384]{3,2,1,0:T(8,128)S(1)}, f32[4,2,48,384]{3,2,1,0:T(8,128)}, u32[]{:S(2)}) copy-start(f32[4,2,48,384]{3,2,1,0:T(8,128)} %get-tuple-element.94.own_ref) | copy-start | bytes 1769476
  82.6 8.0 %copy-start.19 = (bf16[2,96,384]{2,1,0:T(8,128)(2,1)S(1)}, bf16[2,96,384]{2,1,0:T(8,128)(2,1)}, u32[]{:S(2)}) copy-start(bf16[2,96,384]{2,1,0:T(8,128)(2,1)} %get-tuple-element.104) | copy-start | bytes 442372
  82.6 8.1 %copy-start.17 = (bf16[2,144,384]{2,1,0:T(8,128)(2,1)S(1)}, bf16[2,144,384]{2,1,0:T(8,128)(2,1)}, u32[]{:S(2)}) copy-start(bf16[2,144,384]{2,1,0:T(8,128)(2,1)} %get-tuple-element.103) | copy-start | bytes 663556
  82.6 8.6 %copy-start.18 = (bf16[2,144,384]{2,1,0:T(8,128)(2,1)S(1)}, bf16[2,144,384]{2,1,0:T(8,128)(2,1)}, u32[]{:S(2)}) copy-start(bf16[2,144,384]{2,1,0:T(8,128)(2,1)} %get-tuple-element.102) | copy-start | bytes 663556
  82.6 8.6 %collective-permute-start.13 = (s16[2,160,384]{2,1,0:T(8,128)(2,1)S(1)}, s16[2,160,384]{2,1,0:T(8,128)(2,1)S(1)}, u32[]{:S(2)}, u32[]{:S(2)}) collective-permute-start(s16[2,160,384]{2,1,0:T(8,128)(2,1)S(1)} %get-tuple-element.92), channel_id=1, source_target_pairs={{0,4},{2,6},{4,0},{6,2},{8,12},{10,14},{12,8},{14,10},{1,5},{3,7},... | collective-permute-start | bytes 737288 | tf_op jit(solution)/shard_map/ppermute | solution.py:529
  83.2 9.8 %collective-permute-start.7 = (s16[2,160,384]{2,1,0:T(8,128)(2,1)S(1)}, s16[2,160,384]{2,1,0:T(8,128)(2,1)S(1)}, u32[]{:S(2)}, u32[]{:S(2)}) collective-permute-start(s16[2,160,384]{2,1,0:T(8,128)(2,1)S(1)} %get-tuple-element.87), channel_id=1, source_target_pairs={{0,2},{2,0},{4,6},{6,4},{8,10},{10,8},{12,14},{14,12},{1,3},{3,1},... | collective-permute-start | bytes 737288 | tf_op jit(solution)/shard_map/ppermute | solution.py:529
  90.5 6.1 %collective-permute-start.19 = (s16[2,112,384]{2,1,0:T(8,128)(2,1)S(1)}, s16[2,112,384]{2,1,0:T(8,128)(2,1)S(1)}, u32[]{:S(2)}, u32[]{:S(2)}) collective-permute-start(s16[2,112,384]{2,1,0:T(8,128)(2,1)S(1)} %get-tuple-element.97), channel_id=1, source_target_pairs={{0,4},{2,6},{4,0},{6,2},{8,12},{10,14},{12,8},{14,10},{1,5},{3,7},... | collective-permute-start | bytes 516104 | tf_op jit(solution)/shard_map/ppermute | solution.py:529
  90.6 8.8 %collective-permute-start.23 = (bf16[2,96,384]{2,1,0:T(8,128)(2,1)S(1)}, bf16[2,96,384]{2,1,0:T(8,128)(2,1)S(1)}, u32[]{:S(2)}, u32[]{:S(2)}) collective-permute-start(bf16[2,96,384]{2,1,0:T(8,128)(2,1)S(1)} %copy-done.19), channel_id=1, source_target_pairs={{0,1},{1,0},{2,3},{3,2},{4,5},{5,4},{6,7},{7,6},{8,9},{9,8},{10,11... | collective-permute-start | bytes 442376 | tf_op jit(solution)/shard_map/ppermute | solution.py:526
  90.7 9.0 %collective-permute-start.22 = (bf16[2,144,384]{2,1,0:T(8,128)(2,1)S(1)}, bf16[2,144,384]{2,1,0:T(8,128)(2,1)S(1)}, u32[]{:S(2)}, u32[]{:S(2)}) collective-permute-start(bf16[2,144,384]{2,1,0:T(8,128)(2,1)S(1)} %copy-done.17), channel_id=1, source_target_pairs={{0,1},{1,0},{2,3},{3,2},{4,5},{5,4},{6,7},{7,6},{8,9},{9,8},{10,11... | collective-permute-start | bytes 663560 | tf_op jit(solution)/shard_map/ppermute | solution.py:526
  91.2 8.5 %collective-permute-start.21 = (bf16[2,144,384]{2,1,0:T(8,128)(2,1)S(1)}, bf16[2,144,384]{2,1,0:T(8,128)(2,1)S(1)}, u32[]{:S(2)}, u32[]{:S(2)}) collective-permute-start(bf16[2,144,384]{2,1,0:T(8,128)(2,1)S(1)} %copy-done.18), channel_id=1, source_target_pairs={{0,1},{1,0},{2,3},{3,2},{4,5},{5,4},{6,7},{7,6},{8,9},{9,8},{10,11... | collective-permute-start | bytes 663560 | tf_op jit(solution)/shard_map/ppermute | solution.py:526
  93.0 18.2 %collective-permute-start.14 = (s16[1,160,384]{2,1,0:T(8,128)(2,1)}, s16[1,160,384]{2,1,0:T(8,128)(2,1)S(1)}, u32[]{:S(2)}, u32[]{:S(2)}) collective-permute-start(s16[1,160,384]{2,1,0:T(8,128)(2,1)} %get-tuple-element.93), channel_id=1, source_target_pairs={{0,8},{2,10},{4,12},{6,14},{8,0},{10,2},{12,4},{14,6},{1,9},{3,11}... | collective-permute-start | bytes 368648 | tf_op jit(solution)/shard_map/ppermute | solution.py:529
  96.6 14.6 %collective-permute-start.8 = (s16[1,160,384]{2,1,0:T(8,128)(2,1)}, s16[1,160,384]{2,1,0:T(8,128)(2,1)S(1)}, u32[]{:S(2)}, u32[]{:S(2)}) collective-permute-start(s16[1,160,384]{2,1,0:T(8,128)(2,1)} %get-tuple-element.88), channel_id=1, source_target_pairs={{0,8},{2,10},{4,12},{6,14},{8,0},{10,2},{12,4},{14,6},{1,9},{3,11}... | collective-permute-start | bytes 368648 | tf_op jit(solution)/shard_map/ppermute | solution.py:529
  99.4 11.7 %collective-permute-start.20 = (s16[1,112,384]{2,1,0:T(8,128)(2,1)S(1)}, s16[1,112,384]{2,1,0:T(8,128)(2,1)S(1)}, u32[]{:S(2)}, u32[]{:S(2)}) collective-permute-start(s16[1,112,384]{2,1,0:T(8,128)(2,1)S(1)} %get-tuple-element.98), channel_id=1, source_target_pairs={{0,8},{2,10},{4,12},{6,14},{8,0},{10,2},{12,4},{14,6},{1,9},{3,11}... | collective-permute-start | bytes 258056 | tf_op jit(solution)/shard_map/ppermute | solution.py:529
  99.7 0.7 copy-start.14
  99.7 0.8 copy-start.15
  100.5 12.8 %copy-start.1 = (bf16[24,384,128]{2,1,0:T(8,128)(2,1)S(1)}, bf16[24,384,128]{2,1,0:T(8,128)(2,1)}, u32[]{:S(2)}) copy-start(bf16[24,384,128]{2,1,0:T(8,128)(2,1)} %refs_6_.5) | copy-start | bytes 7077892
  100.5 12.8 %copy-start.10 = (f32[128]{0:T(128)S(1)}, f32[128]{0:T(128)}, u32[]{:S(2)}) copy-start(f32[128]{0:T(128)} %param.13) | copy-start | bytes 1540
  111.2 2.0 %collective-permute-start.24 = (f32[3,24,384]{2,1,0:T(8,128)S(1)}, f32[3,24,384]{2,1,0:T(8,128)S(1)}, u32[]{:S(2)}, u32[]{:S(2)}) collective-permute-start(f32[3,24,384]{2,1,0:T(8,128)S(1)} %get-tuple-element.116), channel_id=1, source_target_pairs={{0,1},{1,0},{2,3},{3,2},{4,5},{5,4},{6,7},{7,6},{8,9},{9,8},{10,11... | collective-permute-start | bytes 331784 | tf_op jit(solution)/shard_map/ppermute | solution.py:526
  111.3 1.9 %collective-permute-start.25 = (f32[3,24,384]{2,1,0:T(8,128)S(1)}, f32[3,24,384]{2,1,0:T(8,128)S(1)}, u32[]{:S(2)}, u32[]{:S(2)}) collective-permute-start(f32[3,24,384]{2,1,0:T(8,128)S(1)} %get-tuple-element.117), channel_id=1, source_target_pairs={{0,1},{1,0},{2,3},{3,2},{4,5},{5,4},{6,7},{7,6},{8,9},{9,8},{10,11... | collective-permute-start | bytes 331784 | tf_op jit(solution)/shard_map/ppermute | solution.py:526
  111.9 1.3 %collective-permute-start.26 = (f32[2,24,384]{2,1,0:T(8,128)S(1)}, f32[2,24,384]{2,1,0:T(8,128)S(1)}, u32[]{:S(2)}, u32[]{:S(2)}) collective-permute-start(f32[2,24,384]{2,1,0:T(8,128)S(1)} %get-tuple-element.118), channel_id=1, source_target_pairs={{0,1},{1,0},{2,3},{3,2},{4,5},{5,4},{6,7},{7,6},{8,9},{9,8},{10,11... | collective-permute-start | bytes 221192 | tf_op jit(solution)/shard_map/ppermute | solution.py:526
  114.0 1.2 collective-permute-start.27
  115.2 4.9 %collective-permute-start.28 = (f32[16,128]{1,0:T(8,128)S(1)}, f32[16,128]{1,0:T(8,128)S(1)}, u32[]{:S(2)}, u32[]{:S(2)}) collective-permute-start(f32[16,128]{1,0:T(8,128)S(1)} %add.12), channel_id=1, source_target_pairs={{0,2},{2,0},{4,6},{6,4},{8,10},{10,8},{12,14},{14,12},{1,3},{3,1},... | collective-permute-start | bytes 24584 | tf_op jit(solution)/shard_map/ppermute | solution.py:529
  120.1 3.7 %collective-permute-start.29 = (f32[16,128]{1,0:T(8,128)S(1)}, f32[16,128]{1,0:T(8,128)S(1)}, u32[]{:S(2)}, u32[]{:S(2)}) collective-permute-start(f32[16,128]{1,0:T(8,128)S(1)} %add.13), channel_id=1, source_target_pairs={{0,4},{2,6},{4,0},{6,2},{8,12},{10,14},{12,8},{14,10},{1,5},{3,7},... | collective-permute-start | bytes 24584 | tf_op jit(solution)/shard_map/ppermute | solution.py:529
  123.7 4.5 %collective-permute-start.30 = (f32[16,128]{1,0:T(8,128)S(1)}, f32[16,128]{1,0:T(8,128)S(1)}, u32[]{:S(2)}, u32[]{:S(2)}) collective-permute-start(f32[16,128]{1,0:T(8,128)S(1)} %add.14), channel_id=1, source_target_pairs={{0,8},{2,10},{4,12},{6,14},{8,0},{10,2},{12,4},{14,6},{1,9},{3,11}... | collective-permute-start | bytes 24584 | tf_op jit(solution)/shard_map/ppermute | solution.py:529
  (3 other events, 2.0 us)
